TPU v7x, 32 devices: a whole 2x2x4 slice. The times are simulated.
32 devices in a mesh: stream: 4 (over y, x), tm: 8 (over z, core).
Axes of the slice: x: 2, y: 2, z: 4, core: 2. Of those that a mesh axis runs over, the one named last changes fastest.
Arguments:
- frames: bfloat16 [16, 8, 256, 512], P('stream', 'tm'), may hold values from -6 to 6
- space_gain: float32 [512], replicated, may hold values from 0.1 to 1.9
- space_input: bfloat16 [512, 1536], replicated, may hold values from -0.25 to 0.25
- space_output: bfloat16 [512, 512], replicated, may hold values from -2 to 2
- space_scale: float32 [512], replicated, may hold values from 0.1 to 1.9
- space_up: bfloat16 [512, 2048], replicated, may hold values from -0.25 to 0.25
- space_down: bfloat16 [2048, 512], replicated, may hold values from -0.125 to 0.125
- time_gain: float32 [512], replicated, may hold values from 0.1 to 1.9
- time_input: bfloat16 [512, 1536], replicated, may hold values from -0.25 to 0.25
- time_output: bfloat16 [512, 512], replicated, may hold values from -1 to 1
- time_scale: float32 [512], replicated, may hold values from 0.1 to 1.9
- time_up: bfloat16 [512, 2048], replicated, may hold values from -0.25 to 0.25
- time_down: bfloat16 [2048, 512], replicated, may hold values from -0.125 to 0.125
- clip_labels: int32 [16, 8], P('stream'), may hold values from 0 to 7, as said below
- output_grad: bfloat16 [16, 8, 256, 512], P('stream', 'tm'), may hold values from -6 to 6
Outputs:
- block_out: float32 [16, 8, 256, 512], P('stream', 'tm')
- input_grad: float32 [16, 8, 256, 512], P('stream', 'tm')
- space_gain_grad: float32 [512], P('tm')
- space_input_grad: float32 [512, 1536], P('tm')
- space_output_grad: float32 [512, 512], P('tm')
- space_scale_grad: float32 [512], P('tm')
- space_up_grad: float32 [512, 2048], P('tm')
- space_down_grad: float32 [2048, 512], P('tm')
- time_gain_grad: float32 [512], P('tm')
- time_input_grad: float32 [512, 1536], P('tm')
- time_output_grad: float32 [512, 512], P('tm')
- time_scale_grad: float32 [512], P('tm')
- time_up_grad: float32 [512, 2048], P('tm')
- time_down_grad: float32 [2048, 512], P('tm')
Inputs may be any that keep to these rules, and one draw needn't show every extreme that they name: `clip_labels`: in every pack the labels start at 0 and rise by 0 or 1 from one frame-slot to the next; frame-slots with one label form a clip. In each aligned group of 4 packs one pack is a single clip over all 8 frame-slots, and another pack has a clip of one frame-slot at every frame-slot.
All inputs are finite; a program needn't handle non-finite values.
Results may differ from a plain program's by a relative error of at most 0.025.
Values may be sent and summed in bfloat16 or wider, within the bound.
No kernel may reach another device: no remote copies, remote signals or barrier semaphores. Data moves between devices by JAX's collectives and lax.ppermute only.
A program may use at most 192 MiB of HBM per device.

v0:
```python
import jax
import jax.numpy as jnp
from jax import lax
from jax.sharding import PartitionSpec as P

HEADS = 8


space_forms = ("bfphe,bfrhe->bfhpr", "bfhpr,bfrhe->bfphe", "bfhpr,bfphe->bfrhe")
time_forms = ("bfphe,bgphe->bphfg", "bphfg,bgphe->bfphe", "bphfg,bfphe->bgphe")
gelu_coeff = 0.7978845608028654


def project(left, right):
    return jnp.dot(left, right, preferred_element_type=jnp.float32)


def contract_rows(left, right):
    return lax.dot_general(
        left, right, (((0,), (0,)), ((), ())), preferred_element_type=jnp.float32
    )


def contract_cols(left, right):
    return lax.dot_general(
        left, right, (((1,), (1,)), ((), ())), preferred_element_type=jnp.float32
    )


def norm_forward(values, gain_vector):
    average = jnp.mean(values, axis=-1, keepdims=True)
    centered = values - average
    inverse = lax.rsqrt(jnp.mean(centered * centered, axis=-1, keepdims=True) + 1e-05)
    unit_rows = centered * inverse
    return ((unit_rows * gain_vector).astype(jnp.bfloat16), unit_rows, inverse)


def norm_backward(grad_normed, gain_vector, unit_rows, inverse):
    scaled = grad_normed * gain_vector
    gain_grad = jnp.sum(grad_normed * unit_rows, axis=0)
    grad_in = inverse * (
        scaled
        - jnp.mean(scaled, axis=-1, keepdims=True)
        - unit_rows * jnp.mean(scaled * unit_rows, axis=-1, keepdims=True)
    )
    return (grad_in, gain_grad)


def gelu_parts(before):
    argument = gelu_coeff * (before + 0.044715 * before * before * before)
    tangent = jnp.tanh(argument)
    gelu_value = 0.5 * before * (1.0 + tangent)
    gelu_slope = 0.5 * (1.0 + tangent) + 0.5 * before * (1.0 - tangent * tangent) * gelu_coeff * (
        1.0 + 3.0 * 0.044715 * before * before
    )
    return (gelu_value, gelu_slope)


def feed_forward(residual, scale_vector, up_weight, down_weight):
    normed, unit_rows, inverse = norm_forward(residual, scale_vector)
    before = project(normed, up_weight)
    gelu_value, gelu_slope = gelu_parts(before)
    hidden = gelu_value.astype(jnp.bfloat16)
    return (
        residual + project(hidden, down_weight),
        (normed, unit_rows, inverse, gelu_slope, hidden),
    )


def feed_backward(grad_out, kept_state, scale_vector, up_weight, down_weight):
    normed, unit_rows, inverse, gelu_slope, hidden = kept_state
    rounded = grad_out.astype(jnp.bfloat16)
    down_grad = contract_rows(hidden, rounded)
    grad_hidden = contract_cols(rounded, down_weight)
    grad_before = (grad_hidden * gelu_slope).astype(jnp.bfloat16)
    up_grad = contract_rows(normed, grad_before)
    grad_normed = contract_cols(grad_before, up_weight)
    grad_in, scale_grad = norm_backward(grad_normed, scale_vector, unit_rows, inverse)
    return (grad_out + grad_in, (scale_grad, up_grad, down_grad))


def attention_in(residual, gain_vector, input_weight):
    normed, unit_rows, inverse = norm_forward(residual, gain_vector)
    packed = project(normed, input_weight).astype(jnp.bfloat16)
    return (packed, (normed, unit_rows, inverse))


def attention_back_out(grad_out, mixed, output_weight):
    rounded = grad_out.astype(jnp.bfloat16)
    output_grad_part = contract_rows(mixed, rounded)
    grad_mixed = contract_cols(rounded, output_weight).astype(jnp.bfloat16)
    return (grad_mixed, output_grad_part)


def attention_back_in(grad_out, grad_packed, kept_state, gain_vector, input_weight):
    normed, unit_rows, inverse = kept_state
    input_grad_part = contract_rows(normed, grad_packed)
    grad_normed = contract_cols(grad_packed, input_weight)
    grad_in, gain_grad = norm_backward(grad_normed, gain_vector, unit_rows, inverse)
    return (grad_out + grad_in, (gain_grad, input_grad_part))


def masked_scores(queries, key_rows, allowed, form):
    scores = jnp.einsum(
        form, queries, key_rows, preferred_element_type=jnp.float32
    ) * queries.shape[-1] ** (-0.5)
    if allowed is None:
        return scores
    return jnp.where(allowed, scores, -1e30)


def attend_forward(packed, allowed, einsum_forms):
    queries = packed[:, :, :, 0]
    key_rows = packed[:, :, :, 1]
    value_rows = packed[:, :, :, 2]
    scores = masked_scores(queries, key_rows, allowed, einsum_forms[0])
    highest_score = jnp.max(scores, axis=-1, keepdims=True)
    exponent = jnp.exp(scores - highest_score)
    total_weight = jnp.sum(exponent, axis=-1, keepdims=True)
    weights = (exponent / total_weight).astype(jnp.bfloat16)
    mixed = jnp.einsum(einsum_forms[1], weights, value_rows, preferred_element_type=jnp.float32)
    return (mixed, highest_score + jnp.log(total_weight))


def attend_backward(packed, allowed, einsum_forms, logsum, grad_mixed):
    queries = packed[:, :, :, 0]
    key_rows = packed[:, :, :, 1]
    value_rows = packed[:, :, :, 2]
    factor = queries.shape[-1] ** (-0.5)
    softmax_rows = jnp.exp(masked_scores(queries, key_rows, allowed, einsum_forms[0]) - logsum)
    weights = softmax_rows.astype(jnp.bfloat16)
    grad_values = jnp.einsum(
        einsum_forms[2], weights, grad_mixed, preferred_element_type=jnp.float32
    )
    grad_weights = jnp.einsum(
        einsum_forms[0], grad_mixed, value_rows, preferred_element_type=jnp.float32
    )
    grad_scores = (
        softmax_rows * (grad_weights - jnp.sum(grad_weights * softmax_rows, axis=-1, keepdims=True))
    ).astype(jnp.bfloat16)
    grad_queries = (
        jnp.einsum(einsum_forms[1], grad_scores, key_rows, preferred_element_type=jnp.float32)
        * factor
    )
    grad_keys = (
        jnp.einsum(einsum_forms[2], grad_scores, queries, preferred_element_type=jnp.float32)
        * factor
    )
    return jnp.stack([grad_queries, grad_keys, grad_values], axis=3).astype(jnp.bfloat16)


def per_device(
    frames,
    space_gain,
    space_input,
    space_output,
    space_scale,
    space_up,
    space_down,
    time_gain,
    time_input,
    time_output,
    time_scale,
    time_up,
    time_down,
    clip_labels,
    output_grad,
):
    pack_count, slot_count, patches, model_width = frames.shape
    head_count = HEADS
    head_size = model_width // head_count
    token_count = pack_count * slot_count * patches
    initial = frames.astype(jnp.float32).reshape(token_count, model_width)
    packed, space_kept = attention_in(initial, space_gain, space_input)
    space_packed = packed.reshape(pack_count, slot_count, patches, 3, head_count, head_size)
    mixed, space_logsum = attend_forward(space_packed, None, space_forms)
    space_mixed = mixed.astype(jnp.bfloat16).reshape(token_count, model_width)
    after_one = initial + project(space_mixed, space_output)
    after_two, space_feed = feed_forward(after_one, space_scale, space_up, space_down)
    packed, time_kept = attention_in(after_two, time_gain, time_input)
    exchanged = lax.all_to_all(
        packed.reshape(pack_count, slot_count, patches, 3 * model_width),
        "tm",
        split_axis=2,
        concat_axis=1,
        tiled=True,
    )
    frame_count = exchanged.shape[1]
    local_count = exchanged.shape[2]
    time_packed = exchanged.reshape(pack_count, frame_count, local_count, 3, head_count, head_size)
    positions = jnp.arange(frame_count)
    allowed = (
        (clip_labels[:, :, None] == clip_labels[:, None, :])
        & (positions[None, None, :] <= positions[None, :, None])
    )[:, None, None]
    mixed, time_logsum = attend_forward(time_packed, allowed, time_forms)
    mixed = mixed.astype(jnp.bfloat16).reshape(pack_count, frame_count, local_count, model_width)
    time_mixed = lax.all_to_all(mixed, "tm", split_axis=1, concat_axis=2, tiled=True).reshape(
        token_count, model_width
    )
    after_three = after_two + project(time_mixed, time_output)
    result, time_feed = feed_forward(after_three, time_scale, time_up, time_down)
    grad_top = output_grad.astype(jnp.float32).reshape(token_count, model_width)
    grad_three, (time_scale_grad, time_up_grad, time_down_grad) = feed_backward(
        grad_top, time_feed, time_scale, time_up, time_down
    )
    grad_mixed, time_output_grad = attention_back_out(grad_three, time_mixed, time_output)
    grad_exchanged = lax.all_to_all(
        grad_mixed.reshape(pack_count, slot_count, patches, model_width),
        "tm",
        split_axis=2,
        concat_axis=1,
        tiled=True,
    )
    grad_packed = attend_backward(
        time_packed,
        allowed,
        time_forms,
        time_logsum,
        grad_exchanged.reshape(pack_count, frame_count, local_count, head_count, head_size),
    )
    grad_packed = lax.all_to_all(
        grad_packed.reshape(pack_count, frame_count, local_count, 3 * model_width),
        "tm",
        split_axis=1,
        concat_axis=2,
        tiled=True,
    ).reshape(token_count, 3 * model_width)
    grad_two, (time_gain_grad, time_input_grad) = attention_back_in(
        grad_three, grad_packed, time_kept, time_gain, time_input
    )
    grad_one, (space_scale_grad, space_up_grad, space_down_grad) = feed_backward(
        grad_two, space_feed, space_scale, space_up, space_down
    )
    grad_mixed, space_output_grad = attention_back_out(grad_one, space_mixed, space_output)
    grad_packed = attend_backward(
        space_packed,
        None,
        space_forms,
        space_logsum,
        grad_mixed.reshape(pack_count, slot_count, patches, head_count, head_size),
    )
    grad_zero, (space_gain_grad, space_input_grad) = attention_back_in(
        grad_one,
        grad_packed.reshape(token_count, 3 * model_width),
        space_kept,
        space_gain,
        space_input,
    )
    partial_sums = (
        space_gain_grad,
        space_input_grad,
        space_output_grad,
        space_scale_grad,
        space_up_grad,
        space_down_grad,
        time_gain_grad,
        time_input_grad,
        time_output_grad,
        time_scale_grad,
        time_up_grad,
        time_down_grad,
    )
    shares = (
        lax.psum_scatter(
            partial_sums[0].astype(jnp.bfloat16), "tm", scatter_dimension=0, tiled=True
        ).astype(jnp.float32),
        lax.psum_scatter(
            partial_sums[1].astype(jnp.bfloat16), "tm", scatter_dimension=0, tiled=True
        ).astype(jnp.float32),
        lax.psum_scatter(
            partial_sums[2].astype(jnp.bfloat16), "tm", scatter_dimension=0, tiled=True
        ).astype(jnp.float32),
        lax.psum_scatter(
            partial_sums[3].astype(jnp.bfloat16), "tm", scatter_dimension=0, tiled=True
        ).astype(jnp.float32),
        lax.psum_scatter(
            partial_sums[4].astype(jnp.bfloat16), "tm", scatter_dimension=0, tiled=True
        ).astype(jnp.float32),
        lax.psum_scatter(
            partial_sums[5].astype(jnp.bfloat16), "tm", scatter_dimension=0, tiled=True
        ).astype(jnp.float32),
        lax.psum_scatter(
            partial_sums[6].astype(jnp.bfloat16), "tm", scatter_dimension=0, tiled=True
        ).astype(jnp.float32),
        lax.psum_scatter(
            partial_sums[7].astype(jnp.bfloat16), "tm", scatter_dimension=0, tiled=True
        ).astype(jnp.float32),
        lax.psum_scatter(
            partial_sums[8].astype(jnp.bfloat16), "tm", scatter_dimension=0, tiled=True
        ).astype(jnp.float32),
        lax.psum_scatter(
            partial_sums[9].astype(jnp.bfloat16), "tm", scatter_dimension=0, tiled=True
        ).astype(jnp.float32),
        lax.psum_scatter(
            partial_sums[10].astype(jnp.bfloat16), "tm", scatter_dimension=0, tiled=True
        ).astype(jnp.float32),
        lax.psum_scatter(
            partial_sums[11].astype(jnp.bfloat16), "tm", scatter_dimension=0, tiled=True
        ).astype(jnp.float32),
    )
    totals = (
        lax.psum(shares[0].astype(jnp.bfloat16), "stream").astype(jnp.float32),
        lax.psum(shares[1].astype(jnp.bfloat16), "stream").astype(jnp.float32),
        lax.psum(shares[2].astype(jnp.bfloat16), "stream").astype(jnp.float32),
        lax.psum(shares[3].astype(jnp.bfloat16), "stream").astype(jnp.float32),
        lax.psum(shares[4].astype(jnp.bfloat16), "stream").astype(jnp.float32),
        lax.psum(shares[5].astype(jnp.bfloat16), "stream").astype(jnp.float32),
        lax.psum(shares[6].astype(jnp.bfloat16), "stream").astype(jnp.float32),
        lax.psum(shares[7].astype(jnp.bfloat16), "stream").astype(jnp.float32),
        lax.psum(shares[8].astype(jnp.bfloat16), "stream").astype(jnp.float32),
        lax.psum(shares[9].astype(jnp.bfloat16), "stream").astype(jnp.float32),
        lax.psum(shares[10].astype(jnp.bfloat16), "stream").astype(jnp.float32),
        lax.psum(shares[11].astype(jnp.bfloat16), "stream").astype(jnp.float32),
    )
    return (result.reshape(frames.shape), grad_zero.reshape(frames.shape)) + tuple(totals)


def solution(mesh):
    placed = (
        P("stream", "tm", None, None),
        P(),
        P(),
        P(),
        P(),
        P(),
        P(),
        P(),
        P(),
        P(),
        P(),
        P(),
        P(),
        P("stream", None),
        P("stream", "tm", None, None),
    )
    return jax.shard_map(
        per_device,
        mesh=mesh,
        in_specs=placed,
        out_specs=(
            P("stream", "tm", None, None),
            P("stream", "tm", None, None),
            P("tm"),
            P("tm", None),
            P("tm", None),
            P("tm"),
            P("tm", None),
            P("tm", None),
            P("tm"),
            P("tm", None),
            P("tm", None),
            P("tm"),
            P("tm", None),
            P("tm", None),
        ),
        check_vma=False,
    )
```

profile of v0, /device:TPU:16, one launch (start us, length us, event | category | flops | bytes accessed | tf_op | source)
XLA Modules:
  0.0 679.0 jit_solution(7981250288194597821)
XLA Ops:
  15.2 8.9 %reshape.421 = bf16[4,1,256,3,8,64]{5,4,3,2,0,1:T(8,128)(2,1)} reshape(bf16[1024,1536]{1,0:T(8,128)(2,1)} %convolution_convert_fusion.1) | data formatting | bytes 6291456 | tf_op jit(solution)/shard_map/reshape | solution.py:175
  24.0 5.7 fusion.76
  61.5 4.1 copy.102
  65.6 5.3 all-to-all-start
  71.0 68.2 %all-to-all-done = bf16[4,1,256,1536]{3,0,1,2:T(4,128)(2,1)} async-done(((bf16[4,1,256,1536]{3,0,1,2:T(4,128)(2,1)}), bf16[4,1,256,1536]{3,0,1,2:T(4,128)(2,1)}, u32[]{:S(2)}, u32[]{:S(2)}) %all-to-all-start) | async-done | bytes 3145760 | tf_op jit(solution)/shard_map/all_to_all | solution.py:181
  139.2 9.3 %reshape.422 = bf16[4,8,32,3,8,64]{5,4,3,0,2,1:T(8,128)(2,1)} reshape(bf16[4,1,256,1536]{3,0,1,2:T(4,128)(2,1)} %all-to-all-done) | data formatting | bytes 6291456 | tf_op jit(solution)/shard_map/reshape | solution.py:190
  148.4 4.5 fusion.75
  166.7 30.6 %all_to_all.16 = bf16[4,8,32,512]{3,2,0,1:T(8,128)(2,1)S(1)} all-to-all(bf16[4,8,32,512]{3,2,0,1:T(8,128)(2,1)} %reshape.415), channel_id=1, replica_groups=mesh['stream'=4,'tm'=8] {'tm'}, dimensions={1} | all-to-all | bytes 2097152 | tf_op jit(solution)/shard_map/all_to_all | solution.py:198
  201.5 6.9 %fusion.8 = bf16[1024,2048]{1,0:T(8,128)(2,1)S(1)} fusion(f32[1024,2048]{1,0:T(8,128)S(1)} %fusion.74, bf16[1024,512]{1,0:T(8,128)(2,1)S(1)} %bitcast.201, bf16[2048,512]{1,0:T(8,128)(2,1)S(1)} %copy-done.63), kind=kOutput, calls=%fused_computation.12 | convolution fusion | flops 2187329536 | bytes 15728640 | tf_op jit(solution)/shard_map/dot_general | solution.py:25
  214.9 7.9 %all-to-all-start.2 = ((bf16[4,1,256,512]{3,0,1,2:T(4,128)(2,1)}), bf16[4,1,256,512]{3,0,1,2:T(4,128)(2,1)}, u32[]{:S(2)}, u32[]{:S(2)}) async-start(bf16[4,1,256,512]{3,0,1,2:T(4,128)(2,1)} %copy.111), calls=%async_computation.2 | async-start | bytes 2097152 | tf_op jit(solution)/shard_map/all_to_all | solution.py:208
  225.0 21.2 %all-to-all-done.2 = bf16[4,1,256,512]{3,0,1,2:T(4,128)(2,1)} async-done(((bf16[4,1,256,512]{3,0,1,2:T(4,128)(2,1)}), bf16[4,1,256,512]{3,0,1,2:T(4,128)(2,1)}, u32[]{:S(2)}, u32[]{:S(2)}) %all-to-all-start.2) | async-done | bytes 1048608 | tf_op jit(solution)/shard_map/all_to_all | solution.py:208
  250.1 5.1 convert_bitcast_fusion
  266.1 4.2 copy.135
  270.3 9.2 %reshape.416 = bf16[4,8,32,1536]{3,2,0,1:T(8,128)(2,1)} reshape(bf16[4,8,32,3,8,64]{5,4,3,2,0,1:T(8,128)(2,1)} %copy.135) | data formatting | bytes 6291456 | tf_op jit(solution)/shard_map/convert_element_type | solution.py:149
  279.5 7.8 %all-to-all-start.3 = ((bf16[4,8,32,1536]{3,2,0,1:T(8,128)(2,1)}), bf16[4,8,32,1536]{3,2,0,1:T(8,128)(2,1)}, u32[]{:S(2)}, u32[]{:S(2)}) async-start(bf16[4,8,32,1536]{3,2,0,1:T(8,128)(2,1)} %reshape.416), calls=%async_computation.3 | async-start | bytes 6291456 | tf_op jit(solution)/shard_map/all_to_all | solution.py:222
  290.3 8.6 %convolution_convert_fusion.2 = bf16[2048,512]{1,0:T(8,128)(2,1)} fusion(bf16[1024,512]{1,0:T(8,128)(2,1)} %bitcast.200, f32[1024,2048]{1,0:T(8,128)} %copy-done.69), kind=kOutput, calls=%fused_computation.46 | convolution fusion | flops 2167406592 | bytes 11534336 | tf_op jit(solution)/shard_map/dot_general | solution.py:19
  300.9 6.1 convolution_convert_fusion.3
  307.1 71.4 %all-to-all-done.3 = bf16[4,8,32,1536]{3,2,0,1:T(8,128)(2,1)} async-done(((bf16[4,8,32,1536]{3,2,0,1:T(8,128)(2,1)}), bf16[4,8,32,1536]{3,2,0,1:T(8,128)(2,1)}, u32[]{:S(2)}, u32[]{:S(2)}) %all-to-all-start.3) | async-done | bytes 3145760 | tf_op jit(solution)/shard_map/all_to_all | solution.py:222
  386.0 6.5 fusion.13
  408.1 5.7 convolution_convert_fusion.6
  414.2 6.5 multiply_reduce_fusion
  420.7 4.6 multiply_convert_fusion
  438.5 9.0 %convolution_convert_fusion.4 = bf16[2048,512]{1,0:T(8,128)(2,1)} fusion(f32[1024,512]{1,0:T(8,128)} %copy-done.23, f32[1024,2048]{1,0:T(8,128)} %copy-done.70), kind=kOutput, calls=%fused_computation.48 | convolution fusion | flops 2167930880 | bytes 12582912 | tf_op jit(solution)/shard_map/dot_general | solution.py:19
  447.6 6.7 convolution_convert_fusion.5
  456.3 26.0 %reduce-scatter.17.cloned.1.call-done = bf16[64,1536]{1,0:T(8,128)(2,1)} async-done(((bf16[512,1536]{1,0:T(8,128)(2,1)}), bf16[64,1536]{1,0:T(8,128)(2,1)}) %reduce-scatter.17.cloned.1.call-update) | async-done | bytes 196624 | tf_op jit(solution)/shard_map/reduce_scatter | solution.py:286
  482.2 34.6 %reduce-scatter.9.cloned.1.call-done = bf16[64,1536]{1,0:T(8,128)(2,1)} async-done(((bf16[512,1536]{1,0:T(8,128)(2,1)}), bf16[64,1536]{1,0:T(8,128)(2,1)}) %reduce-scatter.9.cloned.1.call-update) | async-done | bytes 196624 | tf_op jit(solution)/shard_map/reduce_scatter | solution.py:268
  516.8 36.0 %reduce-scatter.15.cloned.1.call-done = bf16[256,512]{1,0:T(8,128)(2,1)} async-done(((bf16[2048,512]{1,0:T(8,128)(2,1)}), bf16[256,512]{1,0:T(8,128)(2,1)}) %reduce-scatter.15.cloned.1.call-update) | async-done | bytes 262160 | tf_op jit(solution)/shard_map/reduce_scatter | solution.py:280
  552.8 37.7 %reduce-scatter.13.cloned.1.call-done = bf16[64,2048]{1,0:T(8,128)(2,1)} async-done(((bf16[512,2048]{1,0:T(8,128)(2,1)}), bf16[64,2048]{1,0:T(8,128)(2,1)}) %reduce-scatter.13.cloned.1.call-update) | async-done | bytes 262160 | tf_op jit(solution)/shard_map/reduce_scatter | solution.py:277
  590.6 8.9 %convolution_add_fusion.1 = f32[1024,512]{1,0:T(8,128)} fusion(f32[1024,512]{1,0:T(8,128)} %copy-done.12, bf16[2048,512]{1,0:T(8,128)(2,1)} %param.27, f32[1024,2048]{1,0:T(8,128)} %copy-done.69), kind=kOutput, calls=%fused_computation.111 | convolution fusion | flops 2166882304 | bytes 14680064 | tf_op jit(solution)/shard_map/dot_general | solution.py:15
  603.2 13.8 %all-reduce.4 = (bf16[512]{0:T(512)(128)(2,1)S(1)}, bf16[512]{0:T(512)(128)(2,1)S(1)}, bf16[512]{0:T(512)(128)(2,1)S(1)}, bf16[512]{0:T(512)(128)(2,1)S(1)}) all-reduce(bf16[512]{0:T(512)(128)(2,1)S(1)} %get-tuple-element.76, bf16[512]{0:T(512)(128)(2,1)S(1)} %get-tuple-element.74, ...), channel_id=2, replica_groups=mesh['stream'=4,'tm'=8] {'tm'}, use_global_device_ids=true, to_apply=%region_23.24.clone | all-reduce | flops 2048 | bytes 8192
  617.4 9.5 %all-reduce.5 = (bf16[64]{0:T(256)(128)(2,1)S(1)}, bf16[64]{0:T(256)(128)(2,1)S(1)}, bf16[64]{0:T(256)(128)(2,1)S(1)}, bf16[64]{0:T(256)(128)(2,1)S(1)}) all-reduce(bf16[64]{0:T(256)(128)(2,1)S(1)} %dynamic-slice.1, bf16[64]{0:T(256)(128)(2,1)S(1)} %dynamic-slice.3, ...), channel_id=1, replica_groups=mesh['stream'=4,'tm'=8] {'stream'}, use_global_device_ids=true, to_apply=%region_24.25 | all-reduce | flops 256 | bytes 1024 | tf_op jit(solution)/shard_map/psum | solution.py:303
  632.1 29.3 %all-reduce.9.cloned.1.call-done = (bf16[64,1536]{1,0:T(8,128)(2,1)}, bf16[64,512]{1,0:T(8,128)(2,1)}, bf16[64,2048]{1,0:T(8,128)(2,1)}, bf16[256,512]{1,0:T(8,1...) async-done(((bf16[64,1536]{1,0:T(8,128)(2,1)}, bf16[64,512]{1,0:T(8,128)(2,1)}, ...) | async-done | bytes 1572880 | tf_op jit(solution)/shard_map/psum | solution.py:304
  (273 shorter events, 143.7 us)
Async XLA Ops:
  7.2 191.7 %copy-start = (bf16[512,2048]{1,0:T(8,128)(2,1)S(1)}, bf16[512,2048]{1,0:T(8,128)(2,1)}, u32[]{:S(2)}) copy-start(bf16[512,2048]{1,0:T(8,128)(2,1)} %param.26) | copy-start | bytes 6291460
  65.6 73.6 %all-to-all-start = ((bf16[4,1,256,1536]{3,0,1,2:T(4,128)(2,1)}), bf16[4,1,256,1536]{3,0,1,2:T(4,128)(2,1)}, u32[]{:S(2)}, u32[]{:S(2)}) async-start(bf16[4,1,256,1536]{3,0,1,2:T(4,128)(2,1)} %copy.102), calls=%async_computation | async-start | bytes 6291456 | tf_op jit(solution)/shard_map/all_to_all | solution.py:181
  166.7 30.7 %copy-start.7 = (f32[1024,512]{1,0:T(8,128)S(1)}, f32[1024,512]{1,0:T(8,128)}, u32[]{:S(2)}) copy-start(f32[1024,512]{1,0:T(8,128)} %copy-done.6) | copy-start | bytes 6291460
  166.7 30.7 %copy-start.32 = (bf16[512,512]{1,0:T(8,128)(2,1)S(1)}, bf16[512,512]{1,0:T(8,128)(2,1)}, u32[]{:S(2)}) copy-start(bf16[512,512]{1,0:T(8,128)(2,1)} %param.24) | copy-start | bytes 1572868
  198.4 12.9 %copy-start.12 = (f32[1024,512]{1,0:T(8,128)}, f32[1024,512]{1,0:T(8,128)S(1)}, u32[]{:S(2)}) copy-start(f32[1024,512]{1,0:T(8,128)S(1)} %get-tuple-element.117) | copy-start | bytes 6291460
  201.5 6.9 %copy-start.69 = (f32[1024,2048]{1,0:T(8,128)}, f32[1024,2048]{1,0:T(8,128)S(1)}, u32[]{:S(2)}) copy-start(f32[1024,2048]{1,0:T(8,128)S(1)} %fusion.74) | copy-start | bytes 25165828
  214.9 31.2 %all-to-all-start.2 = ((bf16[4,1,256,512]{3,0,1,2:T(4,128)(2,1)}), bf16[4,1,256,512]{3,0,1,2:T(4,128)(2,1)}, u32[]{:S(2)}, u32[]{:S(2)}) async-start(bf16[4,1,256,512]{3,0,1,2:T(4,128)(2,1)} %copy.111), calls=%async_computation.2 | async-start | bytes 2097152 | tf_op jit(solution)/shard_map/all_to_all | solution.py:208
  279.5 98.9 %all-to-all-start.3 = ((bf16[4,8,32,1536]{3,2,0,1:T(8,128)(2,1)}), bf16[4,8,32,1536]{3,2,0,1:T(8,128)(2,1)}, u32[]{:S(2)}, u32[]{:S(2)}) async-start(bf16[4,8,32,1536]{3,2,0,1:T(8,128)(2,1)} %reshape.416), calls=%async_computation.3 | async-start | bytes 6291456 | tf_op jit(solution)/shard_map/all_to_all | solution.py:222
  287.3 168.9 %reduce-scatter.19.cloned.1.call-start = ((), (), s32[]{:S(2)}) async-start(), calls=%async_computation.17 | async-start | bytes 589824 | tf_op jit(solution)/shard_map/reduce_scatter | solution.py:289
  290.0 166.2 %reduce-scatter.23.cloned.1.call-start = ((), (), s32[]{:S(2)}) async-start(), calls=%async_computation.19 | async-start | bytes 2359296 | tf_op jit(solution)/shard_map/reduce_scatter | solution.py:298
  298.9 157.4 %reduce-scatter.21.cloned.1.call-start = ((), (), s32[]{:S(2)}) async-start(), calls=%async_computation.18 | async-start | bytes 2359296 | tf_op jit(solution)/shard_map/reduce_scatter | solution.py:295
  307.0 149.3 %reduce-scatter.11.cloned.1.call-start = ((), (), s32[]{:S(2)}) async-start(), calls=%async_computation.13 | async-start | bytes 589824 | tf_op jit(solution)/shard_map/reduce_scatter | solution.py:271
  386.0 9.5 %copy-start.23 = (f32[1024,512]{1,0:T(8,128)}, f32[1024,512]{1,0:T(8,128)S(1)}, u32[]{:S(2)}) copy-start(f32[1024,512]{1,0:T(8,128)S(1)} %multiply_add_fusion.3) | copy-start | bytes 6291460
  386.0 6.6 copy-start.51
  386.0 6.6 copy-start.54
  386.0 6.6 copy-start.57
  386.0 6.6 copy-start.62
  398.3 84.0 %reduce-scatter.17.cloned.1.call-start = ((), (), s32[]{:S(2)}) async-start(), calls=%async_computation.16 | async-start | bytes 1769472 | tf_op jit(solution)/shard_map/reduce_scatter | solution.py:286
  413.7 103.1 %reduce-scatter.9.cloned.1.call-start = ((), (), s32[]{:S(2)}) async-start(), calls=%async_computation.12 | async-start | bytes 1769472 | tf_op jit(solution)/shard_map/reduce_scatter | solution.py:268
  414.2 13.4 %slice-start = ((s8[8388608]{0:T(1024)(128)(4,1)}), s8[4194304]{0:T(1024)(128)(4,1)S(1)}, s32[]{:S(2)}) async-start(s8[8388608]{0:T(1024)(128)(4,1)} %bitcast.184), calls=%async_computation.21 | async-start | bytes 8388608
  420.7 6.9 %slice-start.1 = ((s8[8388608]{0:T(1024)(128)(4,1)}), s8[4194304]{0:T(1024)(128)(4,1)S(1)}, s32[]{:S(2)}) async-start(s8[8388608]{0:T(1024)(128)(4,1)} %bitcast.184), calls=%async_computation.22 | async-start | bytes 8388608
  438.3 114.5 %reduce-scatter.15.cloned.1.call-start = ((), (), s32[]{:S(2)}) async-start(), calls=%async_computation.15 | async-start | bytes 2359296 | tf_op jit(solution)/shard_map/reduce_scatter | solution.py:280
  447.5 143.0 %reduce-scatter.13.cloned.1.call-start = ((), (), s32[]{:S(2)}) async-start(), calls=%async_computation.14 | async-start | bytes 2359296 | tf_op jit(solution)/shard_map/reduce_scatter | solution.py:277
  454.3 207.0 %all-reduce.9.cloned.1.call-start = ((), (), s32[]{:S(2)}) async-start(), calls=%async_computation.20 | async-start | bytes 3145728 | tf_op jit(solution)/shard_map/psum | solution.py:304
  590.5 8.9 %copy-start.31 = (bf16[192,8,4,256]{3,1,2,0:T(8,128)(2,1)S(1)}, bf16[192,8,4,256]{3,1,2,0:T(8,128)(2,1)}, u32[]{:S(2)}) copy-start(bf16[192,8,4,256]{3,1,2,0:T(8,128)(2,1)} %copy-done.30) | copy-start | bytes 9437188
  590.6 8.9 %copy-start.47 = (f32[1,2,4,128]{3,1,2,0:T(2,128)S(1)}, f32[1,2,4,128]{3,1,2,0:T(2,128)}, u32[]{:S(2)}) copy-start(f32[1,2,4,128]{3,1,2,0:T(2,128)} %copy-done.46) | copy-start | bytes 12292
  590.6 8.9 %copy-start.49 = (f32[1,2,4,128]{3,1,2,0:T(2,128)S(1)}, f32[1,2,4,128]{3,1,2,0:T(2,128)}, u32[]{:S(2)}) copy-start(f32[1,2,4,128]{3,1,2,0:T(2,128)} %copy-done.48) | copy-start | bytes 12292
  590.6 8.9 %copy-start.67 = (bf16[512,1536]{1,0:T(8,128)(2,1)S(1)}, bf16[512,1536]{1,0:T(8,128)(2,1)}, u32[]{:S(2)}) copy-start(bf16[512,1536]{1,0:T(8,128)(2,1)} %param.17) | copy-start | bytes 4718596
  661.3 8.4 %copy-start.42 = (bf16[256,512]{1,0:T(8,128)(2,1)S(1)}, bf16[256,512]{1,0:T(8,128)(2,1)}, u32[]{:S(2)}) copy-start(bf16[256,512]{1,0:T(8,128)(2,1)} %get-tuple-element.93) | copy-start | bytes 786436
  661.3 9.3 %copy-start.41 = (bf16[64,2048]{1,0:T(8,128)(2,1)S(1)}, bf16[64,2048]{1,0:T(8,128)(2,1)}, u32[]{:S(2)}) copy-start(bf16[64,2048]{1,0:T(8,128)(2,1)} %get-tuple-element.96) | copy-start | bytes 786436
  661.3 10.1 %copy-start.40 = (bf16[256,512]{1,0:T(8,128)(2,1)S(1)}, bf16[256,512]{1,0:T(8,128)(2,1)}, u32[]{:S(2)}) copy-start(bf16[256,512]{1,0:T(8,128)(2,1)} %get-tuple-element.97) | copy-start | bytes 786436
  664.4 7.9 %copy-start.1 = (bf16[512,2048]{1,0:T(8,128)(2,1)S(1)}, bf16[512,2048]{1,0:T(8,128)(2,1)}, u32[]{:S(2)}) copy-start(bf16[512,2048]{1,0:T(8,128)(2,1)} %param.26) | copy-start | bytes 6291460
  (57 other events, 159.5 us)
Sparse Core Ops, SparseCore 0:
  290.9 31.3 reduce-scatter.18
  324.7 58.6 reduce-scatter.22
  385.8 29.8 reduce-scatter.20
  418.5 29.3 reduce-scatter.10
  450.1 32.1 reduce-scatter.16
  484.4 32.3 reduce-scatter.8
  519.1 33.6 reduce-scatter.14
  555.7 34.8 reduce-scatter.12
  594.3 66.9 all-reduce.8
where the time goes:
time: 687 us; the launch traced here: 679 us
  waiting for transfers between devices  324 us (47%)
  matrix products  128 us (19%)
  local copies, waits for them, and re-layouts  95 us (14%)
  blocking collectives  54 us (8%)
  other arithmetic  39.3 us (6%)
  starting transfers between devices  22.1 us (3%)
  between operations  15.8 us (2%)
    all_to_all x1, waiting for transfers between devices, per_device(): lax.all_to_all(grad_packed.reshape(pack_count, frame_count, local_count,...  71.4 us
    all_to_all x1, waiting for transfers between devices, per_device(): lax.all_to_all(packed.reshape(pack_count, slot_count, patches, 3 * model_...  68.2 us
    dot_general x8, matrix products, contract_rows(): lax.dot_general(left, right, (((0,), (0,)), ((), ())), preferred_element_...  43.4 us
    reduce_scatter x1, waiting for transfers between devices, per_device(): lax.psum_scatter(partial_sums[4].astype(jnp.bfloat16), 'tm', scatter_dime...  37.7 us
    reduce_scatter x1, waiting for transfers between devices, per_device(): lax.psum_scatter(partial_sums[5].astype(jnp.bfloat16), 'tm', scatter_dime...  36 us
    reduce_scatter x1, waiting for transfers between devices, per_device(): lax.psum_scatter(partial_sums[1].astype(jnp.bfloat16), 'tm', scatter_dime...  34.6 us
    all_to_all x1, blocking collectives, per_device(): lax.all_to_all(mixed, 'tm', split_axis=1, concat_axis=2, tiled=True)  30.6 us
    psum x1, waiting for transfers between devices, per_device(): lax.psum(shares[1].astype(jnp.bfloat16), 'stream').astype(jnp.float32)  29.3 us
  transfers between devices with their start and end apart: 12, of which 8 were waited for; matrix products, arithmetic and copies ran while one was open for 16% of the time, Pallas kernels for 0%

commit v1 on v0

v1 whole, which is shorter than its diff:
```python
import functools

import jax
import jax.numpy as jnp
from jax import lax
from jax.experimental import pallas as pl
from jax.experimental.pallas import tpu as pltpu
from jax.sharding import PartitionSpec as P

HEADS = 8
EPS = 1e-05
GELU_A = 0.7978845608028654
GELU_B = 0.044715
BF = jnp.bfloat16
F32 = jnp.float32
CHUNK = 512
VMEM = 44 * 1024 * 1024


def nn(a, b):
    return jnp.dot(a, b, preferred_element_type=F32)


def nt(a, b):
    return lax.dot_general(a, b, (((1,), (1,)), ((), ())), preferred_element_type=F32)


def tn(a, b):
    return lax.dot_general(a, b, (((0,), (0,)), ((), ())), preferred_element_type=F32)


def unit(values):
    average = jnp.mean(values, axis=-1, keepdims=True)
    centered = values - average
    inverse = lax.rsqrt(jnp.mean(centered * centered, axis=-1, keepdims=True) + EPS)
    return centered * inverse, inverse


def unit_backward(grad, unit_rows, inverse):
    first = jnp.mean(grad, axis=-1, keepdims=True)
    second = jnp.mean(grad * unit_rows, axis=-1, keepdims=True)
    return inverse * (grad - first - unit_rows * second)


def gelu_parts(u):
    square = u * u
    tangent = jnp.tanh(u * (GELU_A + (GELU_A * GELU_B) * square))
    half = 0.5 * u
    value = half + half * tangent
    slope = (0.5 + 0.5 * tangent) + half * (1.0 - tangent * tangent) * (
        GELU_A + (3.0 * GELU_A * GELU_B) * square
    )
    return value, slope


def head_masks(width):
    lane = lax.broadcasted_iota(jnp.int32, (1, 2 * width), 1)
    low = lane < width
    return low, (low.astype(F32).astype(BF), (1.0 - low.astype(F32)).astype(BF))


def attend(qkv_ref, p_ref, o_ref, bias_ref):
    width = qkv_ref.shape[1] // 3
    size = width // HEADS
    low, masks = head_masks(size)
    for pair in range(HEADS // 2):
        at = pair * 2 * size
        q = qkv_ref[:, at : at + 2 * size] * BF(size**-0.5)
        k = qkv_ref[:, width + at : width + at + 2 * size]
        v = qkv_ref[:, 2 * width + at : 2 * width + at + 2 * size]
        both = []
        for side in range(2):
            scores = nt(k * masks[side], q)
            if bias_ref is not None:
                scores = scores + bias_ref[...]
            top = jnp.max(scores, axis=0, keepdims=True)
            e = jnp.exp(scores - top)
            total = jnp.sum(e, axis=0, keepdims=True)
            p = (e * (1.0 / total)).astype(BF)
            p_ref[2 * pair + side] = p
            both.append(tn(p, v))
        o_ref[:, at : at + 2 * size] = jnp.where(low, both[0], both[1]).astype(BF)


def attend_backward(qkv_ref, p_ref, go_ref, out_ref):
    width = qkv_ref.shape[1] // 3
    size = width // HEADS
    low, masks = head_masks(size)
    for pair in range(HEADS // 2):
        at = pair * 2 * size
        q = qkv_ref[:, at : at + 2 * size] * BF(size**-0.5)
        k = qkv_ref[:, width + at : width + at + 2 * size] * BF(size**-0.5)
        v = qkv_ref[:, 2 * width + at : 2 * width + at + 2 * size]
        go = go_ref[:, at : at + 2 * size]
        gq, gk, gv = [], [], []
        for side in range(2):
            p = p_ref[2 * pair + side]
            gv.append(nn(p, go))
            gp = nt(v * masks[side], go)
            p32 = p.astype(F32)
            weighted = p32 * gp
            gs = (weighted - p32 * jnp.sum(weighted, axis=0, keepdims=True)).astype(BF)
            gk.append(nn(gs, q))
            gq.append(tn(gs, k))
        out_ref[:, at : at + 2 * size] = jnp.where(low, gq[0], gq[1]).astype(BF)
        out_ref[:, width + at : width + at + 2 * size] = jnp.where(low, gk[0], gk[1]).astype(BF)
        out_ref[:, 2 * width + at : 2 * width + at + 2 * size] = jnp.where(
            low, gv[0], gv[1]
        ).astype(BF)


def feed_up(m, up_ref, down_ref, h_ref, slope_ref):
    total = None
    for at in range(0, up_ref.shape[1], CHUNK):
        value, slope = gelu_parts(nn(m, up_ref[:, at : at + CHUNK]))
        h = value.astype(BF)
        h_ref[:, at : at + CHUNK] = h
        slope_ref[:, at : at + CHUNK] = slope.astype(BF)
        term = nn(h, down_ref[at : at + CHUNK, :])
        total = term if total is None else total + term
    return total


def feed_back(e2, up_ref, down_ref, slope_ref, eu_ref):
    total = None
    for at in range(0, up_ref.shape[1], CHUNK):
        gh = nt(e2, down_ref[at : at + CHUNK, :])
        eu = (gh * slope_ref[:, at : at + CHUNK].astype(F32)).astype(BF)
        eu_ref[:, at : at + CHUNK] = eu
        term = nt(eu, up_ref[:, at : at + CHUNK])
        total = term if total is None else total + term
    return total


def rows_of(block):
    slots, _, patches, width = block.shape
    return block[:, 0].astype(F32).reshape(slots * patches, width)


def block_of(rows, ref):
    slots, _, patches, width = ref.shape
    ref[:, 0] = rows.reshape(slots, patches, width).astype(ref.dtype)


def space_forward(
    local, order, frames, gain, w_in, w_out, scale, w_up, w_down, *rest
):
    x2, z0, inv0, qkv, p, o, z1, inv1, h, slope = rest[-10:]
    x = frames[0, 0].astype(F32)
    unit0, inverse0 = unit(x)
    z0[0] = unit0.astype(BF)
    inv0[0] = inverse0
    qkv[0] = nn((unit0 * gain[...]).astype(BF), w_in[...]).astype(BF)
    attend(qkv.at[0], p.at[0], o.at[0], None)
    r1 = x + nn(o[0], w_out[...])
    unit1, inverse1 = unit(r1)
    z1[0] = unit1.astype(BF)
    inv1[0] = inverse1
    m = (unit1 * scale[...]).astype(BF)
    r2 = r1 + feed_up(m, w_up, w_down, h.at[0], slope.at[0])
    if local:
        x2[0] = r2
    else:
        block_of(r2, x2)


def build_bias(labels, pack, slots, patches, bias):
    tokens = slots * patches
    row = lax.broadcasted_iota(jnp.int32, (1, tokens), 1)
    column = lax.broadcasted_iota(jnp.int32, (tokens, 1), 0)

    def label_of(position):
        slot = position // patches
        value = jnp.zeros_like(position)
        for f in range(slots):
            value = jnp.where(slot == f, labels[pack, f], value)
        return value

    same_patch = (row % patches) == (column % patches)
    allowed = same_patch & (column <= row) & (label_of(column) == label_of(row))
    bias[...] = jnp.where(allowed, 0.0, -1e30)


def time_both(
    order, labels, x2, grad, gain, w_in, w_out, scale, w_up, w_down, *rest
):
    g0, out, z0, gqkv, o, e1, z1, eu, h, e2 = rest[-14:-4]
    qkv, p, slope, bias = rest[-4:]
    slots, _, patches, _ = x2.shape
    build_bias(labels, order[pl.program_id(0)], slots, patches, bias)
    x = rows_of(x2[...])
    unit0, inverse0 = unit(x)
    z0[0] = unit0.astype(BF)
    qkv[...] = nn((unit0 * gain[...]).astype(BF), w_in[...]).astype(BF)
    attend(qkv, p, o.at[0], bias)
    r1 = x + nn(o[0], w_out[...])
    unit1, inverse1 = unit(r1)
    z1[0] = unit1.astype(BF)
    m = (unit1 * scale[...]).astype(BF)
    block_of(r1 + feed_up(m, w_up, w_down, h.at[0], slope), out)
    g2 = rows_of(grad[...])
    e2[0] = g2.astype(BF)
    gm = feed_back(e2[0], w_up, w_down, slope, eu.at[0])
    g1 = g2 + unit_backward(gm * scale[...], unit1, inverse1)
    e1[0] = g1.astype(BF)
    slope[:, : g1.shape[1]] = nt(e1[0], w_out[...]).astype(BF)
    attend_backward(qkv, p, slope, gqkv.at[0])
    gn = nt(gqkv[0], w_in[...])
    block_of(g1 + unit_backward(gn * gain[...], unit0, inverse0), g0)


def time_alone(
    order, x2, grad, gain, w_in, w_out, scale, w_up, w_down, *rest
):
    g0, out, z0, gqkv, o, e1, z1, eu, h, e2 = rest[-11:-1]
    slope = rest[-1]
    x = x2[0]
    width = x.shape[1]
    unit0, inverse0 = unit(x)
    z0[0] = unit0.astype(BF)
    o[0] = nn((unit0 * gain[...]).astype(BF), w_in[:, 2 * width :]).astype(BF)
    r1 = x + nn(o[0], w_out[...])
    unit1, inverse1 = unit(r1)
    z1[0] = unit1.astype(BF)
    m = (unit1 * scale[...]).astype(BF)
    out[0, 0] = r1 + feed_up(m, w_up, w_down, h.at[0], slope)
    e2[0] = grad[0, 0]
    g2 = grad[0, 0].astype(F32)
    gm = feed_back(e2[0], w_up, w_down, slope, eu.at[0])
    g1 = g2 + unit_backward(gm * scale[...], unit1, inverse1)
    e1[0] = g1.astype(BF)
    gv = nt(e1[0], w_out[...]).astype(BF)
    gqkv[0, :, : 2 * width] = jnp.zeros((x.shape[0], 2 * width), BF)
    gqkv[0, :, 2 * width :] = gv
    gn = nt(gv, w_in[:, 2 * width :])
    g0[0] = g1 + unit_backward(gn * gain[...], unit0, inverse0)


def space_back_feed(
    local, order, grad, z1, inv1, slope, w_out, scale, w_up, w_down, *rest
):
    eu, e2, e1, go, g1 = rest[-5:]
    g2 = grad[0] if local else rows_of(grad[...])
    e2[0] = g2.astype(BF)
    gm = feed_back(e2[0], w_up, w_down, slope.at[0], eu.at[0])
    total = g2 + unit_backward(gm * scale[...], z1[0].astype(F32), inv1[0])
    g1[0] = total
    e1[0] = total.astype(BF)
    go[0] = nt(e1[0], w_out[...]).astype(BF)


def space_back_attend(order, qkv, p, go, *rest):
    attend_backward(qkv.at[0], p.at[0], go.at[0], rest[-1].at[0])


def space_back_in(order, gqkv, w_in, gain, z0, inv0, g1, *rest):
    gn = nt(gqkv[0], w_in[...])
    rest[-1][0, 0] = g1[0] + unit_backward(gn * gain[...], z0[0].astype(F32), inv0[0])


def to_send(order, grad, out):
    block_of(grad[0, 0].astype(F32), out)


def from_received(order, block, before, out):
    out[0, 0] = rows_of(block[...])


class Packs:
    def __init__(self, order, labels, first, count, slots, patches):
        self.scalars = (order, labels)
        self.first, self.count = first, count
        self.slots, self.patches = slots, patches

    def call(self, kernel, args, outs, scratch=(), labels=False, flops=0):
        first = self.first
        scalars = self.scalars if labels else self.scalars[:1]

        def spec(kind, shape):
            rank = len(shape)
            if kind == "whole":
                return pl.BlockSpec(shape, lambda i, *s: (0,) * rank)
            if kind == "pack":
                return pl.BlockSpec(
                    (1,) + tuple(shape[1:]), lambda i, *s: (s[0][first + i],) + (0,) * (rank - 1)
                )
            if kind == "place":
                return pl.BlockSpec(
                    (1,) + tuple(shape[1:]), lambda i, *s: (first + i,) + (0,) * (rank - 1)
                )
            if kind == "step":
                return pl.BlockSpec(
                    (1,) + tuple(shape[1:]), lambda i, *s: (i,) + (0,) * (rank - 1)
                )
            if kind == "moved":
                return pl.BlockSpec(
                    (shape[0], 1, shape[2], shape[3]), lambda i, *s: (0, i, 0, 0)
                )
            return pl.BlockSpec(memory_space=pl.ANY)

        in_specs = [spec(kind, array.shape) for kind, array in args]
        operands = [array for _, array in args]
        aliases = {}
        for index, (kind, shape, dtype, into) in enumerate(outs):
            if into is not None:
                aliases[len(scalars) + len(operands)] = index
                operands.append(into)
                in_specs.append(pl.BlockSpec(memory_space=pl.ANY))
        moved = sum(a.size * a.dtype.itemsize for a in operands)
        return pl.pallas_call(
            kernel,
            out_shape=[jax.ShapeDtypeStruct(shape, dtype) for _, shape, dtype, _ in outs],
            grid_spec=pltpu.PrefetchScalarGridSpec(
                num_scalar_prefetch=len(scalars),
                grid=(self.count,),
                in_specs=in_specs,
                out_specs=[spec(kind, shape) for kind, shape, _, _ in outs],
                scratch_shapes=list(scratch),
            ),
            input_output_aliases=aliases,
            compiler_params=pltpu.CompilerParams(
                vmem_limit_bytes=VMEM, dimension_semantics=("arbitrary",)
            ),
            cost_estimate=pl.CostEstimate(
                flops=int(flops * self.count), bytes_accessed=int(moved), transcendentals=0
            ),
        )(*scalars, *operands)


def feed_weights_kernel(ids, z1, e2, eu, h, mine, other, left):
    step = pl.program_id(0)
    core, z_at, s_at = ids[0], ids[1], ids[2]
    first = core == 0

    def put(at, rows, even, odd):
        mine[at[0], at[1], rows] = jnp.where(first, even, odd)
        other[at[0], at[1], rows] = jnp.where(first, odd, even)

    @pl.when(step == 0)
    def _():
        left[...] = z1[...].T

    @pl.when(step == 4)
    def _():
        left[...] = e2[...].T

    @pl.when(step < 4)
    def _():
        tile = nn(left[...], eu[...]).astype(BF)
        for z in range(4):
            even, odd = tile[128 * z : 128 * z + 64], tile[128 * z + 64 : 128 * z + 128]
            put((step ^ s_at, z ^ z_at), slice(0, 64), even, odd)

    @pl.when(step >= 4)
    def _():
        tile = nn(left[...], h[...]).astype(BF)
        z = step - 4
        for s in range(4):
            upper, lower = tile[128 * s : 128 * s + 64], tile[128 * s + 64 : 128 * s + 128]
            even = jnp.concatenate([upper[:, :256], lower[:, :256]], axis=1)
            odd = jnp.concatenate([upper[:, 256:], lower[:, 256:]], axis=1)
            put((s ^ s_at, z ^ z_at), slice(64, 128), even, odd)


def attend_weights_kernel(ids, z0, o, gqkv, e1, mine, other, left):
    step = pl.program_id(0)
    core, z_at, s_at = ids[0], ids[1], ids[2]
    first = core == 0

    def put_all(tile, index):
        for z in range(4):
            for s in range(4):
                at = 128 * z + 16 * s
                even, odd = tile[at : at + 16], tile[at + 64 : at + 80]
                rows = slice(16 * index, 16 * index + 16)
                mine[s ^ s_at, z ^ z_at, rows] = jnp.where(first, even, odd)
                other[s ^ s_at, z ^ z_at, rows] = jnp.where(first, odd, even)

    @pl.when(step == 0)
    def _():
        left[...] = z0[...].T

    @pl.when(step == 3)
    def _():
        left[...] = o[...].T

    for index in range(4):

        @pl.when(step == index)
        def _():
            right = gqkv if index < 3 else e1
            put_all(nn(left[...], right[...]).astype(BF), index)


def weights_call(kernel, ids, steps, rows, args):
    def spec(kind, shape):
        if kind == "whole":
            return pl.BlockSpec(shape, lambda i, *s: (0, 0))
        low, high = kind
        return pl.BlockSpec(
            (shape[0], CHUNK), lambda i, *s: (0, jnp.clip(i - low, 0, high - low))
        )

    tokens = args[0][1].shape[0]
    out = jax.ShapeDtypeStruct((4, 4, rows, CHUNK), BF)
    out_spec = pl.BlockSpec((4, 4, rows, CHUNK), lambda i, *s: (0, 0, 0, 0))
    return pl.pallas_call(
        kernel,
        out_shape=[out, out],
        grid_spec=pltpu.PrefetchScalarGridSpec(
            num_scalar_prefetch=1,
            grid=(steps,),
            in_specs=[spec(kind, array.shape) for kind, array in args],
            out_specs=[out_spec, out_spec],
            scratch_shapes=[pltpu.VMEM((CHUNK, tokens), BF)],
        ),
        compiler_params=pltpu.CompilerParams(
            vmem_limit_bytes=VMEM, dimension_semantics=("arbitrary",)
        ),
        cost_estimate=pl.CostEstimate(
            flops=steps * 2 * tokens * CHUNK * CHUNK,
            bytes_accessed=sum(a.size * 2 for _, a in args),
            transcendentals=0,
        ),
    )(ids, *[array for _, array in args])


def swap(array, axis, size, mask):
    return lax.ppermute(array, axis, [(i, i ^ mask) for i in range(size)])


def add(*terms):
    total = terms[0].astype(F32)
    for term in terms[1:]:
        total = total + term.astype(F32)
    return total.astype(BF)


def reduce_parts(mine, other):
    got = swap(other, "tm", 8, 1)
    parts = [add(mine[d], got[d]) for d in range(4)]
    got = [swap(parts[d], "stream", 4, d) for d in range(1, 4)]
    rows = [add(parts[0][d], got[0][d], got[1][d], got[2][d]) for d in range(4)]
    got = [swap(rows[d], "tm", 8, 2 * d) for d in range(1, 4)]
    final = add(rows[0], *got)
    return [final] + [swap(final, "stream", 4, d) for d in range(1, 4)]


def column(row):
    size = row.shape[1]
    eye = lax.broadcasted_iota(jnp.int32, (size, size), 0) == lax.broadcasted_iota(
        jnp.int32, (size, size), 1
    )
    return jnp.sum(jnp.where(eye, row, 0.0), axis=1, keepdims=True)


def as_row(col):
    size = col.shape[0]
    eye = lax.broadcasted_iota(jnp.int32, (size, size), 0) == lax.broadcasted_iota(
        jnp.int32, (size, size), 1
    )
    return jnp.sum(jnp.where(eye, col, 0.0), axis=0, keepdims=True)


def own_rows(ids, vector):
    rank = 2 * ids[1] + ids[0]
    return column(vector[pl.ds(rank, 1), :])


def finish_feed_kernel(ids, p0, p1, p2, p3, w_up, scale, scale_grad, up_grad, down_grad):
    s_at = ids[2]
    factor = own_rows(ids, scale)
    for d, piece in enumerate((p0, p1, p2, p3)):
        s = s_at ^ d
        up_grad[:, pl.ds(pl.multiple_of(512 * s, 512), 512)] = piece[:64].astype(F32)
        lower = piece[64:].astype(F32)
        whole = jnp.concatenate([lower[:, :256], lower[:, 256:]], axis=0)
        down_grad[:, pl.ds(pl.multiple_of(128 * s, 128), 128)] = whole.T
    total = up_grad[...]
    scale_grad[...] = as_row(jnp.sum(total * w_up[...].astype(F32), axis=1, keepdims=True))
    up_grad[...] = total * factor


def finish_attend_kernel(ids, p0, p1, p2, p3, w_in, gain, gain_grad, in_grad, out_grad):
    s_at = ids[2]
    factor = own_rows(ids, gain)
    for d, piece in enumerate((p0, p1, p2, p3)):
        rows = pl.ds(pl.multiple_of(16 * (s_at ^ d), 16), 16)
        for third in range(3):
            in_grad[rows, 512 * third : 512 * third + 512] = piece[
                16 * third : 16 * third + 16
            ].astype(F32)
        out_grad[rows, :] = piece[48:].astype(F32)
    total = in_grad[...]
    gain_grad[...] = as_row(jnp.sum(total * w_in[...].astype(F32), axis=1, keepdims=True))
    in_grad[...] = total * factor


def finish_call(kernel, ids, pieces, weight, vector, outs):
    height = weight.shape[0] // 8
    whole = pl.BlockSpec(pieces[0].shape, lambda i, *s: (0, 0))
    results = pl.pallas_call(
        kernel,
        out_shape=[jax.ShapeDtypeStruct(shape, F32) for shape in outs],
        grid_spec=pltpu.PrefetchScalarGridSpec(
            num_scalar_prefetch=1,
            grid=(1,),
            in_specs=[whole] * 4
            + [
                pl.BlockSpec((height, weight.shape[1]), lambda i, s: (2 * s[1] + s[0], 0)),
                pl.BlockSpec((8, height), lambda i, *s: (0, 0)),
            ],
            out_specs=[pl.BlockSpec(shape, lambda i, *s: (0, 0)) for shape in outs],
        ),
        compiler_params=pltpu.CompilerParams(vmem_limit_bytes=VMEM),
    )(ids, *pieces, weight, vector.reshape(8, height))
    return [results[0].reshape(-1)] + list(results[1:])


def plain_weights(z, grads, weight, vector):
    product = tn(z, grads)
    vector_grad = jnp.sum(product * weight.astype(F32), axis=1)
    return vector_grad, product * vector[:, None]


def plain_reduce(array):
    share = lax.psum_scatter(array.astype(BF), "tm", scatter_dimension=0, tiled=True)
    return lax.psum(share, "stream").astype(F32)


def per_device(
    ranks,
    streams,
    frames,
    space_gain,
    space_input,
    space_output,
    space_scale,
    space_up,
    space_down,
    time_gain,
    time_input,
    time_output,
    time_scale,
    time_up,
    time_down,
    clip_labels,
    output_grad,
):
    packs, _, tokens, width = frames.shape
    slots = clip_labels.shape[1]
    patches = tokens // ranks
    hidden = space_up.shape[1]
    some = packs - 1
    hierarchical = (ranks, streams) == (8, 4)
    tm = lax.axis_index("tm")
    ids = jnp.stack([tm % 2, tm // 2, lax.axis_index("stream")]).astype(jnp.int32)

    alone = jnp.argmax(clip_labels[:, -1] == slots - 1).astype(jnp.int32)
    place = jnp.arange(packs, dtype=jnp.int32)
    order = jnp.where(place == packs - 1, alone, place + (place >= alone))
    shared = Packs(order, clip_labels, 0, some, slots, patches)
    single = Packs(order, clip_labels, some, 1, slots, patches)

    row = lambda vector: vector.reshape(1, -1)
    moved = ("moved", (slots, some, patches, width), BF, None)

    def kept(*widths):
        return [("place", (packs, tokens) + w, t, None) for *w, t in [tuple(w) for w in widths]]

    def into(specs, arrays):
        return [(kind, shape, dtype, a) for (kind, shape, dtype, _), a in zip(specs, arrays)]

    def exchange(array):
        return lax.all_to_all(array, "tm", split_axis=0, concat_axis=0, tiled=True)

    def place_spec(*tail, dtype=BF):
        return ("place", (packs,) + tail, dtype, None)

    (sent,) = shared.call(to_send, [("pack", output_grad)], [moved])
    grad_moved = exchange(sent)

    space_args = [
        ("pack", frames),
        ("whole", row(space_gain)),
        ("whole", space_input),
        ("whole", space_output),
        ("whole", row(space_scale)),
        ("whole", space_up),
        ("whole", space_down),
    ]
    state = [
        place_spec(tokens, width),
        place_spec(tokens, 1, dtype=F32),
        place_spec(tokens, 3 * width),
        place_spec(HEADS, tokens, tokens),
        place_spec(tokens, width),
        place_spec(tokens, width),
        place_spec(tokens, 1, dtype=F32),
        place_spec(tokens, hidden),
        place_spec(tokens, hidden),
    ]
    flops = 2 * tokens * width * (4 * width + 2 * hidden)
    x2, *held = shared.call(
        functools.partial(space_forward, False), space_args, [moved] + state, flops=flops
    )
    x2_moved = exchange(x2)
    local = ("step", (1, tokens, width), F32, None)
    x2_alone, *held = single.call(
        functools.partial(space_forward, True),
        space_args,
        [local] + into(state, held),
        flops=flops,
    )
    sz0, sinv0, sqkv, sp, so, sz1, sinv1, sh, sslope = held

    time_args = [
        ("whole", row(time_gain)),
        ("whole", time_input),
        ("whole", time_output),
        ("whole", row(time_scale)),
        ("whole", time_up),
        ("whole", time_down),
    ]
    state = [
        place_spec(tokens, width),
        place_spec(tokens, 3 * width),
        place_spec(tokens, width),
        place_spec(tokens, width),
        place_spec(tokens, width),
        place_spec(tokens, hidden),
        place_spec(tokens, hidden),
        place_spec(tokens, width),
    ]
    g0_alone, result, *held = single.call(
        time_alone,
        [("step", x2_alone), ("pack", output_grad)] + time_args,
        [local, ("pack", frames.shape, F32, None)] + state,
        scratch=[pltpu.VMEM((tokens, hidden), BF)],
        flops=3 * flops,
    )
    g0, out, *held = shared.call(
        time_both,
        [("moved", x2_moved), ("moved", grad_moved)] + time_args,
        [moved, moved] + into(state, held),
        scratch=[
            pltpu.VMEM((tokens, 3 * width), BF),
            pltpu.VMEM((HEADS, tokens, tokens), BF),
            pltpu.VMEM((tokens, hidden), BF),
            pltpu.VMEM((tokens, tokens), F32),
        ],
        labels=True,
        flops=3 * flops,
    )
    tz0, tgqkv, to, te1, tz1, teu, th, te2 = held
    g0_moved = exchange(g0)
    out_moved = exchange(out)

    def flat(array):
        return array.reshape(packs * tokens, array.shape[-1])

    def feed_weights(z1, eu, h, e2):
        return weights_call(
            feed_weights_kernel,
            ids,
            8,
            128,
            [("whole", flat(z1)), ("whole", flat(e2)), ((0, 3), flat(eu)), ((4, 7), flat(h))],
        )

    def attend_weights(z0, gqkv, o, e1):
        return weights_call(
            attend_weights_kernel,
            ids,
            4,
            64,
            [("whole", flat(z0)), ("whole", flat(o)), ((0, 2), flat(gqkv)), ("whole", flat(e1))],
        )

    def feed_grads(z1, eu, h, e2, scale, up):
        if hierarchical:
            pieces = reduce_parts(*feed_weights(z1, eu, h, e2))
            return finish_call(
                finish_feed_kernel,
                ids,
                pieces,
                up,
                scale,
                [(1, width // 8), (width // 8, hidden), (hidden // 8, width)],
            )
        scale_grad, up_grad = plain_weights(flat(z1), flat(eu), up, scale)
        return [plain_reduce(a) for a in (scale_grad, up_grad, tn(flat(h), flat(e2)))]

    def attend_grads(z0, gqkv, o, e1, gain, w_in):
        if hierarchical:
            pieces = reduce_parts(*attend_weights(z0, gqkv, o, e1))
            return finish_call(
                finish_attend_kernel,
                ids,
                pieces,
                w_in,
                gain,
                [(1, width // 8), (width // 8, 3 * width), (width // 8, width)],
            )
        gain_grad, in_grad = plain_weights(flat(z0), flat(gqkv), w_in, gain)
        return [plain_reduce(a) for a in (gain_grad, in_grad, tn(flat(o), flat(e1)))]

    time_feed = feed_grads(tz1, teu, th, te2, time_scale, time_up)
    time_attend = attend_grads(tz0, tgqkv, to, te1, time_gain, time_input)

    back = [
        place_spec(tokens, hidden),
        place_spec(tokens, width),
        place_spec(tokens, width),
        place_spec(tokens, width),
        place_spec(tokens, width, dtype=F32),
    ]
    feed_args = [
        ("place", sz1),
        ("place", sinv1),
        ("place", sslope),
        ("whole", space_output),
        ("whole", row(space_scale)),
        ("whole", space_up),
        ("whole", space_down),
    ]
    held = single.call(
        functools.partial(space_back_feed, True), [("step", g0_alone)] + feed_args, back, flops=flops
    )
    held = shared.call(
        functools.partial(space_back_feed, False),
        [("moved", g0_moved)] + feed_args,
        into(back, held),
        flops=flops,
    )
    seu, se2, se1, sgo, sg1 = held
    space_feed = feed_grads(sz1, seu, sh, se2, space_scale, space_up)
    whole_packs = Packs(order, clip_labels, 0, packs, slots, patches)
    (sgqkv,) = whole_packs.call(
        space_back_attend,
        [("place", sqkv), ("place", sp), ("place", sgo)],
        [place_spec(tokens, 3 * width)],
        flops=flops,
    )
    space_attend = attend_grads(sz0, sgqkv, so, se1, space_gain, space_input)
    (input_grad,) = whole_packs.call(
        space_back_in,
        [
            ("place", sgqkv),
            ("whole", space_input),
            ("whole", row(space_gain)),
            ("place", sz0),
            ("place", sinv0),
            ("place", sg1),
        ],
        [("pack", frames.shape, F32, None)],
        flops=flops // 4,
    )
    (result,) = shared.call(
        from_received, [("moved", out_moved)], [("pack", frames.shape, F32, result)]
    )
    return (
        result,
        input_grad,
        space_attend[0],
        space_attend[1],
        space_attend[2],
        space_feed[0],
        space_feed[1],
        space_feed[2],
        time_attend[0],
        time_attend[1],
        time_attend[2],
        time_feed[0],
        time_feed[1],
        time_feed[2],
    )


def solution(mesh):
    tokens = P("stream", "tm", None, None)
    vector, matrix = P("tm"), P("tm", None)
    return jax.shard_map(
        functools.partial(per_device, mesh.shape["tm"], mesh.shape["stream"]),
        mesh=mesh,
        in_specs=(tokens,) + (P(),) * 12 + (P("stream", None), tokens),
        out_specs=(tokens, tokens) + (vector, matrix, matrix, vector, matrix, matrix) * 2,
        check_vma=False,
    )
```

time: 687 us -> 367 us (0.53)
  the two profiles are of different devices: /device:TPU:16 before, /device:TPU:0 now
where the time goes in v1:
time: 367 us; the launch traced here: 361 us
  Pallas kernels  146 us (40%)
  starting transfers between devices  72.6 us (20%)
  local copies, waits for them, and re-layouts  65.8 us (18%)
  waiting for transfers between devices  50.8 us (14%)
  other arithmetic  23.7 us (6%)
    pallas_call x10, Pallas kernels, call(): pl.pallas_call(kernel, out_shape=[jax.ShapeDtypeStruct(shape, dtype) for...  105 us
    unnamed x208, local copies, waits for them, and re-layouts  65.5 us
    ppermute x40, starting transfers between devices, swap(): return lax.ppermute(array, axis, [(i, i ^ mask) for i in range(size)])  51.4 us
    pallas_call x4, Pallas kernels, weights_call(): pl.pallas_call(kernel, out_shape=[out, out], grid_spec=pltpu.PrefetchScal...  35 us
    ppermute x40, waiting for transfers between devices, swap(): return lax.ppermute(array, axis, [(i, i ^ mask) for i in range(size)])  32.6 us
    all_to_all x4, starting transfers between devices, exchange(): return lax.all_to_all(array, 'tm', split_axis=0, concat_axis=0, tiled=True)  21.1 us
    all_to_all x4, waiting for transfers between devices, exchange(): return lax.all_to_all(array, 'tm', split_axis=0, concat_axis=0, tiled=True)  18.2 us
    convert_element_type x8, other arithmetic, add(): return total.astype(BF)  15.5 us
  transfers between devices with their start and end apart: 44, of which 10 were waited for; matrix products, arithmetic and copies ran while one was open for 6% of the time, Pallas kernels for 26%

profile of v1, /device:TPU:0, one launch (start us, length us, event | category | flops | bytes accessed | tf_op | source)
XLA Modules:
  0.0 360.7 jit_solution(9645873741205588255)
XLA Ops:
  9.5 17.8 %shard_map.254 = (bf16[8,3,32,512]{3,2,1,0:T(8,128)(2,1)S(1)}, bf16[4,256,512]{2,1,0:T(8,128)(2,1)S(1)}, f32[4,256,1]{2,1,0:T(8,128)S(1)}, bf16[4,256,1536]{2,1,...) custom-call(s32[4]{0:T(128)S(1)} %compare_select_fusion.order, ...), custom_call_target="tpu_custom_call" | custom-call | flops 4831838208 | bytes 7344128 | tf_op jit(solution)/shard_map/pallas_call | solution.py:310
  31.7 6.3 %all-to-all-start = ((bf16[8,3,32,512]{3,2,1,0:T(8,128)(2,1)}), bf16[8,3,32,512]{3,2,1,0:T(8,128)(2,1)}, u32[]{:S(2)}, u32[]{:S(2)}) async-start(bf16[8,3,32,512]{3,2,1,0:T(8,128)(2,1)} %copy-done.59), calls=%async_computation | async-start | bytes 1572864 | tf_op jit(solution)/shard_map/all_to_all | solution.py:575
  40.9 18.2 %all-to-all-done.x2 = bf16[8,3,32,512]{3,2,1,0:T(8,128)(2,1)} async-done(((bf16[8,3,32,512]{3,2,1,0:T(8,128)(2,1)}), bf16[8,3,32,512]{3,2,1,0:T(8,128)(2,1)}, u32[]{:S(2)}, u32[]{:S(2)}) %all-to-all-start) | async-done | bytes 786464 | tf_op jit(solution)/shard_map/all_to_all | solution.py:575
  59.1 4.8 %all-to-all-start.1 = ((bf16[8,3,32,512]{3,2,1,0:T(8,128)(2,1)}), bf16[8,3,32,512]{3,2,1,0:T(8,128)(2,1)}, u32[]{:S(2)}, u32[]{:S(2)}) async-start(bf16[8,3,32,512]{3,2,1,0:T(8,128)(2,1)} %copy-done.23), calls=%async_computation.1 | async-start | bytes 1572864 | tf_op jit(solution)/shard_map/all_to_all | solution.py:575
  72.1 8.1 %shard_map.256 = (f32[1,256,512]{2,1,0:T(8,128)S(1)}, bf16[4,256,512]{2,1,0:T(8,128)(2,1)S(1)}, f32[4,256,1]{2,1,0:T(8,128)S(1)}, bf16[4,256,1536]{2,1,0:T(8,128...) custom-call(s32[4]{0:T(128)S(1)} %compare_select_fusion.order, ...), custom_call_target="tpu_custom_call", output_to_operand_aliasing={{1}: (8, {}), {2}: (9, {}), {3}: (10, {}), {4}: (11, {}), {... | custom-call | flops 1610612736 | bytes 26226688 | tf_op jit(solution)/shard_map/pallas_call | solution.py:310
  83.8 8.8 %shard_map.257 = (f32[1,256,512]{2,1,0:T(8,128)S(1)}, f32[4,1,256,512]{3,2,1,0:T(8,128)}, bf16[4,256,512]{2,1,0:T(8,128)(2,1)S(1)}, bf16[4,256,1536]{2,1,0:T(8,1...) custom-call(s32[4]{0:T(128)S(1)} %compare_select_fusion.order, ...), custom_call_target="tpu_custom_call" | custom-call | flops 4831838208 | bytes 7868416 | tf_op jit(solution)/shard_map/pallas_call | solution.py:310
  105.5 33.6 %shard_map.258 = (bf16[8,3,32,512]{3,2,1,0:T(8,128)(2,1)S(1)}, bf16[8,3,32,512]{3,2,1,0:T(8,128)(2,1)S(1)}, bf16[4,256,512]{2,1,0:T(8,128)(2,1)S(1)}, bf16[4,256...) custom-call(s32[4]{0:T(128)S(1)} %compare_select_fusion.order, ...), custom_call_target="tpu_custom_call", output_to_operand_aliasing={{2}: (10, {}), {3}: (11, {}), {4}: (12, {}), {5}: (13, {}),... | custom-call | flops 14495514624 | bytes 24645632 | tf_op jit(solution)/shard_map/pallas_call | solution.py:310
  145.8 5.3 %all-to-all-start.3 = ((bf16[8,3,32,512]{3,2,1,0:T(8,128)(2,1)}), bf16[8,3,32,512]{3,2,1,0:T(8,128)(2,1)}, u32[]{:S(2)}, u32[]{:S(2)}) async-start(bf16[8,3,32,512]{3,2,1,0:T(8,128)(2,1)} %copy-done.58), calls=%async_computation.3 | async-start | bytes 1572864 | tf_op jit(solution)/shard_map/all_to_all | solution.py:575
  154.4 5.0 %shard_map.260 = (bf16[4,256,2048]{2,1,0:T(8,128)(2,1)}, bf16[4,256,512]{2,1,0:T(8,128)(2,1)S(1)}, bf16[4,256,512]{2,1,0:T(8,128)(2,1)S(1)}, bf16[4,256,512]{2,1,0:T(8,128)(2,1)S(1)}, f32[4,256,512]{2,1,0:T(8,128)S(1)}) custom-call(s32[4]{0:T(128)S(1)} %compare_select_fusion.order, f32[1,256,512]{2,1,0:T(8,128)S(1)} %copy-done.61, ...), custom_call_target="tpu_custom_call" | custom-call | flops 1610612736 | bytes 10491904 | tf_op jit(solution)/shard_map/pallas_call | solution.py:310
  163.7 11.5 %shard_map.270 = (bf16[4,4,128,512]{3,2,1,0:T(8,128)(2,1)S(1)}, bf16[4,4,128,512]{3,2,1,0:T(8,128)(2,1)}) custom-call(s32[3]{0:T(128)S(1)} %pad_add_fusion.ids, bf16[1024,512]{1,0:T(8,128)(2,1)S(1)} %bitcast.196, bf16[1024,512]{1,0:T(8,128)(2,1)S(1)} %bitcast.197, bf16[1024,2048]{1,0:T(8,128)(2,1)} %bitcast.204, bf16[1024,2048]{1,0:T(8,128)(2,1)} %bitcast.205), custom_call_target="tpu_custom_call" | custom-call | flops 4294967296 | bytes 10485760 | tf_op jit(solution)/shard_map/pallas_call | solution.py:407
  177.1 5.4 %shard_map.268 = (bf16[4,4,64,512]{3,2,1,0:T(8,128)(2,1)S(1)}, bf16[4,4,64,512]{3,2,1,0:T(8,128)(2,1)}) custom-call(s32[3]{0:T(128)S(1)} %pad_add_fusion.ids, bf16[1024,512]{1,0:T(8,128)(2,1)S(1)} %bitcast.193, bf16[1024,512]{1,0:T(8,128)(2,1)S(1)} %bitcast.194, bf16[1024,1536]{1,0:T(8,128)(2,1)S(1)} %bitcast.192, bf16[1024,512]{1,0:T(8,128)(2,1)S(1)} %bitcast.195), custom_call_target="tpu_custom_call" | custom-call | flops 2147483648 | bytes 6291456 | tf_op jit(solution)/shard_map/pallas_call | solution.py:407
  190.9 9.2 %shard_map.261 = (bf16[4,256,2048]{2,1,0:T(8,128)(2,1)}, bf16[4,256,512]{2,1,0:T(8,128)(2,1)S(1)}, bf16[4,256,512]{2,1,0:T(8,128)(2,1)S(1)}, bf16[4,256,512]{2,1,0:T(8,128)(2,1)S(1)}, f32[4,256,512]{2,1,0:T(8,128)S(1)}) custom-call(s32[4]{0:T(128)S(1)} %compare_select_fusion.order, ...), custom_call_target="tpu_custom_call", output_to_operand_aliasing={{0}: (9, {}), {1}: (10, {}), {2}: (11, {}), {3}: (12, {}), ... | custom-call | flops 4831838208 | bytes 20191232 | tf_op jit(solution)/shard_map/pallas_call | solution.py:310
  202.1 12.3 %shard_map.266 = (bf16[4,4,128,512]{3,2,1,0:T(8,128)(2,1)S(1)}, bf16[4,4,128,512]{3,2,1,0:T(8,128)(2,1)}) custom-call(s32[3]{0:T(128)S(1)} %pad_add_fusion.ids, bf16[1024,512]{1,0:T(8,128)(2,1)S(1)} %bitcast.175, bf16[1024,512]{1,0:T(8,128)(2,1)S(1)} %bitcast.178, bf16[1024,2048]{1,0:T(8,128)(2,1)} %bitcast.199, bf16[1024,2048]{1,0:T(8,128)(2,1)} %bitcast.198), custom_call_target="tpu_custom_call" | custom-call | flops 4294967296 | bytes 10485760 | tf_op jit(solution)/shard_map/pallas_call | solution.py:407
  215.0 13.4 %shard_map.262.gqkv = bf16[4,256,1536]{2,1,0:T(8,128)(2,1)S(1)} custom-call(s32[4]{0:T(128)S(1)} %compare_select_fusion.order, bf16[4,256,1536]{2,1,0:T(8,128)(2,1)S(1)} %copy-done.22, bf16[4,8,256,256]{3,2,1,0:T(8,128)(2,1)} %get-tuple-element.108.p, bf16[4,256,512]{2,1,0:T(8,128)(2,1)S(1)} %copy-done.50), custom_call_target="tpu_custom_call" | custom-call | flops 6442450944 | bytes 8388608 | tf_op jit(solution)/shard_map/pallas_call | solution.py:310
  228.4 5.7 %shard_map.264 = (bf16[4,4,64,512]{3,2,1,0:T(8,128)(2,1)S(1)}, bf16[4,4,64,512]{3,2,1,0:T(8,128)(2,1)}) custom-call(s32[3]{0:T(128)S(1)} %pad_add_fusion.ids, bf16[1024,512]{1,0:T(8,128)(2,1)S(1)} %bitcast.176, bf16[1024,512]{1,0:T(8,128)(2,1)S(1)} %bitcast.180, bf16[1024,1536]{1,0:T(8,128)(2,1)S(1)} %bitcast.177, bf16[1024,512]{1,0:T(8,128)(2,1)S(1)} %bitcast.179), custom_call_target="tpu_custom_call" | custom-call | flops 2147483648 | bytes 6291456 | tf_op jit(solution)/shard_map/pallas_call | solution.py:407
  235.7 4.7 %all-to-all-start.2 = ((bf16[8,3,32,512]{3,2,1,0:T(8,128)(2,1)}), bf16[8,3,32,512]{3,2,1,0:T(8,128)(2,1)}, u32[]{:S(2)}, u32[]{:S(2)}) async-start(bf16[8,3,32,512]{3,2,1,0:T(8,128)(2,1)} %copy-done.57), calls=%async_computation.2 | async-start | bytes 1572864 | tf_op jit(solution)/shard_map/all_to_all | solution.py:575
  246.0 3.3 add_convert_fusion.3
  249.2 2.3 collective-permute-done.21
  253.1 4.8 %collective-permute-done.22 = bf16[4,64,512]{2,1,0:T(8,128)(2,1)S(1)} collective-permute-done((bf16[4,64,512]{2,1,0:T(8,128)(2,1)S(1)}, bf16[4,64,512]{2,1,0:T(8,128)(2,1)S(1)}, u32[]{:S(2)}, u32[]{:S(2)}) %collective-permute-start.22) | collective-permute-done | bytes 262176 | tf_op jit(solution)/shard_map/ppermute | solution.py:429
  264.1 2.7 add_convert_fusion.15
  268.6 3.0 collective-permute-start.25
  271.5 11.2 %collective-permute-done.32 = bf16[4,128,512]{2,1,0:T(8,128)(2,1)} collective-permute-done((bf16[4,128,512]{2,1,0:T(8,128)(2,1)}, bf16[4,128,512]{2,1,0:T(8,128)(2,1)}, u32[]{:S(2)}, u32[]{:S(2)}) %collective-permute-start.32) | collective-permute-done | bytes 524320 | tf_op jit(solution)/shard_map/ppermute | solution.py:429
  282.7 2.3 collective-permute-start.26
  290.7 3.3 add_convert_fusion.7
  298.1 4.8 %collective-permute-start.13 = (bf16[4,128,512]{2,1,0:T(8,128)(2,1)}, bf16[4,128,512]{2,1,0:T(8,128)(2,1)}, u32[]{:S(2)}, u32[]{:S(2)}) collective-permute-start(bf16[4,128,512]{2,1,0:T(8,128)(2,1)} %get-tuple-element.161), channel_id=1, source_target_pairs={{0,24},{8,16},{16,8},{24,0},{1,25},{9,17},{17,9},{25,1},{2,26},{10... | collective-permute-start | bytes 1572872 | tf_op jit(solution)/shard_map/ppermute | solution.py:429
  304.0 3.9 %shard_map.259 = f32[4,1,256,512]{3,2,1,0:T(8,128)} custom-call(s32[4]{0:T(128)S(1)} %compare_select_fusion.order, bf16[8,3,32,512]{3,2,1,0:T(8,128)(2,1)} %all-to-all-done.2.block, f32[4,1,256,512]{3,2,1,0:T(8,128)} %get-tuple-element.106.before), custom_call_target="tpu_custom_call", output_to_operand_aliasing={{}: (2, {})} | custom-call | bytes 2883584 | tf_op jit(solution)/shard_map/pallas_call | solution.py:310
  308.0 2.8 collective-permute-start.36
  311.8 4.7 %collective-permute-done.35 = bf16[128,512]{1,0:T(8,128)(2,1)S(1)} collective-permute-done((bf16[128,512]{1,0:T(8,128)(2,1)S(1)}, bf16[128,512]{1,0:T(8,128)(2,1)S(1)}, u32[]{:S(2)}, u32[]{:S(2)}) %collective-permute-start.35) | collective-permute-done | bytes 131104 | tf_op jit(solution)/shard_map/ppermute | solution.py:429
  326.3 4.1 %collective-permute-done.5 = bf16[64,512]{1,0:T(8,128)(2,1)S(1)} collective-permute-done((bf16[64,512]{1,0:T(8,128)(2,1)S(1)}, bf16[64,512]{1,0:T(8,128)(2,1)S(1)}, u32[]{:S(2)}, u32[]{:S(2)}) %collective-permute-start.5) | collective-permute-done | bytes 65568 | tf_op jit(solution)/shard_map/ppermute | solution.py:429
  330.5 3.3 collective-permute-start.16
  335.0 2.8 collective-permute-start.37
  349.6 4.4 %shard_map.263 = f32[4,1,256,512]{3,2,1,0:T(8,128)} custom-call(s32[4]{0:T(128)S(1)} %compare_select_fusion.order, bf16[4,256,1536]{2,1,0:T(8,128)(2,1)S(1)} %copy-done.25, bf16[512,1536]{1,0:T(8,128)(2,1)S(1)} %copy-done.4, f32[1,512]{1,0:T(1,128)S(1)} %bitcast.187, bf16[4,256,512]{2,1,0:T(8,128)(2,1)S(1)} %copy-done.21, f32[4,256,1]{2,1,0:T(8,128)S(1)} %copy-done.33, ...), custom_call_target="tpu_custom_call" | custom-call | flops 1610612736 | bytes 7870464 | tf_op jit(solution)/shard_map/pallas_call | solution.py:310
  (302 shorter events, 125.5 us)
Async XLA Ops:
  31.7 27.4 %all-to-all-start = ((bf16[8,3,32,512]{3,2,1,0:T(8,128)(2,1)}), bf16[8,3,32,512]{3,2,1,0:T(8,128)(2,1)}, u32[]{:S(2)}, u32[]{:S(2)}) async-start(bf16[8,3,32,512]{3,2,1,0:T(8,128)(2,1)} %copy-done.59), calls=%async_computation | async-start | bytes 1572864 | tf_op jit(solution)/shard_map/all_to_all | solution.py:575
  59.1 39.2 %all-to-all-start.1 = ((bf16[8,3,32,512]{3,2,1,0:T(8,128)(2,1)}), bf16[8,3,32,512]{3,2,1,0:T(8,128)(2,1)}, u32[]{:S(2)}, u32[]{:S(2)}) async-start(bf16[8,3,32,512]{3,2,1,0:T(8,128)(2,1)} %copy-done.23), calls=%async_computation.1 | async-start | bytes 1572864 | tf_op jit(solution)/shard_map/all_to_all | solution.py:575
  145.8 37.8 %all-to-all-start.3 = ((bf16[8,3,32,512]{3,2,1,0:T(8,128)(2,1)}), bf16[8,3,32,512]{3,2,1,0:T(8,128)(2,1)}, u32[]{:S(2)}, u32[]{:S(2)}) async-start(bf16[8,3,32,512]{3,2,1,0:T(8,128)(2,1)} %copy-done.58), calls=%async_computation.3 | async-start | bytes 1572864 | tf_op jit(solution)/shard_map/all_to_all | solution.py:575
  176.6 68.9 %collective-permute-start.30 = (bf16[4,4,128,512]{3,2,1,0:T(8,128)(2,1)}, bf16[4,4,128,512]{3,2,1,0:T(8,128)(2,1)}, u32[]{:S(2)}, u32[]{:S(2)}) collective-permute-start(bf16[4,4,128,512]{3,2,1,0:T(8,128)(2,1)} %get-tuple-element.152), channel_id=1, source_target_pairs={{0,1},{1,0},{2,3},{3,2},{4,5},{5,4},{6,7},{7,6},{8,9},{9,8},{10,11... | collective-permute-start | bytes 6291464 | tf_op jit(solution)/shard_map/ppermute | solution.py:429
  183.5 56.9 %collective-permute-start.20 = (bf16[4,4,64,512]{3,2,1,0:T(8,128)(2,1)}, bf16[4,4,64,512]{3,2,1,0:T(8,128)(2,1)}, u32[]{:S(2)}, u32[]{:S(2)}) collective-permute-start(bf16[4,4,64,512]{3,2,1,0:T(8,128)(2,1)} %get-tuple-element.143), channel_id=1, source_target_pairs={{0,1},{1,0},{2,3},{3,2},{4,5},{5,4},{6,7},{7,6},{8,9},{9,8},{10,11... | collective-permute-start | bytes 3145736 | tf_op jit(solution)/shard_map/ppermute | solution.py:429
  214.5 74.5 %collective-permute-start.10 = (bf16[4,4,128,512]{3,2,1,0:T(8,128)(2,1)}, bf16[4,4,128,512]{3,2,1,0:T(8,128)(2,1)}, u32[]{:S(2)}, u32[]{:S(2)}) collective-permute-start(bf16[4,4,128,512]{3,2,1,0:T(8,128)(2,1)} %get-tuple-element.134), channel_id=1, source_target_pairs={{0,1},{1,0},{2,3},{3,2},{4,5},{5,4},{6,7},{7,6},{8,9},{9,8},{10,11... | collective-permute-start | bytes 6291464 | tf_op jit(solution)/shard_map/ppermute | solution.py:429
  235.1 26.9 %collective-permute-start = (bf16[4,4,64,512]{3,2,1,0:T(8,128)(2,1)}, bf16[4,4,64,512]{3,2,1,0:T(8,128)(2,1)}, u32[]{:S(2)}, u32[]{:S(2)}) collective-permute-start(bf16[4,4,64,512]{3,2,1,0:T(8,128)(2,1)} %get-tuple-element.126), channel_id=1, source_target_pairs={{0,1},{1,0},{2,3},{3,2},{4,5},{5,4},{6,7},{7,6},{8,9},{9,8},{10,11... | collective-permute-start | bytes 3145736 | tf_op jit(solution)/shard_map/ppermute | solution.py:429
  235.7 68.2 %all-to-all-start.2 = ((bf16[8,3,32,512]{3,2,1,0:T(8,128)(2,1)}), bf16[8,3,32,512]{3,2,1,0:T(8,128)(2,1)}, u32[]{:S(2)}, u32[]{:S(2)}) async-start(bf16[8,3,32,512]{3,2,1,0:T(8,128)(2,1)} %copy-done.57), calls=%async_computation.2 | async-start | bytes 1572864 | tf_op jit(solution)/shard_map/all_to_all | solution.py:575
  244.0 13.9 %collective-permute-start.22 = (bf16[4,64,512]{2,1,0:T(8,128)(2,1)S(1)}, bf16[4,64,512]{2,1,0:T(8,128)(2,1)S(1)}, u32[]{:S(2)}, u32[]{:S(2)}) collective-permute-start(bf16[4,64,512]{2,1,0:T(8,128)(2,1)S(1)} %get-tuple-element.169), channel_id=1, source_target_pairs={{0,16},{8,24},{16,0},{24,8},{1,17},{9,25},{17,1},{25,9},{2,18},{10... | collective-permute-start | bytes 786440 | tf_op jit(solution)/shard_map/ppermute | solution.py:429
  245.5 14.1 %collective-permute-start.23 = (bf16[4,64,512]{2,1,0:T(8,128)(2,1)S(1)}, bf16[4,64,512]{2,1,0:T(8,128)(2,1)S(1)}, u32[]{:S(2)}, u32[]{:S(2)}) collective-permute-start(bf16[4,64,512]{2,1,0:T(8,128)(2,1)S(1)} %get-tuple-element.168), channel_id=1, source_target_pairs={{0,24},{8,16},{16,8},{24,0},{1,25},{9,17},{17,9},{25,1},{2,26},{10... | collective-permute-start | bytes 786440 | tf_op jit(solution)/shard_map/ppermute | solution.py:429
  251.6 17.0 %collective-permute-start.31 = (bf16[4,128,512]{2,1,0:T(8,128)(2,1)}, bf16[4,128,512]{2,1,0:T(8,128)(2,1)}, u32[]{:S(2)}, u32[]{:S(2)}) collective-permute-start(bf16[4,128,512]{2,1,0:T(8,128)(2,1)} %get-tuple-element.159), channel_id=1, source_target_pairs={{0,8},{8,0},{16,24},{24,16},{1,9},{9,1},{17,25},{25,17},{2,10},{10... | collective-permute-start | bytes 1572872 | tf_op jit(solution)/shard_map/ppermute | solution.py:429
  257.8 24.9 %collective-permute-start.32 = (bf16[4,128,512]{2,1,0:T(8,128)(2,1)}, bf16[4,128,512]{2,1,0:T(8,128)(2,1)}, u32[]{:S(2)}, u32[]{:S(2)}) collective-permute-start(bf16[4,128,512]{2,1,0:T(8,128)(2,1)} %get-tuple-element.158), channel_id=1, source_target_pairs={{0,16},{8,24},{16,0},{24,8},{1,17},{9,25},{17,1},{25,9},{2,18},{10... | collective-permute-start | bytes 1572872 | tf_op jit(solution)/shard_map/ppermute | solution.py:429
  260.3 24.7 %collective-permute-start.33 = (bf16[4,128,512]{2,1,0:T(8,128)(2,1)}, bf16[4,128,512]{2,1,0:T(8,128)(2,1)}, u32[]{:S(2)}, u32[]{:S(2)}) collective-permute-start(bf16[4,128,512]{2,1,0:T(8,128)(2,1)} %get-tuple-element.157), channel_id=1, source_target_pairs={{0,24},{8,16},{16,8},{24,0},{1,25},{9,17},{17,9},{25,1},{2,26},{10... | collective-permute-start | bytes 1572872 | tf_op jit(solution)/shard_map/ppermute | solution.py:429
  262.0 25.2 %collective-permute-start.24 = (bf16[64,512]{1,0:T(8,128)(2,1)S(1)}, bf16[64,512]{1,0:T(8,128)(2,1)S(1)}, u32[]{:S(2)}, u32[]{:S(2)}) collective-permute-start(bf16[64,512]{1,0:T(8,128)(2,1)S(1)} %get-tuple-element.178), channel_id=1, source_target_pairs={{0,2},{1,3},{2,0},{3,1},{4,6},{5,7},{6,4},{7,5},{8,10},{9,11},{10,... | collective-permute-start | bytes 196616 | tf_op jit(solution)/shard_map/ppermute | solution.py:429
  268.6 25.4 %collective-permute-start.25 = (bf16[64,512]{1,0:T(8,128)(2,1)S(1)}, bf16[64,512]{1,0:T(8,128)(2,1)S(1)}, u32[]{:S(2)}, u32[]{:S(2)}) collective-permute-start(bf16[64,512]{1,0:T(8,128)(2,1)S(1)} %get-tuple-element.180), channel_id=1, source_target_pairs={{0,4},{1,5},{2,6},{3,7},{4,0},{5,1},{6,2},{7,3},{8,12},{9,13},{10,... | collective-permute-start | bytes 196616 | tf_op jit(solution)/shard_map/ppermute | solution.py:429
  282.7 11.3 %collective-permute-start.26 = (bf16[64,512]{1,0:T(8,128)(2,1)S(1)}, bf16[64,512]{1,0:T(8,128)(2,1)S(1)}, u32[]{:S(2)}, u32[]{:S(2)}) collective-permute-start(bf16[64,512]{1,0:T(8,128)(2,1)S(1)} %get-tuple-element.179), channel_id=1, source_target_pairs={{0,6},{1,7},{2,4},{3,5},{4,2},{5,3},{6,0},{7,1},{8,14},{9,15},{10,... | collective-permute-start | bytes 196616 | tf_op jit(solution)/shard_map/ppermute | solution.py:429
  287.2 10.8 %collective-permute-start.2 = (bf16[4,64,512]{2,1,0:T(8,128)(2,1)S(1)}, bf16[4,64,512]{2,1,0:T(8,128)(2,1)S(1)}, u32[]{:S(2)}, u32[]{:S(2)}) collective-permute-start(bf16[4,64,512]{2,1,0:T(8,128)(2,1)S(1)} %get-tuple-element.176), channel_id=1, source_target_pairs={{0,16},{8,24},{16,0},{24,8},{1,17},{9,25},{17,1},{25,9},{2,18},{10... | collective-permute-start | bytes 786440 | tf_op jit(solution)/shard_map/ppermute | solution.py:429
  289.0 18.9 %collective-permute-start.3 = (bf16[4,64,512]{2,1,0:T(8,128)(2,1)}, bf16[4,64,512]{2,1,0:T(8,128)(2,1)}, u32[]{:S(2)}, u32[]{:S(2)}) collective-permute-start(bf16[4,64,512]{2,1,0:T(8,128)(2,1)} %get-tuple-element.175), channel_id=1, source_target_pairs={{0,24},{8,16},{16,8},{24,0},{1,25},{9,17},{17,9},{25,1},{2,26},{10... | collective-permute-start | bytes 786440 | tf_op jit(solution)/shard_map/ppermute | solution.py:429
  294.0 14.0 %collective-permute-start.34 = (bf16[128,512]{1,0:T(8,128)(2,1)}, bf16[128,512]{1,0:T(8,128)(2,1)}, u32[]{:S(2)}, u32[]{:S(2)}) collective-permute-start(bf16[128,512]{1,0:T(8,128)(2,1)} %get-tuple-element.164), channel_id=1, source_target_pairs={{0,2},{1,3},{2,0},{3,1},{4,6},{5,7},{6,4},{7,5},{8,10},{9,11},{10,... | collective-permute-start | bytes 393224 | tf_op jit(solution)/shard_map/ppermute | solution.py:429
  294.0 25.0 %collective-permute-start.11 = (bf16[4,128,512]{2,1,0:T(8,128)(2,1)}, bf16[4,128,512]{2,1,0:T(8,128)(2,1)}, u32[]{:S(2)}, u32[]{:S(2)}) collective-permute-start(bf16[4,128,512]{2,1,0:T(8,128)(2,1)} %get-tuple-element.163), channel_id=1, source_target_pairs={{0,8},{8,0},{16,24},{24,16},{1,9},{9,1},{17,25},{25,17},{2,10},{10... | collective-permute-start | bytes 1572872 | tf_op jit(solution)/shard_map/ppermute | solution.py:429
  294.4 26.2 %collective-permute-start.12 = (bf16[4,128,512]{2,1,0:T(8,128)(2,1)}, bf16[4,128,512]{2,1,0:T(8,128)(2,1)}, u32[]{:S(2)}, u32[]{:S(2)}) collective-permute-start(bf16[4,128,512]{2,1,0:T(8,128)(2,1)} %get-tuple-element.162), channel_id=1, source_target_pairs={{0,16},{8,24},{16,0},{24,8},{1,17},{9,25},{17,1},{25,9},{2,18},{10... | collective-permute-start | bytes 1572872 | tf_op jit(solution)/shard_map/ppermute | solution.py:429
  298.1 24.7 %collective-permute-start.13 = (bf16[4,128,512]{2,1,0:T(8,128)(2,1)}, bf16[4,128,512]{2,1,0:T(8,128)(2,1)}, u32[]{:S(2)}, u32[]{:S(2)}) collective-permute-start(bf16[4,128,512]{2,1,0:T(8,128)(2,1)} %get-tuple-element.161), channel_id=1, source_target_pairs={{0,24},{8,16},{16,8},{24,0},{1,25},{9,17},{17,9},{25,1},{2,26},{10... | collective-permute-start | bytes 1572872 | tf_op jit(solution)/shard_map/ppermute | solution.py:429
  316.5 18.2 %collective-permute-start.27 = (bf16[64,512]{1,0:T(8,128)(2,1)S(1)}, bf16[64,512]{1,0:T(8,128)(2,1)S(1)}, u32[]{:S(2)}, u32[]{:S(2)}) collective-permute-start(bf16[64,512]{1,0:T(8,128)(2,1)S(1)} %fusion.61.p0), channel_id=1, source_target_pairs={{0,8},{8,0},{16,24},{24,16},{1,9},{9,1},{17,25},{25,17},{2,10},{10... | collective-permute-start | bytes 196616 | tf_op jit(solution)/shard_map/ppermute | solution.py:429
  316.5 18.5 %collective-permute-start.28 = (bf16[64,512]{1,0:T(8,128)(2,1)S(1)}, bf16[64,512]{1,0:T(8,128)(2,1)S(1)}, u32[]{:S(2)}, u32[]{:S(2)}) collective-permute-start(bf16[64,512]{1,0:T(8,128)(2,1)S(1)} %fusion.61.p0), channel_id=1, source_target_pairs={{0,16},{8,24},{16,0},{24,8},{1,17},{9,25},{17,1},{25,9},{2,18},{10... | collective-permute-start | bytes 196616 | tf_op jit(solution)/shard_map/ppermute | solution.py:429
  320.6 9.9 %collective-permute-start.5 = (bf16[64,512]{1,0:T(8,128)(2,1)S(1)}, bf16[64,512]{1,0:T(8,128)(2,1)S(1)}, u32[]{:S(2)}, u32[]{:S(2)}) collective-permute-start(bf16[64,512]{1,0:T(8,128)(2,1)S(1)} %get-tuple-element.183), channel_id=1, source_target_pairs={{0,4},{1,5},{2,6},{3,7},{4,0},{5,1},{6,2},{7,3},{8,12},{9,13},{10,... | collective-permute-start | bytes 196616 | tf_op jit(solution)/shard_map/ppermute | solution.py:429
  325.8 12.0 %collective-permute-start.14 = (bf16[128,512]{1,0:T(8,128)(2,1)S(1)}, bf16[128,512]{1,0:T(8,128)(2,1)S(1)}, u32[]{:S(2)}, u32[]{:S(2)}) collective-permute-start(bf16[128,512]{1,0:T(8,128)(2,1)S(1)} %get-tuple-element.171), channel_id=1, source_target_pairs={{0,2},{1,3},{2,0},{3,1},{4,6},{5,7},{6,4},{7,5},{8,10},{9,11},{10,... | collective-permute-start | bytes 393224 | tf_op jit(solution)/shard_map/ppermute | solution.py:429
  335.0 12.4 %collective-permute-start.37 = (bf16[128,512]{1,0:T(8,128)(2,1)S(1)}, bf16[128,512]{1,0:T(8,128)(2,1)S(1)}, u32[]{:S(2)}, u32[]{:S(2)}) collective-permute-start(bf16[128,512]{1,0:T(8,128)(2,1)S(1)} %fusion.23.p0), channel_id=1, source_target_pairs={{0,8},{8,0},{16,24},{24,16},{1,9},{9,1},{17,25},{25,17},{2,10},{10... | collective-permute-start | bytes 393224 | tf_op jit(solution)/shard_map/ppermute | solution.py:429
  342.8 14.2 %collective-permute-start.38 = (bf16[128,512]{1,0:T(8,128)(2,1)S(1)}, bf16[128,512]{1,0:T(8,128)(2,1)S(1)}, u32[]{:S(2)}, u32[]{:S(2)}) collective-permute-start(bf16[128,512]{1,0:T(8,128)(2,1)S(1)} %fusion.23.p0), channel_id=1, source_target_pairs={{0,16},{8,24},{16,0},{24,8},{1,17},{9,25},{17,1},{25,9},{2,18},{10... | collective-permute-start | bytes 393224 | tf_op jit(solution)/shard_map/ppermute | solution.py:429
  343.9 13.1 %collective-permute-start.39 = (bf16[128,512]{1,0:T(8,128)(2,1)S(1)}, bf16[128,512]{1,0:T(8,128)(2,1)S(1)}, u32[]{:S(2)}, u32[]{:S(2)}) collective-permute-start(bf16[128,512]{1,0:T(8,128)(2,1)S(1)} %fusion.23.p0), channel_id=1, source_target_pairs={{0,24},{8,16},{16,8},{24,0},{1,25},{9,17},{17,9},{25,1},{2,26},{10... | collective-permute-start | bytes 393224 | tf_op jit(solution)/shard_map/ppermute | solution.py:429
  346.0 12.7 %collective-permute-start.17 = (bf16[128,512]{1,0:T(8,128)(2,1)S(1)}, bf16[128,512]{1,0:T(8,128)(2,1)S(1)}, u32[]{:S(2)}, u32[]{:S(2)}) collective-permute-start(bf16[128,512]{1,0:T(8,128)(2,1)S(1)} %fusion.38.p0), channel_id=1, source_target_pairs={{0,8},{8,0},{16,24},{24,16},{1,9},{9,1},{17,25},{25,17},{2,10},{10... | collective-permute-start | bytes 393224 | tf_op jit(solution)/shard_map/ppermute | solution.py:429
  346.3 12.4 %collective-permute-start.18 = (bf16[128,512]{1,0:T(8,128)(2,1)S(1)}, bf16[128,512]{1,0:T(8,128)(2,1)S(1)}, u32[]{:S(2)}, u32[]{:S(2)}) collective-permute-start(bf16[128,512]{1,0:T(8,128)(2,1)S(1)} %fusion.38.p0), channel_id=1, source_target_pairs={{0,16},{8,24},{16,0},{24,8},{1,17},{9,25},{17,1},{25,9},{2,18},{10... | collective-permute-start | bytes 393224 | tf_op jit(solution)/shard_map/ppermute | solution.py:429
  347.4 11.4 %collective-permute-start.19 = (bf16[128,512]{1,0:T(8,128)(2,1)S(1)}, bf16[128,512]{1,0:T(8,128)(2,1)S(1)}, u32[]{:S(2)}, u32[]{:S(2)}) collective-permute-start(bf16[128,512]{1,0:T(8,128)(2,1)S(1)} %fusion.38.p0), channel_id=1, source_target_pairs={{0,24},{8,16},{16,8},{24,0},{1,25},{9,17},{17,9},{25,1},{2,26},{10... | collective-permute-start | bytes 393224 | tf_op jit(solution)/shard_map/ppermute | solution.py:429
  (116 other events, 775.7 us)

commit v2 on v1

v2 whole, which is shorter than its diff:
```python
import functools

import jax
import jax.numpy as jnp
from jax import lax
from jax.experimental import pallas as pl
from jax.experimental.pallas import tpu as pltpu
from jax.sharding import PartitionSpec as P

HEADS = 8
EPS = 1e-05
GELU_A = 0.7978845608028654
GELU_B = 0.044715
BF = jnp.bfloat16
F32 = jnp.float32
CHUNK = 512
LANES = 128
VMEM = 60 * 1024 * 1024


def nn(a, b):
    return jnp.dot(a, b, preferred_element_type=F32)


def nt(a, b):
    return lax.dot_general(a, b, (((1,), (1,)), ((), ())), preferred_element_type=F32)


def tn(a, b):
    return lax.dot_general(a, b, (((0,), (0,)), ((), ())), preferred_element_type=F32)


def unit(values):
    average = jnp.mean(values, axis=-1, keepdims=True)
    centered = values - average
    inverse = lax.rsqrt(jnp.mean(centered * centered, axis=-1, keepdims=True) + EPS)
    return centered * inverse, inverse


def unit_backward(grad, unit_rows, inverse):
    first = jnp.mean(grad, axis=-1, keepdims=True)
    second = jnp.mean(grad * unit_rows, axis=-1, keepdims=True)
    return inverse * (grad - first - unit_rows * second)


def gelu_parts(u):
    square = u * u
    tangent = jnp.tanh(u * (BF(GELU_A) + BF(GELU_A * GELU_B) * square))
    half = BF(0.5) * u
    value = half + half * tangent
    slope = (BF(0.5) + BF(0.5) * tangent) + half * (BF(1.0) - tangent * tangent) * (
        BF(GELU_A) + BF(3.0 * GELU_A * GELU_B) * square
    )
    return value, slope


def head_masks(width):
    lane = lax.broadcasted_iota(jnp.int32, (1, 2 * width), 1)
    low = lane < width
    return low, (low.astype(F32).astype(BF), (1.0 - low.astype(F32)).astype(BF))


def attend(qkv_ref, p_ref, o_ref, bias_ref, s_ref):
    width = qkv_ref.shape[1] // 3
    size = width // HEADS
    _, masks = head_masks(size)

    def lanes(part, head):
        at = part * width + (head // 2) * 2 * size
        return qkv_ref[:, at : at + 2 * size]

    def score(head):
        s_ref[head % 4] = nt(lanes(1, head) * masks[head % 2], lanes(0, head) * BF(size**-0.5))

    def soften(head):
        scores = s_ref[head % 4]
        if bias_ref is not None:
            scores = scores + bias_ref[...]
        e = jnp.exp(scores - jnp.max(scores, axis=0, keepdims=True))
        p_ref[head] = (e * (1.0 / jnp.sum(e, axis=0, keepdims=True))).astype(BF)

    for head in range(0, HEADS, 2):
        if head == 0:
            score(0)
            score(1)
        if head + 2 < HEADS:
            score(head + 2)
            score(head + 3)
        soften(head)
        soften(head + 1)
    for head in range(0, HEADS, 2):
        v = lanes(2, head).T
        both = jnp.concatenate([nn(v[:size], p_ref[head]), nn(v[size:], p_ref[head + 1])], axis=0)
        o_ref[:, head * size : (head + 2) * size] = both.T.astype(BF)


def attend_backward(qkv_ref, p_ref, go_ref, out_ref, gp_ref, gs_ref):
    width = qkv_ref.shape[1] // 3
    size = width // HEADS
    _, masks = head_masks(size)

    def lanes(part, head):
        at = part * width + (head // 2) * 2 * size
        return qkv_ref[:, at : at + 2 * size]

    def gos(head):
        return go_ref[:, (head // 2) * 2 * size : (head // 2 + 1) * 2 * size]

    def put(part, head, value):
        at = part * width + head * size
        out_ref[:, at : at + 2 * size] = value.astype(BF)

    def start(head):
        for h in (head, head + 1):
            gp_ref[h % 4] = nt(lanes(2, h) * masks[h % 2], gos(h)).astype(BF)
        g = gos(head)
        put(2, head, nn(p_ref[head], g * masks[0]) + nn(p_ref[head + 1], g * masks[1]))

    def middle(head):
        p = p_ref[head]
        weighted = p * gp_ref[head % 4]
        total = jnp.sum(weighted.astype(F32), axis=0, keepdims=True).astype(BF)
        gs_ref[head] = weighted - p * total

    def finish(head):
        q = lanes(0, head) * BF(size**-0.5)
        k = (lanes(1, head) * BF(size**-0.5)).T
        put(1, head, nn(gs_ref[head], q * masks[0]) + nn(gs_ref[head + 1], q * masks[1]))
        both = jnp.concatenate([nn(k[:size], gs_ref[head]), nn(k[size:], gs_ref[head + 1])], axis=0)
        put(0, head, both.T)

    start(0)
    for head in range(0, HEADS, 2):
        middle(head)
        middle(head + 1)
        if head + 2 < HEADS:
            start(head + 2)
        if head > 0:
            finish(head - 2)
    finish(HEADS - 2)


def feed_up(m, up_ref, down_ref, h_ref, slope_ref, u_ref):
    steps = up_ref.shape[1] // CHUNK

    def before(step):
        u_ref[step % 2] = nn(m, up_ref[:, step * CHUNK : (step + 1) * CHUNK]).astype(BF)

    before(0)
    for step in range(steps):
        if step + 1 < steps:
            before(step + 1)
        at = step * CHUNK
        h_ref[:, at : at + CHUNK], slope_ref[:, at : at + CHUNK] = gelu_parts(u_ref[step % 2])
    return nn(h_ref[...], down_ref[...])


def feed_back(e2, up_ref, down_ref, slope_ref, eu_ref):
    for at in range(0, up_ref.shape[1], CHUNK):
        gh = nt(e2, down_ref[at : at + CHUNK, :]).astype(BF)
        eu_ref[:, at : at + CHUNK] = gh * slope_ref[:, at : at + CHUNK]
    return nt(eu_ref[...], up_ref[...])


def rows_of(block):
    slots, _, patches, width = block.shape
    return block[:, 0].astype(F32).reshape(slots * patches, width)


def block_of(rows, ref):
    slots, _, patches, width = ref.shape
    ref[:, 0] = rows.reshape(slots, patches, width).astype(ref.dtype)


def work_shapes(tokens):
    return [
        pltpu.VMEM((4, tokens, tokens), F32),
        pltpu.VMEM((2, tokens, CHUNK), BF),
        pltpu.VMEM((4, tokens, tokens), BF),
        pltpu.VMEM((HEADS, tokens, tokens), BF),
    ]


def wide(column):
    return jnp.broadcast_to(column, (column.shape[0], LANES))


def space_rows(x, weights, state, work):
    gain, w_in, w_out, scale, w_up, w_down = weights
    z0, inv0, qkv, p, o, z1, inv1, h, slope = state
    unit0, inverse0 = unit(x)
    z0[...] = unit0.astype(BF)
    inv0[...] = wide(inverse0)
    qkv[...] = nn((unit0 * gain[...]).astype(BF), w_in[...]).astype(BF)
    attend(qkv, p, o, None, work[0])
    r1 = x + nn(o[...], w_out[...])
    unit1, inverse1 = unit(r1)
    z1[...] = unit1.astype(BF)
    inv1[...] = wide(inverse1)
    m = (unit1 * scale[...]).astype(BF)
    return r1 + feed_up(m, w_up, w_down, h, slope, work[1])


def space_forward(labels, frames, *rest):
    weights, x2, state, work = rest[:6], rest[6], rest[7:16], rest[16:]
    rows = space_rows(frames[0, 0].astype(F32), weights, [ref.at[0] for ref in state], work)
    block_of(rows, x2)


def build_bias(labels, pack, slots, patches, bias):
    tokens = slots * patches
    row = lax.broadcasted_iota(jnp.int32, (1, tokens), 1)
    column = lax.broadcasted_iota(jnp.int32, (tokens, 1), 0)

    def label_of(position):
        slot = position // patches
        value = jnp.zeros_like(position)
        for f in range(slots):
            value = jnp.where(slot == f, labels[pack, f], value)
        return value

    same_patch = (row % patches) == (column % patches)
    allowed = same_patch & (column <= row) & (label_of(column) == label_of(row))
    bias[...] = jnp.where(allowed, 0.0, -1e30)


def time_both(labels, x2, grad, *rest):
    gain, w_in, w_out, scale, w_up, w_down = rest[:6]
    g0, out, z0, gqkv, o, e1, z1, eu, h, e2 = rest[6:16]
    qkv, p, slope, bias, *work = rest[16:]
    slots, _, patches, _ = x2.shape
    build_bias(labels, pack_at(labels, pl.program_id(0)), slots, patches, bias)
    x = rows_of(x2[...])
    unit0, inverse0 = unit(x)
    z0[0] = unit0.astype(BF)
    qkv[...] = nn((unit0 * gain[...]).astype(BF), w_in[...]).astype(BF)
    attend(qkv, p, o.at[0], bias, work[0])
    r1 = x + nn(o[0], w_out[...])
    unit1, inverse1 = unit(r1)
    z1[0] = unit1.astype(BF)
    m = (unit1 * scale[...]).astype(BF)
    block_of(r1 + feed_up(m, w_up, w_down, h.at[0], slope, work[1]), out)
    g2 = rows_of(grad[...])
    e2[0] = g2.astype(BF)
    gm = feed_back(e2[0], w_up, w_down, slope, eu.at[0])
    g1 = g2 + unit_backward(gm * scale[...], unit1, inverse1)
    e1[0] = g1.astype(BF)
    slope[:, : g1.shape[1]] = nt(e1[0], w_out[...]).astype(BF)
    attend_backward(qkv, p, slope, gqkv.at[0], work[2], work[3])
    gn = nt(gqkv[0], w_in[...])
    block_of(g1 + unit_backward(gn * gain[...], unit0, inverse0), g0)


def alone_both(labels, frames, grad, *rest):
    space, (gain, w_in, w_out, scale, w_up, w_down) = rest[:6], rest[6:12]
    input_grad, out = rest[12:14]
    sz0, so, se1, sgqkv, sz1, seu, sh, se2 = [ref.at[0] for ref in rest[14:22]]
    z0, o, e1, gv, z1, eu, h, e2 = [ref.at[0] for ref in rest[22:30]]
    inv0, inv1, qkv, p, sslope, slope, go, *work = rest[30:]
    state = sz0, inv0, qkv, p, so, sz1, inv1, sh, sslope
    x = space_rows(frames[0, 0].astype(F32), space, state, work)
    width = x.shape[1]
    unit0, inverse0 = unit(x)
    z0[...] = unit0.astype(BF)
    o[...] = nn((unit0 * gain[...]).astype(BF), w_in[:, 2 * width :]).astype(BF)
    r1 = x + nn(o[...], w_out[...])
    unit1, inverse1 = unit(r1)
    z1[...] = unit1.astype(BF)
    m = (unit1 * scale[...]).astype(BF)
    out[0, 0] = r1 + feed_up(m, w_up, w_down, h, slope, work[1])
    e2[...] = grad[0, 0]
    g2 = grad[0, 0].astype(F32)
    gm = feed_back(e2[...], w_up, w_down, slope, eu)
    g1 = g2 + unit_backward(gm * scale[...], unit1, inverse1)
    e1[...] = g1.astype(BF)
    gv[...] = nt(e1[...], w_out[...]).astype(BF)
    gn = nt(gv[...], w_in[:, 2 * width :])
    g2 = g1 + unit_backward(gn * gain[...], unit0, inverse0)
    gain, w_in, w_out, scale, w_up, w_down = space
    se2[...] = g2.astype(BF)
    gm = feed_back(se2[...], w_up, w_down, sslope, seu)
    g1 = g2 + unit_backward(gm * scale[...], sz1[...].astype(F32), inv1[:, :1])
    se1[...] = g1.astype(BF)
    go[...] = nt(se1[...], w_out[...]).astype(BF)
    attend_backward(qkv, p, go, sgqkv, work[2], work[3])
    gn = nt(sgqkv[...], w_in[...])
    input_grad[0, 0] = g1 + unit_backward(gn * gain[...], sz0[...].astype(F32), inv0[:, :1])


def space_back_in(labels, gqkv, w_in, gain, z0, inv0, g1, moved, *rest):
    input_grad, result = rest[-2:]
    gn = nt(gqkv[0], w_in[...])
    grad = unit_backward(gn * gain[...], z0[0].astype(F32), inv0[0, :, :1])
    input_grad[0, 0] = g1[0] + grad
    result[0, 0] = rows_of(moved[...])


class Copies:
    def __init__(self, semaphores):
        self.semaphores, self.count, self.sent = semaphores, 0, []

    def fetch(self, source, target):
        copy = pltpu.make_async_copy(source, target, self.semaphores.at[self.count])
        self.count += 1
        copy.start()
        return copy

    def send(self, source, target):
        self.sent.append(self.fetch(source, target))

    def finish(self):
        for copy in self.sent:
            copy.wait()


def wait(*copies):
    for copy in copies:
        copy.wait()


def space_feed_kernel(
    hierarchical, ids, scale, inv1, g2_in, slope_in, z1_in, w_out_in, w_up_in, w_down_in, h_in, z1_one, h_one, eu_one, e2_one, *rest
):
    outs, scratch = rest[: 5], rest[5:]
    e1_out, go_out, g1_out = outs[:3]
    g2, slope, z1, w_out, w_up, w_down, h, eu, e2, e1, go, g1 = scratch[:12]
    copies = Copies(scratch[-1])
    packs, tokens, _ = e1.shape
    have = packs * tokens
    got_g2 = copies.fetch(g2_in, g2)
    got_down = [
        copies.fetch(w_down_in.at[pl.ds(at, CHUNK)], w_down.at[pl.ds(at, CHUNK)])
        for at in range(0, w_down.shape[0], CHUNK)
    ]
    got_slope = [copies.fetch(slope_in.at[pack], slope.at[pack]) for pack in range(packs)]
    got_up = copies.fetch(w_up_in, w_up)
    got_z1 = [
        copies.fetch(z1_in.at[pack], z1.at[pl.ds(pack * tokens, tokens)]) for pack in range(packs)
    ]
    got_out = copies.fetch(w_out_in, w_out)
    if hierarchical:
        got_rest = [
            copies.fetch(z1_one.at[0], z1.at[pl.ds(have, tokens)]),
            copies.fetch(eu_one.at[0], eu.at[pl.ds(have, tokens)]),
            copies.fetch(e2_one.at[0], e2.at[pl.ds(have, tokens)]),
            copies.fetch(h_one.at[0], h.at[pl.ds(have, tokens)]),
        ] + [
            copies.fetch(h_in.at[pack], h.at[pl.ds(pack * tokens, tokens)]) for pack in range(packs)
        ]
    wait(got_g2)
    for pack in range(packs):
        rows = slice(pack * tokens, (pack + 1) * tokens)
        e2[rows] = rows_of(g2[:, pack : pack + 1]).astype(BF)
        wait(got_slope[pack])
        if pack == 0:
            wait(*got_down, got_up)
        gm = feed_back(e2[rows], w_up, w_down, slope.at[pack], eu.at[rows])
        if pack == 0:
            wait(*got_z1, got_out)
        grad = unit_backward(gm * scale[...], z1[rows].astype(F32), inv1[pack, :, :1])
        total = rows_of(g2[:, pack : pack + 1]) + grad
        g1[pack] = total
        e1[pack] = total.astype(BF)
        go[pack] = nt(e1[pack], w_out[...]).astype(BF)
        copies.send(g1.at[pack], g1_out.at[pack])
        copies.send(e1.at[pack], e1_out.at[pack])
        copies.send(go.at[pack], go_out.at[pack])
    if hierarchical:
        wait(*got_rest)
        feed_tiles(copies, ids, z1, e2, eu, h, 0, scratch[12:14], outs[3:])
    else:
        copies.send(eu, outs[3])
        copies.send(e2, outs[4])
    copies.finish()


def space_attend_kernel(
    hierarchical, ids, qkv_in, p_in, go_in, z0_in, o_in, e1_in, z0_one, o_one, e1_one, gqkv_one, *rest
):
    outs, scratch = rest[: 3 if hierarchical else 1], rest[3 if hierarchical else 1 :]
    qkv, p, go, z0, o, e1, gqkv, gp, gs = scratch[:9]
    copies = Copies(scratch[-1])
    packs, tokens, _ = qkv.shape
    have = packs * tokens
    got = [
        [
            copies.fetch(qkv_in.at[pack], qkv.at[pack]),
            copies.fetch(go_in.at[pack], go.at[pack]),
            copies.fetch(p_in.at[pack], p.at[pack]),
        ]
        for pack in range(packs)
    ]
    if hierarchical:
        pairs = (z0_in, z0_one, z0), (o_in, o_one, o), (e1_in, e1_one, e1)
        got_rest = [
            copies.fetch(source.at[pack], target.at[pl.ds(pack * tokens, tokens)])
            for source, _, target in pairs
            for pack in range(packs)
        ]
        got_rest += [copies.fetch(one.at[0], target.at[pl.ds(have, tokens)]) for _, one, target in pairs]
        got_rest.append(copies.fetch(gqkv_one.at[0], gqkv.at[pl.ds(have, tokens)]))
    for pack in range(packs):
        wait(*got[pack])
        rows = pl.ds(pack * tokens, tokens)
        attend_backward(qkv.at[pack], p.at[pack], go.at[pack], gqkv.at[rows], gp, gs)
        copies.send(gqkv.at[rows], outs[0].at[pack])
    if hierarchical:
        wait(*got_rest)
        attend_tiles(copies, ids, z0, o, gqkv, e1, 0, scratch[9:11], outs[1:], gqkv.shape[0])
    copies.finish()


def to_send(labels, grad, out):
    for place in range(out.shape[1]):
        rows = grad[pack_at(labels, place), 0].astype(F32)
        out[:, place] = rows.reshape(out.shape[0], out.shape[2], out.shape[3]).astype(BF)


def pack_at(labels, place):
    packs, slots = labels.shape
    alone = packs - 1
    for pack in range(packs - 2, -1, -1):
        alone = jnp.where(labels[pack, slots - 1] == slots - 1, pack, alone)
    return jnp.where(place == packs - 1, alone, place + (place >= alone).astype(jnp.int32))


def without(kernel, first, count):
    def call(*refs):
        return kernel(*refs[:first], *refs[first + count :])

    return call


class Packs:
    def __init__(self, labels, first, count):
        self.labels, self.first, self.count = labels, first, count

    def call(self, kernel, args, outs, scratch=(), flops=0, after=()):
        first, last = self.first, self.labels.shape[0] - 2
        scalars = (self.labels,)

        def spec(kind, shape):
            rank = len(shape)
            if kind == "whole":
                return pl.BlockSpec(shape, lambda i, *s: (0,) * rank)
            if kind == "pack":
                return pl.BlockSpec(
                    (1,) + tuple(shape[1:]), lambda i, s: (pack_at(s, first + i),) + (0,) * (rank - 1)
                )
            if kind == "place":
                return pl.BlockSpec(
                    (1,) + tuple(shape[1:]), lambda i, *s: (first + i,) + (0,) * (rank - 1)
                )
            if kind == "step":
                return pl.BlockSpec(
                    (1,) + tuple(shape[1:]), lambda i, *s: (i,) + (0,) * (rank - 1)
                )
            if kind == "moved":
                return pl.BlockSpec(
                    (shape[0], 1, shape[2], shape[3]),
                    lambda i, *s: (0, jnp.minimum(i, last), 0, 0),
                )
            return pl.BlockSpec(memory_space=pl.ANY)

        in_specs = [spec(kind, array.shape) for kind, array in args]
        operands = [array for _, array in args]
        aliases = {}
        for index, (kind, shape, dtype, into) in enumerate(outs):
            if into is not None:
                aliases[len(scalars) + len(operands)] = index
                operands.append(into)
                in_specs.append(pl.BlockSpec(memory_space=pl.ANY))
        for array in after:
            operands.append(array)
            in_specs.append(pl.BlockSpec(memory_space=pl.ANY))
        moved = sum(a.size * a.dtype.itemsize for a in operands)
        unread = len(operands) - len(args)
        return pl.pallas_call(
            without(kernel, len(scalars) + len(args), unread),
            out_shape=[jax.ShapeDtypeStruct(shape, dtype) for _, shape, dtype, _ in outs],
            grid_spec=pltpu.PrefetchScalarGridSpec(
                num_scalar_prefetch=len(scalars),
                grid=(self.count,),
                in_specs=in_specs,
                out_specs=[spec(kind, shape) for kind, shape, _, _ in outs],
                scratch_shapes=list(scratch),
            ),
            input_output_aliases=aliases,
            compiler_params=pltpu.CompilerParams(
                vmem_limit_bytes=VMEM, dimension_semantics=("arbitrary",)
            ),
            cost_estimate=pl.CostEstimate(
                flops=int(flops * self.count), bytes_accessed=int(moved), transcendentals=0
            ),
        )(*scalars, *operands)


def feed_tiles(copies, ids, z1, e2, eu, h, at, held, outs):
    first = ids[0] == 0
    for step in range(4):
        tile = tn(z1[...], eu[:, step * CHUNK : (step + 1) * CHUNK]).astype(BF)
        s = step ^ ids[2]
        for z in range(4):
            even, odd = tile[128 * z : 128 * z + 64], tile[128 * z + 64 : 128 * z + 128]
            held[0][s, z ^ ids[1], at : at + 64] = jnp.where(first, even, odd)
            held[1][s, z ^ ids[1], at : at + 64] = jnp.where(first, odd, even)
        for ref, out in zip(held, outs):
            copies.send(ref.at[s, :, pl.ds(at, 64)], out.at[s, :, pl.ds(at, 64)])
    at = at + 64
    for step in range(4):
        tile = tn(e2[...], h[:, step * CHUNK : (step + 1) * CHUNK]).astype(BF)
        z = step ^ ids[1]
        for s in range(4):
            upper, lower = tile[128 * s : 128 * s + 64], tile[128 * s + 64 : 128 * s + 128]
            even = jnp.concatenate([upper[:, :256], lower[:, :256]], axis=1)
            odd = jnp.concatenate([upper[:, 256:], lower[:, 256:]], axis=1)
            held[0][s ^ ids[2], z, at : at + 64] = jnp.where(first, even, odd)
            held[1][s ^ ids[2], z, at : at + 64] = jnp.where(first, odd, even)
        for ref, out in zip(held, outs):
            copies.send(ref.at[:, z, pl.ds(at, 64)], out.at[:, z, pl.ds(at, 64)])


def attend_tiles(copies, ids, z0, o, gqkv, e1, at, held, outs, depth):
    first = ids[0] == 0
    for step in range(4):
        if step == 3:
            tile = tn(o[...], e1[...])
        else:
            rows = gqkv.shape[0] if step == 2 else depth
            tile = tn(z0[:rows], gqkv[:rows, step * CHUNK : (step + 1) * CHUNK])
        tile = tile.astype(BF)
        here = at + 16 * step
        for z in range(4):
            for s in range(4):
                row = 128 * z + 16 * s
                even, odd = tile[row : row + 16], tile[row + 64 : row + 80]
                held[0][s ^ ids[2], z ^ ids[1], here : here + 16] = jnp.where(first, even, odd)
                held[1][s ^ ids[2], z ^ ids[1], here : here + 16] = jnp.where(first, odd, even)
    for ref, out in zip(held, outs):
        copies.send(ref.at[:, :, pl.ds(at, 64)], out.at[:, :, pl.ds(at, 64)])


def time_weights_kernel(ids, *rest):
    names = 8
    shared, one, outs, scratch = rest[:names], rest[names : 2 * names], rest[16:18], rest[18:]
    z1, eu, e2, h, z0, gqkv, o, e1 = scratch[:names]
    held, copies = scratch[8:10], Copies(scratch[-1])
    packs, tokens, _ = shared[0].shape
    have = packs * tokens
    got = []
    for source, single, target in zip(shared, one, scratch):
        wide_target = target.at[pl.ds(have, tokens)]
        if single.shape[2] < target.shape[1]:
            wide_target = target.at[pl.ds(have, tokens), pl.ds(target.shape[1] - single.shape[2], single.shape[2])]
        got.append(
            [copies.fetch(source.at[pack], target.at[pl.ds(pack * tokens, tokens)]) for pack in range(packs)]
            + [copies.fetch(single.at[0], wide_target)]
        )
    wait(*got[0], *got[1], *got[2], *got[3])
    feed_tiles(copies, ids, z1, e2, eu, h, 0, held, outs)
    wait(*got[4], *got[5], *got[6], *got[7])
    attend_tiles(copies, ids, z0, o, gqkv, e1, 128, held, outs, have)
    copies.finish()


def manual_call(kernel, ids, args, outs, scratch, semaphores, small=0, after=(), flops=0):
    anywhere = pl.BlockSpec(memory_space=pl.ANY)
    return pl.pallas_call(
        without(kernel, 1 + len(args), len(after)),
        out_shape=[jax.ShapeDtypeStruct(shape, dtype) for shape, dtype in outs],
        in_specs=[pl.BlockSpec(memory_space=pltpu.SMEM)]
        + [pl.BlockSpec(memory_space=pltpu.VMEM)] * small
        + [anywhere] * (len(args) - small + len(after)),
        out_specs=[anywhere] * len(outs),
        scratch_shapes=[pltpu.VMEM(shape, dtype) for shape, dtype in scratch]
        + [pltpu.SemaphoreType.DMA((semaphores,))],
        compiler_params=pltpu.CompilerParams(vmem_limit_bytes=VMEM),
        cost_estimate=pl.CostEstimate(
            flops=int(flops), bytes_accessed=sum(a.size * 2 for a in args), transcendentals=0
        ),
    )(ids, *args, *after)


def swap(array, axis, size, mask):
    return lax.ppermute(array, axis, [(i, i ^ mask) for i in range(size)])


def add(*terms):
    total = terms[0].astype(F32)
    for term in terms[1:]:
        total = total + term.astype(F32)
    return total.astype(BF)


def core_sum(mine, other):
    got = swap(other, "tm", 8, 1)
    return [add(mine[d], got[d]) for d in range(1, 4)], (mine[0], got[0])


def rest_sum(parts, own):
    got = [swap(part, "stream", 4, d + 1) for d, part in enumerate(parts)]
    rows = [add(*[term[d] for term in (*own, *got)]) for d in range(4)]
    got = [swap(rows[d], "tm", 8, 2 * d) for d in range(1, 4)]
    final = add(rows[0], *got)
    return [final] + [swap(final, "stream", 4, d) for d in range(1, 4)]


def column(row):
    size = row.shape[1]
    eye = lax.broadcasted_iota(jnp.int32, (size, size), 0) == lax.broadcasted_iota(
        jnp.int32, (size, size), 1
    )
    return jnp.sum(jnp.where(eye, row, 0.0), axis=1, keepdims=True)


def as_row(col):
    size = col.shape[0]
    eye = lax.broadcasted_iota(jnp.int32, (size, size), 0) == lax.broadcasted_iota(
        jnp.int32, (size, size), 1
    )
    return jnp.sum(jnp.where(eye, col, 0.0), axis=0, keepdims=True)


def own_rows(ids, vector):
    rank = 2 * ids[1] + ids[0]
    return column(vector[pl.ds(rank, 1), :])


def finish_feed(ids, pieces, at, w_up, scale, scale_grad, up_grad, down_grad):
    factor = own_rows(ids, scale)
    for d, piece in enumerate(pieces):
        s = ids[2] ^ d
        up_grad[:, pl.ds(pl.multiple_of(512 * s, 512), 512)] = piece[at : at + 64].astype(F32)
        lower = piece[at + 64 : at + 128].astype(F32)
        whole = jnp.concatenate([lower[:, :256], lower[:, 256:]], axis=0)
        down_grad[:, pl.ds(pl.multiple_of(128 * s, 128), 128)] = whole.T
    total = up_grad[...]
    scale_grad[...] = as_row(jnp.sum(total * w_up[...].astype(F32), axis=1, keepdims=True))
    up_grad[...] = total * factor


def finish_attend(ids, pieces, at, w_in, gain, gain_grad, in_grad, out_grad):
    factor = own_rows(ids, gain)
    for d, piece in enumerate(pieces):
        rows = pl.ds(pl.multiple_of(16 * (ids[2] ^ d), 16), 16)
        for third in range(3):
            in_grad[rows, 512 * third : 512 * third + 512] = piece[
                at + 16 * third : at + 16 * third + 16
            ].astype(F32)
        out_grad[rows, :] = piece[at + 48 : at + 64].astype(F32)
    total = in_grad[...]
    gain_grad[...] = as_row(jnp.sum(total * w_in[...].astype(F32), axis=1, keepdims=True))
    in_grad[...] = total * factor


def finish_feed_kernel(ids, p0, p1, p2, p3, w_up, scale, *outs):
    finish_feed(ids, (p0, p1, p2, p3), 0, w_up, scale, *outs)


def finish_attend_kernel(ids, p0, p1, p2, p3, w_in, gain, *outs):
    finish_attend(ids, (p0, p1, p2, p3), 0, w_in, gain, *outs)


def finish_all_kernel(ids, p0, p1, p2, p3, w_up, scale, w_in, gain, *outs):
    finish_feed(ids, (p0, p1, p2, p3), 0, w_up, scale, *outs[:3])
    finish_attend(ids, (p0, p1, p2, p3), 128, w_in, gain, *outs[3:])


def finish_call(kernel, ids, pieces, pairs, outs):
    whole = pl.BlockSpec(pieces[0].shape, lambda i, *s: (0, 0))
    specs, operands = [], []
    for weight, vector in pairs:
        height = weight.shape[0] // 8
        specs += [
            pl.BlockSpec((height, weight.shape[1]), lambda i, s: (2 * s[1] + s[0], 0)),
            pl.BlockSpec((8, height), lambda i, *s: (0, 0)),
        ]
        operands += [weight, vector.reshape(8, height)]
    results = pl.pallas_call(
        kernel,
        out_shape=[jax.ShapeDtypeStruct(shape, F32) for shape in outs],
        grid_spec=pltpu.PrefetchScalarGridSpec(
            num_scalar_prefetch=1,
            grid=(1,),
            in_specs=[whole] * 4 + specs,
            out_specs=[pl.BlockSpec(shape, lambda i, *s: (0, 0)) for shape in outs],
        ),
        compiler_params=pltpu.CompilerParams(vmem_limit_bytes=VMEM),
    )(ids, *pieces, *operands)
    return [a.reshape(-1) if a.shape[0] == 1 else a for a in results]


def plain_grads(z, grads, left, right, weight, vector):
    product = tn(z, grads)
    vector_grad = jnp.sum(product * weight.astype(F32), axis=1)
    sums = []
    for term in (vector_grad, product * vector[:, None], tn(left, right)):
        share = lax.psum_scatter(term.astype(BF), "tm", scatter_dimension=0, tiled=True)
        sums.append(lax.psum(share, "stream").astype(F32))
    return sums


def everyone_once(labels, grad, moved):
    _, shape, dtype, _ = moved
    return pl.pallas_call(
        to_send,
        out_shape=[jax.ShapeDtypeStruct(shape, dtype)],
        grid_spec=pltpu.PrefetchScalarGridSpec(
            num_scalar_prefetch=1,
            grid=(1,),
            in_specs=[pl.BlockSpec(grad.shape, lambda i, s: (0, 0, 0, 0))],
            out_specs=[pl.BlockSpec(shape, lambda i, s: (0, 0, 0, 0))],
        ),
        compiler_params=pltpu.CompilerParams(vmem_limit_bytes=VMEM),
    )(labels, grad)


def per_device(
    ranks,
    streams,
    frames,
    space_gain,
    space_input,
    space_output,
    space_scale,
    space_up,
    space_down,
    time_gain,
    time_input,
    time_output,
    time_scale,
    time_up,
    time_down,
    clip_labels,
    output_grad,
):
    packs, _, tokens, width = frames.shape
    slots = clip_labels.shape[1]
    patches = tokens // ranks
    hidden = space_up.shape[1]
    some = packs - 1
    hierarchical = (ranks, streams) == (8, 4)
    tm = lax.axis_index("tm")
    ids = jnp.stack([tm % 2, tm // 2, lax.axis_index("stream")]).astype(jnp.int32)
    shared = Packs(clip_labels, 0, some)
    single = Packs(clip_labels, some, 1)

    def row(vector):
        return vector.reshape(1, -1)

    def exchange(array):
        return lax.all_to_all(array, "tm", split_axis=0, concat_axis=0, tiled=True)

    def steps(count, *tails):
        return [("step", (count,) + tail, BF, None) for tail in tails]

    moved = ("moved", (slots, some, patches, width), BF, None)
    whole = ("pack", frames.shape, F32, None)
    flops = 2 * tokens * width * (4 * width + 2 * hidden)

    (sent,) = everyone_once(clip_labels, output_grad, moved)
    grad_moved = exchange(sent)

    space_args = [
        ("whole", row(space_gain)),
        ("whole", space_input),
        ("whole", space_output),
        ("whole", row(space_scale)),
        ("whole", space_up),
        ("whole", space_down),
    ]
    time_args = [
        ("whole", row(time_gain)),
        ("whole", time_input),
        ("whole", time_output),
        ("whole", row(time_scale)),
        ("whole", time_up),
        ("whole", time_down),
    ]
    rows_w, rows_3, rows_h = (tokens, width), (tokens, 3 * width), (tokens, hidden)
    spread = ("step", (some, tokens, LANES), F32, None)
    x2, sz0, sinv0, sqkv, sp, so, sz1, sinv1, sh, sslope = shared.call(
        space_forward,
        [("pack", frames)] + space_args,
        [moved]
        + steps(some, rows_w)
        + [spread]
        + steps(some, rows_3, (HEADS, tokens, tokens), rows_w, rows_w)
        + [spread]
        + steps(some, rows_h, rows_h),
        scratch=work_shapes(tokens),
        flops=flops,
        after=(sent,),
    )
    x2, grad_moved = lax.optimization_barrier((x2, grad_moved))
    x2_moved = exchange(x2)

    block_tails = [rows_w, rows_w, rows_w, rows_3, rows_w, rows_h, rows_h, rows_w]
    time_tails = [rows_w, rows_w, rows_w, rows_w, rows_w, rows_h, rows_h, rows_w]
    input_grad, result, *alone = single.call(
        alone_both,
        [("pack", frames), ("pack", output_grad)] + space_args + time_args,
        [whole, whole] + steps(1, *block_tails) + steps(1, *time_tails),
        scratch=[
            pltpu.VMEM((tokens, LANES), F32),
            pltpu.VMEM((tokens, LANES), F32),
            pltpu.VMEM(rows_3, BF),
            pltpu.VMEM((HEADS, tokens, tokens), BF),
            pltpu.VMEM(rows_h, BF),
            pltpu.VMEM(rows_h, BF),
            pltpu.VMEM(rows_w, BF),
        ]
        + work_shapes(tokens),
        flops=6 * flops,
        after=(x2,),
    )
    sz0_one, so_one, se1_one, sgqkv_one, sz1_one, seu_one, sh_one, se2_one = alone[:8]
    tz0_one, to_one, te1_one, tgv_one, tz1_one, teu_one, th_one, te2_one = alone[8:]

    g0, out, tz0, tgqkv, to, te1, tz1, teu, th, te2 = shared.call(
        time_both,
        [("moved", x2_moved), ("moved", grad_moved)] + time_args,
        [moved, moved] + steps(some, rows_w, rows_3, rows_w, rows_w, rows_w, rows_h, rows_h, rows_w),
        scratch=[
            pltpu.VMEM(rows_3, BF),
            pltpu.VMEM((HEADS, tokens, tokens), BF),
            pltpu.VMEM(rows_h, BF),
            pltpu.VMEM((tokens, tokens), F32),
        ]
        + work_shapes(tokens),
        flops=3 * flops,
        after=(sz0_one,),
    )
    g0_moved = exchange(g0)
    out, g0_moved = lax.optimization_barrier((out, g0_moved))
    out_moved = exchange(out)

    everything = packs * tokens
    feed_shapes = [(1, width // 8), (width // 8, hidden), (hidden // 8, width)]
    attend_shapes = [(1, width // 8), (width // 8, 3 * width), (width // 8, width)]
    time_shared = [tz1, teu, te2, th, tz0, tgqkv, to, te1]
    time_one = [tz1_one, teu_one, te2_one, th_one, tz0_one, tgv_one, to_one, te1_one]
    time_parts = ()
    if hierarchical:
        parts_shape = ((4, 4, 192, CHUNK), BF)
        mine, other = manual_call(
            time_weights_kernel,
            ids,
            time_shared + time_one,
            [parts_shape] * 2,
            [((everything, a.shape[2]), BF) for a in time_shared] + [parts_shape] * 2,
            8 * packs + 18,
            flops=packs * flops,
        )
        time_parts, own = core_sum(mine, other)
        time_grads = finish_call(
            finish_all_kernel,
            ids,
            rest_sum(time_parts, own),
            [(time_up, time_scale), (time_input, time_gain)],
            feed_shapes + attend_shapes,
        )
    else:
        grad_one = jnp.pad(tgv_one, ((0, 0), (0, 0), (2 * width, 0)))
        joined = [joint(a, b) for a, b in zip(time_shared, time_one[:5] + [grad_one] + time_one[6:])]
        time_grads = plain_grads(joined[0], joined[1], joined[3], joined[2], time_up, time_scale)
        time_grads += plain_grads(joined[4], joined[5], joined[6], joined[7], time_input, time_gain)

    shared_w, shared_h = (some,) + rows_w, (some,) + rows_h
    feed_args = [row(space_scale), sinv1, g0_moved, sslope, sz1, space_output, space_up, space_down]
    feed_args += [sh, sz1_one, sh_one, seu_one, se2_one]
    parts_shape = ((4, 4, 128, CHUNK), BF)
    state_shapes = [((everything, hidden), BF), ((everything, width), BF)]
    se1, sgo, sg1, *weights = manual_call(
        functools.partial(space_feed_kernel, hierarchical),
        ids,
        feed_args,
        [(shared_w, BF), (shared_w, BF), (shared_w, F32)]
        + ([parts_shape] * 2 if hierarchical else state_shapes),
        [
            (g0_moved.shape, BF),
            (shared_h, BF),
            ((everything, width), BF),
            (space_output.shape, BF),
            (space_up.shape, BF),
            (space_down.shape, BF),
            ((everything, hidden), BF),
            *state_shapes,
            (shared_w, BF),
            (shared_w, BF),
            (shared_w, F32),
        ]
        + ([parts_shape] * 2 if hierarchical else []),
        64,
        small=2,
        after=time_parts,
        flops=packs * flops,
    )
    parts = ()
    if hierarchical:
        parts, own = core_sum(*weights)
        feed_grads = finish_call(
            finish_feed_kernel, ids, rest_sum(parts, own), [(space_up, space_scale)], feed_shapes
        )
    else:
        have = some * tokens
        seu, se2 = [a[:have].reshape(some, tokens, -1) for a in weights]
        feed_grads = plain_grads(
            joint(sz1, sz1_one),
            joint(seu, seu_one),
            joint(sh, sh_one),
            joint(se2, se2_one),
            space_up,
            space_scale,
        )
    parts_shape = ((4, 4, 64, CHUNK), BF)
    sgqkv, *weights = manual_call(
        functools.partial(space_attend_kernel, hierarchical),
        ids,
        [sqkv, sp, sgo, sz0, so, se1, sz0_one, so_one, se1_one, sgqkv_one],
        [((some,) + rows_3, BF)] + ([parts_shape] * 2 if hierarchical else []),
        [
            ((some,) + rows_3, BF),
            (sp.shape, BF),
            (shared_w, BF),
            ((everything, width), BF),
            ((everything, width), BF),
            ((everything, width), BF),
            ((everything, 3 * width), BF),
            ((4, tokens, tokens), BF),
            ((HEADS, tokens, tokens), BF),
        ]
        + ([parts_shape] * 2 if hierarchical else []),
        64,
        after=parts,
        flops=packs * flops,
    )
    if hierarchical:
        attend_grads = finish_call(
            finish_attend_kernel,
            ids,
            rest_sum(*core_sum(*weights)),
            [(space_input, space_gain)],
            attend_shapes,
        )
    else:
        attend_grads = plain_grads(
            joint(sz0, sz0_one),
            joint(sgqkv, sgqkv_one),
            joint(so, so_one),
            joint(se1, se1_one),
            space_input,
            space_gain,
        )
    input_grad, result = shared.call(
        space_back_in,
        [
            ("step", sgqkv),
            ("whole", space_input),
            ("whole", row(space_gain)),
            ("step", sz0),
            ("step", sinv0),
            ("step", sg1),
            ("moved", out_moved),
        ],
        [("pack", frames.shape, F32, input_grad), ("pack", frames.shape, F32, result)],
        flops=flops // 4,
    )
    grads = attend_grads + feed_grads + time_grads[3:] + time_grads[:3]
    return (result, input_grad, *grads)


def joint(shared, one):
    return jnp.concatenate([shared, one]).reshape(-1, shared.shape[-1])


def solution(mesh):
    tokens = P("stream", "tm", None, None)
    vector, matrix = P("tm"), P("tm", None)
    return jax.shard_map(
        functools.partial(per_device, mesh.shape["tm"], mesh.shape["stream"]),
        mesh=mesh,
        in_specs=(tokens,) + (P(),) * 12 + (P("stream", None), tokens),
        out_specs=(tokens, tokens) + (vector, matrix, matrix, vector, matrix, matrix) * 2,
        check_vma=False,
    )
```

time: 367 us -> 282 us (0.77)
  local copies, waits for them, and re-layouts: 65.8 us -> 7.06 us
  blocking collectives: 0 us -> 24.7 us
  Pallas kernels: 146 us -> 122 us
  starting transfers between devices: 72.6 us -> 49.8 us
  other arithmetic: 23.7 us -> 17.6 us
  waiting for transfers between devices: 50.8 us -> 56 us
    unnamed x208 -> x42, local copies, waits for them, and re-layouts: 65.5 us -> 4.39 us
    pallas_call x14 -> x8, Pallas kernels: 140 us -> 112 us  [the longest x4 70.4 us: call(): pl.pallas_call(without(kernel, len(scalars) + len(args), unread), out_sha...]
    all_to_all x0 -> x1, blocking collectives: none -> 24.7 us  [exchange(): return lax.all_to_all(array, 'tm', split_axis=0, concat_axis=0, tiled=True)]
    ppermute x40 -> x30, waiting for transfers between devices: 32.6 us -> 50.6 us  [swap(): return lax.ppermute(array, axis, [(i, i ^ mask) for i in range(size)])]
    ppermute x40 -> x30, starting transfers between devices: 51.4 us -> 36.2 us  [swap(): return lax.ppermute(array, axis, [(i, i ^ mask) for i in range(size)])]
    all_to_all x4 -> x3, waiting for transfers between devices: 18.2 us -> 5.44 us  [exchange(): return lax.all_to_all(array, 'tm', split_axis=0, concat_axis=0, tiled=True)]
    all_to_all x4 -> x3, starting transfers between devices: 21.1 us -> 13.6 us  [exchange(): return lax.all_to_all(array, 'tm', split_axis=0, concat_axis=0, tiled=True)]
    add x4 -> x0, other arithmetic: 5.98 us -> none  [add(): total = total + term.astype(F32)]
  transfers between devices with their start and end apart: 44 -> 33, of which waited for: 10 -> 12; matrix products, arithmetic and copies ran while one was open for 6% -> 6% of each run, Pallas kernels for 26% -> 22%
where the time goes in v2:
time: 282 us; the launch traced here: 278 us
  Pallas kernels  122 us (43%)
  waiting for transfers between devices  56 us (20%)
  starting transfers between devices  49.8 us (18%)
  blocking collectives  24.7 us (9%)
  other arithmetic  17.6 us (6%)
  local copies, waits for them, and re-layouts  7.06 us (3%)
    pallas_call x4, Pallas kernels, call(): pl.pallas_call(without(kernel, len(scalars) + len(args), unread), out_sha...  70.4 us
    ppermute x30, waiting for transfers between devices, swap(): return lax.ppermute(array, axis, [(i, i ^ mask) for i in range(size)])  50.6 us
    pallas_call x3, Pallas kernels, manual_call(): pl.pallas_call(without(kernel, 1 + len(args), len(after)), out_shape=[jax...  39.1 us
    ppermute x30, starting transfers between devices, swap(): return lax.ppermute(array, axis, [(i, i ^ mask) for i in range(size)])  36.2 us
    all_to_all x1, blocking collectives, exchange(): return lax.all_to_all(array, 'tm', split_axis=0, concat_axis=0, tiled=True)  24.7 us
    convert_element_type x9, other arithmetic, add(): return total.astype(BF)  17 us
    all_to_all x3, starting transfers between devices, exchange(): return lax.all_to_all(array, 'tm', split_axis=0, concat_axis=0, tiled=True)  13.6 us
    pallas_call x3, Pallas kernels, finish_call(): pl.pallas_call(kernel, out_shape=[jax.ShapeDtypeStruct(shape, F32) for sh...  9.21 us
  transfers between devices with their start and end apart: 33, of which 12 were waited for; matrix products, arithmetic and copies ran while one was open for 6% of the time, Pallas kernels for 22%

profile of v2, /device:TPU:0, one launch (start us, length us, event | category | flops | bytes accessed | tf_op | source)
XLA Modules:
  0.0 277.8 jit_solution(11720559196769258421)
XLA Ops:
  0.6 2.8 %shard_map.254.refs_8_ = bf16[8,3,32,512]{3,2,1,0:T(8,128)(2,1)} custom-call(s32[4,8]{1,0:T(4,128)} %refs_0_.7, bf16[4,1,256,512]{3,2,1,0:T(8,128)(2,1)} %refs_2_.2), custom_call_target="tpu_custom_call" | custom-call | tf_op jit(solution)/shard_map/pallas_call | solution.py:705
  3.5 6.3 %all-to-all-start = ((bf16[8,3,32,512]{3,2,1,0:T(8,128)(2,1)}), bf16[8,3,32,512]{3,2,1,0:T(8,128)(2,1)S(1)}, u32[]{:S(2)}, u32[]{:S(2)}) async-start(bf16[8,3,32,512]{3,2,1,0:T(8,128)(2,1)} %shard_map.254.refs_8_), calls=%async_computation | async-start | bytes 1572864 | tf_op jit(solution)/shard_map/all_to_all | solution.py:752
  9.8 16.9 %shard_map.255 = (bf16[8,3,32,512]{3,2,1,0:T(8,128)(2,1)}, bf16[3,256,512]{2,1,0:T(8,128)(2,1)}, f32[3,256,128]{2,1,0:T(8,128)}, bf16[3,256,1536]{2,1,0:T(8,128)...) custom-call(s32[4,8]{1,0:T(4,128)} %refs_0_.7, ...), custom_call_target="tpu_custom_call" | custom-call | flops 4831838208 | bytes 8130560 | tf_op jit(solution)/shard_map/pallas_call | solution.py:478
  26.8 4.0 %all-to-all-done.refs_2_ = bf16[8,3,32,512]{3,2,1,0:T(8,128)(2,1)S(1)} async-done(((bf16[8,3,32,512]{3,2,1,0:T(8,128)(2,1)}), bf16[8,3,32,512]{3,2,1,0:T(8,128)(2,1)S(1)}, u32[]{:S(2)}, u32[]{:S(2)}) %all-to-all-start) | async-done | bytes 786464 | tf_op jit(solution)/shard_map/all_to_all | solution.py:752
  30.8 3.7 %all-to-all-start.1 = ((bf16[8,3,32,512]{3,2,1,0:T(8,128)(2,1)}), bf16[8,3,32,512]{3,2,1,0:T(8,128)(2,1)S(1)}, u32[]{:S(2)}, u32[]{:S(2)}) async-start(bf16[8,3,32,512]{3,2,1,0:T(8,128)(2,1)} %get-tuple-element.84.refs_15_), calls=%async_computation.1 | async-start | bytes 1572864 | tf_op jit(solution)/shard_map/all_to_all | solution.py:752
  35.2 18.8 %shard_map.256 = (f32[4,1,256,512]{3,2,1,0:T(8,128)}, f32[4,1,256,512]{3,2,1,0:T(8,128)}, bf16[1,256,512]{2,1,0:T(8,128)(2,1)}, bf16[1,256,512]{2,1,0:T(8,128)(2...) custom-call(s32[4,8]{1,0:T(4,128)} %refs_0_.7, ...), custom_call_target="tpu_custom_call" | custom-call | flops 9663676416 | bytes 15474688 | tf_op jit(solution)/shard_map/pallas_call | solution.py:478
  56.3 27.3 %shard_map.257 = (bf16[8,3,32,512]{3,2,1,0:T(8,128)(2,1)}, bf16[8,3,32,512]{3,2,1,0:T(8,128)(2,1)}, bf16[3,256,512]{2,1,0:T(8,128)(2,1)}, bf16[3,256,1536]{2,1,0...) custom-call(s32[4,8]{1,0:T(4,128)} %refs_0_.7, ...), custom_call_target="tpu_custom_call" | custom-call | flops 14495514624 | bytes 8130560 | tf_op jit(solution)/shard_map/pallas_call | solution.py:478
  83.6 13.3 %shard_map.258 = (bf16[4,4,192,512]{3,2,1,0:T(8,128)(2,1)}, bf16[4,4,192,512]{3,2,1,0:T(8,128)(2,1)}) custom-call(s32[3]{0:T(128)} %pad_add_fusion.refs_0_.ids, bf16[3,256,512]{2,1,0:T(8,128)(2,1)} %get-tuple-element.97.refs_1_, bf16[3,256,2048]{2,1,0:T(8,128)(2,1)} %get-tuple-element.98.refs_2_, bf16[3,256,512]{2,1,0:T(8,128)(2,1)} %get-tuple-element.99.refs_3_, ...), custom_call_target="tpu_custom_call" | custom-call | flops 6442450944 | bytes 16252928 | tf_op jit(solution)/shard_map/pallas_call | solution.py:568
  97.0 24.7 %all_to_all.20.refs_3_ = bf16[8,3,32,512]{3,2,1,0:T(8,128)(2,1)} all-to-all(bf16[8,3,32,512]{3,2,1,0:T(8,128)(2,1)S(1)} %copy-done.5), channel_id=1, replica_groups=mesh['stream'=4,'tm'=8] {'tm'}, dimensions={0} | all-to-all | bytes 1572864 | tf_op jit(solution)/shard_map/all_to_all | solution.py:752
  121.7 3.5 %fusion.2 = (bf16[4,192,512]{2,1,0:T(8,128)(2,1)}, bf16[4,192,512]{2,1,0:T(8,128)(2,1)}, bf16[4,192,512]{2,1,0:T(8,128)(2,1)}) fusion(bf16[4,4,192,512]{3,2,1,0:T(8,128)(2,1)S(1)} %collective-permute-done, bf16[4,4,192,512]{3,2,1,0:T(8,128)(2,1)} %get-tuple-element.113), kind=kLoop, calls=%fused_computation.8 | loop fusion | flops 4718592 | bytes 7077888 | tf_op jit(solution)/shard_map/convert_element_type | solution.py:592
  125.2 15.5 %shard_map.259 = (bf16[3,256,512]{2,1,0:T(8,128)(2,1)}, bf16[3,256,512]{2,1,0:T(8,128)(2,1)}, f32[3,256,512]{2,1,0:T(8,128)}, bf16[4,4,128,512]{3,2,1,0:T(8,128)(2,1)}, bf16[4,4,128,512]{3,2,1,0:T(8,128)(2,1)}) custom-call(s32[3]{0:T(128)} %pad_add_fusion.refs_0_.ids, f32[1,512]{1,0:T(1,128)} %bitcast.244, f32[3,256,128]{2,1,0:T(8,128)} %get-tuple-element.82.refs_2_, ...), custom_call_target="tpu_custom_call" | custom-call | flops 6442450944 | bytes 15401984 | tf_op jit(solution)/shard_map/pallas_call | solution.py:568
  140.8 2.5 collective-permute-start.23
  145.1 3.5 %fusion.5 = (bf16[4,128,512]{2,1,0:T(8,128)(2,1)}, bf16[4,128,512]{2,1,0:T(8,128)(2,1)}, bf16[4,128,512]{2,1,0:T(8,128)(2,1)}) fusion(bf16[4,4,128,512]{3,2,1,0:T(8,128)(2,1)S(1)} %collective-permute-done.1, bf16[4,4,128,512]{3,2,1,0:T(8,128)(2,1)} %get-tuple-element.122), kind=kLoop, calls=%fused_computation.11 | loop fusion | flops 3145728 | bytes 4718592 | tf_op jit(solution)/shard_map/convert_element_type | solution.py:592
  148.6 10.3 %shard_map.260 = (bf16[3,256,1536]{2,1,0:T(8,128)(2,1)}, bf16[4,4,64,512]{3,2,1,0:T(8,128)(2,1)}, bf16[4,4,64,512]{3,2,1,0:T(8,128)(2,1)}) custom-call(s32[3]{0:T(128)} %pad_add_fusion.refs_0_.ids, bf16[3,256,1536]{2,1,0:T(8,128)(2,1)} %get-tuple-element.80.refs_1_, bf16[3,8,256,256]{3,2,1,0:T(8,128)(2,1)} %get-tuple-element.81.refs_2_, ...), custom_call_target="tpu_custom_call" | custom-call | flops 6442450944 | bytes 10223616 | tf_op jit(solution)/shard_map/pallas_call | solution.py:568
  159.1 3.2 %collective-permute-done.23 = bf16[4,192,512]{2,1,0:T(8,128)(2,1)S(1)} collective-permute-done((bf16[4,192,512]{2,1,0:T(8,128)(2,1)}, bf16[4,192,512]{2,1,0:T(8,128)(2,1)S(1)}, u32[]{:S(2)}, u32[]{:S(2)}) %collective-permute-start.23) | collective-permute-done | bytes 786464 | tf_op jit(solution)/shard_map/ppermute | solution.py:585
  162.3 16.5 %collective-permute-done.22 = bf16[4,192,512]{2,1,0:T(8,128)(2,1)} collective-permute-done((bf16[4,192,512]{2,1,0:T(8,128)(2,1)}, bf16[4,192,512]{2,1,0:T(8,128)(2,1)}, u32[]{:S(2)}, u32[]{:S(2)}) %collective-permute-start.22) | collective-permute-done | bytes 786464 | tf_op jit(solution)/shard_map/ppermute | solution.py:585
  178.9 1.9 fusion.8
  182.1 3.1 %collective-permute-start.24 = (bf16[192,512]{1,0:T(8,128)(2,1)S(1)}, bf16[192,512]{1,0:T(8,128)(2,1)S(1)}, u32[]{:S(2)}, u32[]{:S(2)}) collective-permute-start(bf16[192,512]{1,0:T(8,128)(2,1)S(1)} %get-tuple-element.146), channel_id=1, source_target_pairs={{0,2},{1,3},{2,0},{3,1},{4,6},{5,7},{6,4},{7,5},{8,10},{9,11},{10,... | collective-permute-start | bytes 589832 | tf_op jit(solution)/shard_map/ppermute | solution.py:585
  186.9 3.6 %collective-permute-done.26 = bf16[192,512]{1,0:T(8,128)(2,1)S(1)} collective-permute-done((bf16[192,512]{1,0:T(8,128)(2,1)S(1)}, bf16[192,512]{1,0:T(8,128)(2,1)S(1)}, u32[]{:S(2)}, u32[]{:S(2)}) %collective-permute-start.26) | collective-permute-done | bytes 196640 | tf_op jit(solution)/shard_map/ppermute | solution.py:585
  192.0 7.4 %collective-permute-done.25 = bf16[192,512]{1,0:T(8,128)(2,1)S(1)} collective-permute-done((bf16[192,512]{1,0:T(8,128)(2,1)S(1)}, bf16[192,512]{1,0:T(8,128)(2,1)S(1)}, u32[]{:S(2)}, u32[]{:S(2)}) %collective-permute-start.25) | collective-permute-done | bytes 196640 | tf_op jit(solution)/shard_map/ppermute | solution.py:585
  202.8 3.5 %all-to-all-start.3 = ((bf16[8,3,32,512]{3,2,1,0:T(8,128)(2,1)}), bf16[8,3,32,512]{3,2,1,0:T(8,128)(2,1)S(1)}, u32[]{:S(2)}, u32[]{:S(2)}) async-start(bf16[8,3,32,512]{3,2,1,0:T(8,128)(2,1)} %get-tuple-element.127), calls=%async_computation.3 | async-start | bytes 1572864 | tf_op jit(solution)/shard_map/all_to_all | solution.py:752
  206.4 10.4 %collective-permute-done.27.p1 = bf16[192,512]{1,0:T(8,128)(2,1)S(1)} collective-permute-done((bf16[192,512]{1,0:T(8,128)(2,1)S(1)}, bf16[192,512]{1,0:T(8,128)(2,1)S(1)}, u32[]{:S(2)}, u32[]{:S(2)}) %collective-permute-start.27) | collective-permute-done | bytes 196640 | tf_op jit(solution)/shard_map/ppermute | solution.py:585
  221.3 5.0 %collective-permute-done.28.p2 = bf16[192,512]{1,0:T(8,128)(2,1)S(1)} collective-permute-done((bf16[192,512]{1,0:T(8,128)(2,1)S(1)}, bf16[192,512]{1,0:T(8,128)(2,1)S(1)}, u32[]{:S(2)}, u32[]{:S(2)}) %collective-permute-start.28) | collective-permute-done | bytes 196640 | tf_op jit(solution)/shard_map/ppermute | solution.py:585
  232.5 3.4 %shard_map.264 = (f32[1,64]{1,0:T(1,128)}, f32[64,2048]{1,0:T(8,128)}, f32[256,512]{1,0:T(8,128)}, f32[1,64]{1,0:T(1,128)}, f32[64,1536]{1,0:T(8,128)}, /*index=5*/f32[64,512]{1,0:T(8,128)}) custom-call(s32[3]{0:T(128)} %pad_add_fusion.refs_0_.ids, bf16[192,512]{1,0:T(8,128)(2,1)} %copy-done.2, bf16[192,512]{1,0:T(8,128)(2,1)} %copy-done.8, ...), custom_call_target="tpu_custom_call" | custom-call | tf_op jit(solution)/shard_map/pallas_call | solution.py:679
  239.3 3.0 %collective-permute-start.15 = (bf16[128,512]{1,0:T(8,128)(2,1)S(1)}, bf16[128,512]{1,0:T(8,128)(2,1)S(1)}, u32[]{:S(2)}, u32[]{:S(2)}) collective-permute-start(bf16[128,512]{1,0:T(8,128)(2,1)S(1)} %get-tuple-element.152), channel_id=1, source_target_pairs={{0,2},{1,3},{2,0},{3,1},{4,6},{5,7},{6,4},{7,5},{8,10},{9,11},{10,... | collective-permute-start | bytes 393224 | tf_op jit(solution)/shard_map/ppermute | solution.py:585
  246.2 2.4 collective-permute-start.6
  248.5 2.3 collective-permute-done.16
  252.2 2.8 %collective-permute-start.18 = (bf16[128,512]{1,0:T(8,128)(2,1)S(1)}, bf16[128,512]{1,0:T(8,128)(2,1)S(1)}, u32[]{:S(2)}, u32[]{:S(2)}) collective-permute-start(bf16[128,512]{1,0:T(8,128)(2,1)S(1)} %add_convert_fusion.10.p0), channel_id=1, source_target_pairs={{0,8},{8,0},{16,24},{24,16},{1,9},{9,1},{17,25},{25,17},{2,10},{10... | collective-permute-start | bytes 393224 | tf_op jit(solution)/shard_map/ppermute | solution.py:585
  257.4 2.0 collective-permute-start.9
  261.9 7.3 %shard_map.261 = (f32[4,1,256,512]{3,2,1,0:T(8,128)}, f32[4,1,256,512]{3,2,1,0:T(8,128)}) custom-call(s32[4,8]{1,0:T(4,128)} %refs_0_.7, bf16[3,256,1536]{2,1,0:T(8,128)(2,1)} %get-tuple-element.124.refs_1_, bf16[512,1536]{1,0:T(8,128)(2,1)} %w_in.2, f32[1,512]{1,0:T(1,128)} %bitcast.241, ...), custom_call_target="tpu_custom_call", output_to_operand_aliasing={{0}: (8, {}), {1}: (9, {})} | custom-call | flops 1207959552 | bytes 11667456 | tf_op jit(solution)/shard_map/pallas_call | solution.py:478
  270.6 3.1 %shard_map.263 = (f32[1,64]{1,0:T(1,128)}, f32[64,2048]{1,0:T(8,128)}, f32[256,512]{1,0:T(8,128)}) custom-call(s32[3]{0:T(128)} %pad_add_fusion.refs_0_.ids, bf16[128,512]{1,0:T(8,128)(2,1)} %copy-done.6, bf16[128,512]{1,0:T(8,128)(2,1)} %copy-done.11, bf16[128,512]{1,0:T(8,128)(2,1)} %copy-done.12, bf16[128,512]{1,0:T(8,128)(2,1)} %copy-done.13, ...), custom_call_target="tpu_custom_call" | custom-call | tf_op jit(solution)/shard_map/pallas_call | solution.py:679
  275.0 2.7 shard_map.262
  (102 shorter events, 39.8 us)
Async XLA Ops:
  3.5 27.3 %all-to-all-start = ((bf16[8,3,32,512]{3,2,1,0:T(8,128)(2,1)}), bf16[8,3,32,512]{3,2,1,0:T(8,128)(2,1)S(1)}, u32[]{:S(2)}, u32[]{:S(2)}) async-start(bf16[8,3,32,512]{3,2,1,0:T(8,128)(2,1)} %shard_map.254.refs_8_), calls=%async_computation | async-start | bytes 1572864 | tf_op jit(solution)/shard_map/all_to_all | solution.py:752
  30.8 24.6 %all-to-all-start.1 = ((bf16[8,3,32,512]{3,2,1,0:T(8,128)(2,1)}), bf16[8,3,32,512]{3,2,1,0:T(8,128)(2,1)S(1)}, u32[]{:S(2)}, u32[]{:S(2)}) async-start(bf16[8,3,32,512]{3,2,1,0:T(8,128)(2,1)} %get-tuple-element.84.refs_15_), calls=%async_computation.1 | async-start | bytes 1572864 | tf_op jit(solution)/shard_map/all_to_all | solution.py:752
  96.9 24.8 %collective-permute-start = (bf16[4,4,192,512]{3,2,1,0:T(8,128)(2,1)}, bf16[4,4,192,512]{3,2,1,0:T(8,128)(2,1)S(1)}, u32[]{:S(2)}, u32[]{:S(2)}) collective-permute-start(bf16[4,4,192,512]{3,2,1,0:T(8,128)(2,1)} %get-tuple-element.114), channel_id=1, source_target_pairs={{0,1},{1,0},{2,3},{3,2},{4,5},{5,4},{6,7},{7,6},{8,9},{9,8},{10,11... | collective-permute-start | bytes 9437192 | tf_op jit(solution)/shard_map/ppermute | solution.py:585
  140.8 21.6 %collective-permute-start.23 = (bf16[4,192,512]{2,1,0:T(8,128)(2,1)}, bf16[4,192,512]{2,1,0:T(8,128)(2,1)S(1)}, u32[]{:S(2)}, u32[]{:S(2)}) collective-permute-start(bf16[4,192,512]{2,1,0:T(8,128)(2,1)} %get-tuple-element.149.refs_16_), channel_id=1, source_target_pairs={{0,24},{8,16},{16,8},{24,0},{1,25},{9,17},{17,9},{25,1},{2,26},{10... | collective-permute-start | bytes 2359304 | tf_op jit(solution)/shard_map/ppermute | solution.py:585
  143.3 35.5 %collective-permute-start.22 = (bf16[4,192,512]{2,1,0:T(8,128)(2,1)}, bf16[4,192,512]{2,1,0:T(8,128)(2,1)}, u32[]{:S(2)}, u32[]{:S(2)}) collective-permute-start(bf16[4,192,512]{2,1,0:T(8,128)(2,1)} %get-tuple-element.150.refs_15_), channel_id=1, source_target_pairs={{0,16},{8,24},{16,0},{24,8},{1,17},{9,25},{17,1},{25,9},{2,18},{10... | collective-permute-start | bytes 2359304 | tf_op jit(solution)/shard_map/ppermute | solution.py:585
  143.8 35.1 %collective-permute-start.21 = (bf16[4,192,512]{2,1,0:T(8,128)(2,1)}, bf16[4,192,512]{2,1,0:T(8,128)(2,1)}, u32[]{:S(2)}, u32[]{:S(2)}) collective-permute-start(bf16[4,192,512]{2,1,0:T(8,128)(2,1)} %get-tuple-element.151.refs_14_), channel_id=1, source_target_pairs={{0,8},{8,0},{16,24},{24,16},{1,9},{9,1},{17,25},{25,17},{2,10},{10... | collective-permute-start | bytes 2359304 | tf_op jit(solution)/shard_map/ppermute | solution.py:585
  158.9 59.5 %collective-permute-start.2 = (bf16[4,4,64,512]{3,2,1,0:T(8,128)(2,1)}, bf16[4,4,64,512]{3,2,1,0:T(8,128)(2,1)}, u32[]{:S(2)}, u32[]{:S(2)}) collective-permute-start(bf16[4,4,64,512]{3,2,1,0:T(8,128)(2,1)} %get-tuple-element.133), channel_id=1, source_target_pairs={{0,1},{1,0},{2,3},{3,2},{4,5},{5,4},{6,7},{7,6},{8,9},{9,8},{10,11... | collective-permute-start | bytes 3145736 | tf_op jit(solution)/shard_map/ppermute | solution.py:585
  180.8 9.7 %collective-permute-start.26 = (bf16[192,512]{1,0:T(8,128)(2,1)S(1)}, bf16[192,512]{1,0:T(8,128)(2,1)S(1)}, u32[]{:S(2)}, u32[]{:S(2)}) collective-permute-start(bf16[192,512]{1,0:T(8,128)(2,1)S(1)} %get-tuple-element.147), channel_id=1, source_target_pairs={{0,6},{1,7},{2,4},{3,5},{4,2},{5,3},{6,0},{7,1},{8,14},{9,15},{10,... | collective-permute-start | bytes 589832 | tf_op jit(solution)/shard_map/ppermute | solution.py:585
  182.1 17.2 %collective-permute-start.25 = (bf16[192,512]{1,0:T(8,128)(2,1)S(1)}, bf16[192,512]{1,0:T(8,128)(2,1)S(1)}, u32[]{:S(2)}, u32[]{:S(2)}) collective-permute-start(bf16[192,512]{1,0:T(8,128)(2,1)S(1)} %get-tuple-element.148), channel_id=1, source_target_pairs={{0,4},{1,5},{2,6},{3,7},{4,0},{5,1},{6,2},{7,3},{8,12},{9,13},{10,... | collective-permute-start | bytes 589832 | tf_op jit(solution)/shard_map/ppermute | solution.py:585
  182.1 18.7 %collective-permute-start.24 = (bf16[192,512]{1,0:T(8,128)(2,1)S(1)}, bf16[192,512]{1,0:T(8,128)(2,1)S(1)}, u32[]{:S(2)}, u32[]{:S(2)}) collective-permute-start(bf16[192,512]{1,0:T(8,128)(2,1)S(1)} %get-tuple-element.146), channel_id=1, source_target_pairs={{0,2},{1,3},{2,0},{3,1},{4,6},{5,7},{6,4},{7,5},{8,10},{9,11},{10,... | collective-permute-start | bytes 589832 | tf_op jit(solution)/shard_map/ppermute | solution.py:585
  185.2 43.7 %collective-permute-start.14 = (bf16[4,128,512]{2,1,0:T(8,128)(2,1)}, bf16[4,128,512]{2,1,0:T(8,128)(2,1)}, u32[]{:S(2)}, u32[]{:S(2)}) collective-permute-start(bf16[4,128,512]{2,1,0:T(8,128)(2,1)} %get-tuple-element.155.refs_13_), channel_id=1, source_target_pairs={{0,24},{8,16},{16,8},{24,0},{1,25},{9,17},{17,9},{25,1},{2,26},{10... | collective-permute-start | bytes 1572872 | tf_op jit(solution)/shard_map/ppermute | solution.py:585
  190.5 45.4 %collective-permute-start.13 = (bf16[4,128,512]{2,1,0:T(8,128)(2,1)}, bf16[4,128,512]{2,1,0:T(8,128)(2,1)}, u32[]{:S(2)}, u32[]{:S(2)}) collective-permute-start(bf16[4,128,512]{2,1,0:T(8,128)(2,1)} %get-tuple-element.156.refs_12_), channel_id=1, source_target_pairs={{0,16},{8,24},{16,0},{24,8},{1,17},{9,25},{17,1},{25,9},{2,18},{10... | collective-permute-start | bytes 1572872 | tf_op jit(solution)/shard_map/ppermute | solution.py:585
  199.3 36.6 %collective-permute-start.12 = (bf16[4,128,512]{2,1,0:T(8,128)(2,1)}, bf16[4,128,512]{2,1,0:T(8,128)(2,1)}, u32[]{:S(2)}, u32[]{:S(2)}) collective-permute-start(bf16[4,128,512]{2,1,0:T(8,128)(2,1)} %get-tuple-element.157.refs_11_), channel_id=1, source_target_pairs={{0,8},{8,0},{16,24},{24,16},{1,9},{9,1},{17,25},{25,17},{2,10},{10... | collective-permute-start | bytes 1572872 | tf_op jit(solution)/shard_map/ppermute | solution.py:585
  202.2 14.6 %collective-permute-start.27 = (bf16[192,512]{1,0:T(8,128)(2,1)S(1)}, bf16[192,512]{1,0:T(8,128)(2,1)S(1)}, u32[]{:S(2)}, u32[]{:S(2)}) collective-permute-start(bf16[192,512]{1,0:T(8,128)(2,1)S(1)} %add_convert_fusion.9.p0), channel_id=1, source_target_pairs={{0,8},{8,0},{16,24},{24,16},{1,9},{9,1},{17,25},{25,17},{2,10},{10... | collective-permute-start | bytes 589832 | tf_op jit(solution)/shard_map/ppermute | solution.py:585
  202.8 58.2 %all-to-all-start.3 = ((bf16[8,3,32,512]{3,2,1,0:T(8,128)(2,1)}), bf16[8,3,32,512]{3,2,1,0:T(8,128)(2,1)S(1)}, u32[]{:S(2)}, u32[]{:S(2)}) async-start(bf16[8,3,32,512]{3,2,1,0:T(8,128)(2,1)} %get-tuple-element.127), calls=%async_computation.3 | async-start | bytes 1572864 | tf_op jit(solution)/shard_map/all_to_all | solution.py:752
  216.8 9.5 %collective-permute-start.28 = (bf16[192,512]{1,0:T(8,128)(2,1)S(1)}, bf16[192,512]{1,0:T(8,128)(2,1)S(1)}, u32[]{:S(2)}, u32[]{:S(2)}) collective-permute-start(bf16[192,512]{1,0:T(8,128)(2,1)S(1)} %add_convert_fusion.9.p0), channel_id=1, source_target_pairs={{0,16},{8,24},{16,0},{24,8},{1,17},{9,25},{17,1},{25,9},{2,18},{10... | collective-permute-start | bytes 589832 | tf_op jit(solution)/shard_map/ppermute | solution.py:585
  218.4 9.2 %collective-permute-start.29 = (bf16[192,512]{1,0:T(8,128)(2,1)S(1)}, bf16[192,512]{1,0:T(8,128)(2,1)S(1)}, u32[]{:S(2)}, u32[]{:S(2)}) collective-permute-start(bf16[192,512]{1,0:T(8,128)(2,1)S(1)} %add_convert_fusion.9.p0), channel_id=1, source_target_pairs={{0,24},{8,16},{16,8},{24,0},{1,25},{9,17},{17,9},{25,1},{2,26},{10... | collective-permute-start | bytes 589832 | tf_op jit(solution)/shard_map/ppermute | solution.py:585
  226.3 13.0 %collective-permute-start.5 = (bf16[4,64,512]{2,1,0:T(8,128)(2,1)S(1)}, bf16[4,64,512]{2,1,0:T(8,128)(2,1)S(1)}, u32[]{:S(2)}, u32[]{:S(2)}) collective-permute-start(bf16[4,64,512]{2,1,0:T(8,128)(2,1)S(1)} %get-tuple-element.162), channel_id=1, source_target_pairs={{0,24},{8,16},{16,8},{24,0},{1,25},{9,17},{17,9},{25,1},{2,26},{10... | collective-permute-start | bytes 786440 | tf_op jit(solution)/shard_map/ppermute | solution.py:585
  227.6 14.6 %collective-permute-start.4 = (bf16[4,64,512]{2,1,0:T(8,128)(2,1)S(1)}, bf16[4,64,512]{2,1,0:T(8,128)(2,1)S(1)}, u32[]{:S(2)}, u32[]{:S(2)}) collective-permute-start(bf16[4,64,512]{2,1,0:T(8,128)(2,1)S(1)} %get-tuple-element.163), channel_id=1, source_target_pairs={{0,16},{8,24},{16,0},{24,8},{1,17},{9,25},{17,1},{25,9},{2,18},{10... | collective-permute-start | bytes 786440 | tf_op jit(solution)/shard_map/ppermute | solution.py:585
  229.0 13.3 %collective-permute-start.3 = (bf16[4,64,512]{2,1,0:T(8,128)(2,1)S(1)}, bf16[4,64,512]{2,1,0:T(8,128)(2,1)S(1)}, u32[]{:S(2)}, u32[]{:S(2)}) collective-permute-start(bf16[4,64,512]{2,1,0:T(8,128)(2,1)S(1)} %get-tuple-element.161), channel_id=1, source_target_pairs={{0,8},{8,0},{16,24},{24,16},{1,9},{9,1},{17,25},{25,17},{2,10},{10... | collective-permute-start | bytes 786440 | tf_op jit(solution)/shard_map/ppermute | solution.py:585
  237.8 8.4 %collective-permute-start.17 = (bf16[128,512]{1,0:T(8,128)(2,1)S(1)}, bf16[128,512]{1,0:T(8,128)(2,1)S(1)}, u32[]{:S(2)}, u32[]{:S(2)}) collective-permute-start(bf16[128,512]{1,0:T(8,128)(2,1)S(1)} %get-tuple-element.153), channel_id=1, source_target_pairs={{0,6},{1,7},{2,4},{3,5},{4,2},{5,3},{6,0},{7,1},{8,14},{9,15},{10,... | collective-permute-start | bytes 393224 | tf_op jit(solution)/shard_map/ppermute | solution.py:585
  239.3 11.6 %collective-permute-start.16 = (bf16[128,512]{1,0:T(8,128)(2,1)S(1)}, bf16[128,512]{1,0:T(8,128)(2,1)S(1)}, u32[]{:S(2)}, u32[]{:S(2)}) collective-permute-start(bf16[128,512]{1,0:T(8,128)(2,1)S(1)} %get-tuple-element.154), channel_id=1, source_target_pairs={{0,4},{1,5},{2,6},{3,7},{4,0},{5,1},{6,2},{7,3},{8,12},{9,13},{10,... | collective-permute-start | bytes 393224 | tf_op jit(solution)/shard_map/ppermute | solution.py:585
  239.3 11.5 %collective-permute-start.15 = (bf16[128,512]{1,0:T(8,128)(2,1)S(1)}, bf16[128,512]{1,0:T(8,128)(2,1)S(1)}, u32[]{:S(2)}, u32[]{:S(2)}) collective-permute-start(bf16[128,512]{1,0:T(8,128)(2,1)S(1)} %get-tuple-element.152), channel_id=1, source_target_pairs={{0,2},{1,3},{2,0},{3,1},{4,6},{5,7},{6,4},{7,5},{8,10},{9,11},{10,... | collective-permute-start | bytes 393224 | tf_op jit(solution)/shard_map/ppermute | solution.py:585
  243.4 11.5 %collective-permute-start.8 = (bf16[64,512]{1,0:T(8,128)(2,1)S(1)}, bf16[64,512]{1,0:T(8,128)(2,1)S(1)}, u32[]{:S(2)}, u32[]{:S(2)}) collective-permute-start(bf16[64,512]{1,0:T(8,128)(2,1)S(1)} %get-tuple-element.159), channel_id=1, source_target_pairs={{0,6},{1,7},{2,4},{3,5},{4,2},{5,3},{6,0},{7,1},{8,14},{9,15},{10,... | collective-permute-start | bytes 196616 | tf_op jit(solution)/shard_map/ppermute | solution.py:585
  244.9 11.6 %collective-permute-start.7 = (bf16[64,512]{1,0:T(8,128)(2,1)S(1)}, bf16[64,512]{1,0:T(8,128)(2,1)S(1)}, u32[]{:S(2)}, u32[]{:S(2)}) collective-permute-start(bf16[64,512]{1,0:T(8,128)(2,1)S(1)} %get-tuple-element.160), channel_id=1, source_target_pairs={{0,4},{1,5},{2,6},{3,7},{4,0},{5,1},{6,2},{7,3},{8,12},{9,13},{10,... | collective-permute-start | bytes 196616 | tf_op jit(solution)/shard_map/ppermute | solution.py:585
  246.2 10.3 %collective-permute-start.6 = (bf16[64,512]{1,0:T(8,128)(2,1)S(1)}, bf16[64,512]{1,0:T(8,128)(2,1)S(1)}, u32[]{:S(2)}, u32[]{:S(2)}) collective-permute-start(bf16[64,512]{1,0:T(8,128)(2,1)S(1)} %get-tuple-element.158), channel_id=1, source_target_pairs={{0,2},{1,3},{2,0},{3,1},{4,6},{5,7},{6,4},{7,5},{8,10},{9,11},{10,... | collective-permute-start | bytes 196616 | tf_op jit(solution)/shard_map/ppermute | solution.py:585
  252.2 7.3 %collective-permute-start.18 = (bf16[128,512]{1,0:T(8,128)(2,1)S(1)}, bf16[128,512]{1,0:T(8,128)(2,1)S(1)}, u32[]{:S(2)}, u32[]{:S(2)}) collective-permute-start(bf16[128,512]{1,0:T(8,128)(2,1)S(1)} %add_convert_fusion.10.p0), channel_id=1, source_target_pairs={{0,8},{8,0},{16,24},{24,16},{1,9},{9,1},{17,25},{25,17},{2,10},{10... | collective-permute-start | bytes 393224 | tf_op jit(solution)/shard_map/ppermute | solution.py:585
  254.9 14.3 %collective-permute-start.19 = (bf16[128,512]{1,0:T(8,128)(2,1)S(1)}, bf16[128,512]{1,0:T(8,128)(2,1)S(1)}, u32[]{:S(2)}, u32[]{:S(2)}) collective-permute-start(bf16[128,512]{1,0:T(8,128)(2,1)S(1)} %add_convert_fusion.10.p0), channel_id=1, source_target_pairs={{0,16},{8,24},{16,0},{24,8},{1,17},{9,25},{17,1},{25,9},{2,18},{10... | collective-permute-start | bytes 393224 | tf_op jit(solution)/shard_map/ppermute | solution.py:585
  254.9 14.4 %collective-permute-start.20 = (bf16[128,512]{1,0:T(8,128)(2,1)S(1)}, bf16[128,512]{1,0:T(8,128)(2,1)S(1)}, u32[]{:S(2)}, u32[]{:S(2)}) collective-permute-start(bf16[128,512]{1,0:T(8,128)(2,1)S(1)} %add_convert_fusion.10.p0), channel_id=1, source_target_pairs={{0,24},{8,16},{16,8},{24,0},{1,25},{9,17},{17,9},{25,1},{2,26},{10... | collective-permute-start | bytes 393224 | tf_op jit(solution)/shard_map/ppermute | solution.py:585
  257.4 16.2 %collective-permute-start.9 = (bf16[64,512]{1,0:T(8,128)(2,1)S(1)}, bf16[64,512]{1,0:T(8,128)(2,1)S(1)}, u32[]{:S(2)}, u32[]{:S(2)}) collective-permute-start(bf16[64,512]{1,0:T(8,128)(2,1)S(1)} %add_convert_fusion.11.p0), channel_id=1, source_target_pairs={{0,8},{8,0},{16,24},{24,16},{1,9},{9,1},{17,25},{25,17},{2,10},{10... | collective-permute-start | bytes 196616 | tf_op jit(solution)/shard_map/ppermute | solution.py:585
  259.5 14.2 %collective-permute-start.10 = (bf16[64,512]{1,0:T(8,128)(2,1)S(1)}, bf16[64,512]{1,0:T(8,128)(2,1)S(1)}, u32[]{:S(2)}, u32[]{:S(2)}) collective-permute-start(bf16[64,512]{1,0:T(8,128)(2,1)S(1)} %add_convert_fusion.11.p0), channel_id=1, source_target_pairs={{0,16},{8,24},{16,0},{24,8},{1,17},{9,25},{17,1},{25,9},{2,18},{10... | collective-permute-start | bytes 196616 | tf_op jit(solution)/shard_map/ppermute | solution.py:585
  259.5 14.3 %collective-permute-start.11 = (bf16[64,512]{1,0:T(8,128)(2,1)S(1)}, bf16[64,512]{1,0:T(8,128)(2,1)S(1)}, u32[]{:S(2)}, u32[]{:S(2)}) collective-permute-start(bf16[64,512]{1,0:T(8,128)(2,1)S(1)} %add_convert_fusion.11.p0), channel_id=1, source_target_pairs={{0,24},{8,16},{16,8},{24,0},{1,25},{9,17},{17,9},{25,1},{2,26},{10... | collective-permute-start | bytes 196616 | tf_op jit(solution)/shard_map/ppermute | solution.py:585
  (22 other events, 264.6 us)

commit v3 on v2

--- a/solution.py
+++ b/solution.py
@@ -15,7 +15,9 @@
 F32 = jnp.float32
 CHUNK = 512
 LANES = 128
+COST = 1
 VMEM = 60 * 1024 * 1024
+SMALL_VMEM = 24 * 1024 * 1024
 
 
 def nn(a, b):
@@ -287,8 +289,7 @@
     input_grad[0, 0] = g1 + unit_backward(gn * gain[...], sz0[...].astype(F32), inv0[:, :1])
 
 
-def space_back_in(labels, gqkv, w_in, gain, z0, inv0, g1, moved, *rest):
-    input_grad, result = rest[-2:]
+def space_back_in(labels, gqkv, w_in, gain, z0, inv0, g1, moved, input_grad, result):
     gn = nt(gqkv[0], w_in[...])
     grad = unit_backward(gn * gain[...], z0[0].astype(F32), inv0[0, :, :1])
     input_grad[0, 0] = g1[0] + grad
@@ -318,95 +319,64 @@
         copy.wait()
 
 
-def space_feed_kernel(
-    hierarchical, ids, scale, inv1, g2_in, slope_in, z1_in, w_out_in, w_up_in, w_down_in, h_in, z1_one, h_one, eu_one, e2_one, *rest
-):
-    outs, scratch = rest[: 5], rest[5:]
-    e1_out, go_out, g1_out = outs[:3]
-    g2, slope, z1, w_out, w_up, w_down, h, eu, e2, e1, go, g1 = scratch[:12]
+def space_kernel(hierarchical, ids, scale, inv1, *rest):
+    (g2_in, slope_in, z1_in, w_out_in, w_up_in, w_down_in, qkv_in, p_in), rest = rest[:8], rest[8:]
+    shared, one, rest = rest[:3], rest[3:11], rest[11:]
+    (g1_out, gqkv_out), outs, scratch = rest[:2], rest[2 : 6 if hierarchical else 5], rest[6 if hierarchical else 5 :]
+    g2, slope, w_out, w_up, w_down, qkv, p, go, g1, gp, gs = scratch[:11]
+    z1, eu, h, e2, z0, gqkv, o, e1 = whole = scratch[11:19]
     copies = Copies(scratch[-1])
-    packs, tokens, _ = e1.shape
+    packs, tokens, _ = g1.shape
     have = packs * tokens
     got_g2 = copies.fetch(g2_in, g2)
-    got_down = [
-        copies.fetch(w_down_in.at[pl.ds(at, CHUNK)], w_down.at[pl.ds(at, CHUNK)])
-        for at in range(0, w_down.shape[0], CHUNK)
-    ]
+    got_down = copies.fetch(w_down_in, w_down)
     got_slope = [copies.fetch(slope_in.at[pack], slope.at[pack]) for pack in range(packs)]
     got_up = copies.fetch(w_up_in, w_up)
     got_z1 = [
         copies.fetch(z1_in.at[pack], z1.at[pl.ds(pack * tokens, tokens)]) for pack in range(packs)
     ]
     got_out = copies.fetch(w_out_in, w_out)
+    got_attend = [
+        (copies.fetch(qkv_in.at[pack], qkv.at[pack]), copies.fetch(p_in.at[pack], p.at[pack]))
+        for pack in range(packs)
+    ]
+    got_rest = []
     if hierarchical:
-        got_rest = [
-            copies.fetch(z1_one.at[0], z1.at[pl.ds(have, tokens)]),
-            copies.fetch(eu_one.at[0], eu.at[pl.ds(have, tokens)]),
-            copies.fetch(e2_one.at[0], e2.at[pl.ds(have, tokens)]),
-            copies.fetch(h_one.at[0], h.at[pl.ds(have, tokens)]),
-        ] + [
-            copies.fetch(h_in.at[pack], h.at[pl.ds(pack * tokens, tokens)]) for pack in range(packs)
-        ]
+        for source, target in zip(shared, (h, z0, o)):
+            for pack in range(packs):
+                rows = pl.ds(pack * tokens, tokens)
+                got_rest.append(copies.fetch(source.at[pack], target.at[rows]))
+        for source, target in zip(one, whole):
+            got_rest.append(copies.fetch(source.at[0], target.at[pl.ds(have, tokens)]))
     wait(got_g2)
     for pack in range(packs):
         rows = slice(pack * tokens, (pack + 1) * tokens)
         e2[rows] = rows_of(g2[:, pack : pack + 1]).astype(BF)
         wait(got_slope[pack])
         if pack == 0:
-            wait(*got_down, got_up)
+            wait(got_down, got_up)
         gm = feed_back(e2[rows], w_up, w_down, slope.at[pack], eu.at[rows])
         if pack == 0:
             wait(*got_z1, got_out)
         grad = unit_backward(gm * scale[...], z1[rows].astype(F32), inv1[pack, :, :1])
         total = rows_of(g2[:, pack : pack + 1]) + grad
         g1[pack] = total
-        e1[pack] = total.astype(BF)
-        go[pack] = nt(e1[pack], w_out[...]).astype(BF)
+        e1[rows] = total.astype(BF)
+        go[pack] = nt(e1[rows], w_out[...]).astype(BF)
         copies.send(g1.at[pack], g1_out.at[pack])
-        copies.send(e1.at[pack], e1_out.at[pack])
-        copies.send(go.at[pack], go_out.at[pack])
+    for pack in range(packs):
+        wait(*got_attend[pack])
+        rows = pl.ds(pack * tokens, tokens)
+        attend_backward(qkv.at[pack], p.at[pack], go.at[pack], gqkv.at[rows], gp, gs)
+        copies.send(gqkv.at[rows], gqkv_out.at[pack])
     if hierarchical:
         wait(*got_rest)
-        feed_tiles(copies, ids, z1, e2, eu, h, 0, scratch[12:14], outs[3:])
+        feed_tiles(Halves(copies, ids, scratch[19:21], outs[:2]), z1, e2, eu, h, 0)
+        place = Halves(copies, ids, scratch[21:23], outs[2:])
+        attend_tiles(place, z0, o, gqkv, e1, 0, gqkv.shape[0])
     else:
-        copies.send(eu, outs[3])
-        copies.send(e2, outs[4])
-    copies.finish()
-
-
-def space_attend_kernel(
-    hierarchical, ids, qkv_in, p_in, go_in, z0_in, o_in, e1_in, z0_one, o_one, e1_one, gqkv_one, *rest
-):
-    outs, scratch = rest[: 3 if hierarchical else 1], rest[3 if hierarchical else 1 :]
-    qkv, p, go, z0, o, e1, gqkv, gp, gs = scratch[:9]
-    copies = Copies(scratch[-1])
-    packs, tokens, _ = qkv.shape
-    have = packs * tokens
-    got = [
-        [
-            copies.fetch(qkv_in.at[pack], qkv.at[pack]),
-            copies.fetch(go_in.at[pack], go.at[pack]),
-            copies.fetch(p_in.at[pack], p.at[pack]),
-        ]
-        for pack in range(packs)
-    ]
-    if hierarchical:
-        pairs = (z0_in, z0_one, z0), (o_in, o_one, o), (e1_in, e1_one, e1)
-        got_rest = [
-            copies.fetch(source.at[pack], target.at[pl.ds(pack * tokens, tokens)])
-            for source, _, target in pairs
-            for pack in range(packs)
-        ]
-        got_rest += [copies.fetch(one.at[0], target.at[pl.ds(have, tokens)]) for _, one, target in pairs]
-        got_rest.append(copies.fetch(gqkv_one.at[0], gqkv.at[pl.ds(have, tokens)]))
-    for pack in range(packs):
-        wait(*got[pack])
-        rows = pl.ds(pack * tokens, tokens)
-        attend_backward(qkv.at[pack], p.at[pack], go.at[pack], gqkv.at[rows], gp, gs)
-        copies.send(gqkv.at[rows], outs[0].at[pack])
-    if hierarchical:
-        wait(*got_rest)
-        attend_tiles(copies, ids, z0, o, gqkv, e1, 0, scratch[9:11], outs[1:], gqkv.shape[0])
+        for source, target in zip((eu, e2, e1), outs):
+            copies.send(source, target)
     copies.finish()
 
 
@@ -490,38 +460,51 @@
                 vmem_limit_bytes=VMEM, dimension_semantics=("arbitrary",)
             ),
             cost_estimate=pl.CostEstimate(
-                flops=int(flops * self.count), bytes_accessed=int(moved), transcendentals=0
+                flops=int(flops * self.count * COST), bytes_accessed=int(moved * COST), transcendentals=0
             ),
         )(*scalars, *operands)
 
 
-def feed_tiles(copies, ids, z1, e2, eu, h, at, held, outs):
-    first = ids[0] == 0
+class Halves:
+    def __init__(self, copies, ids, held, outs, z_first=False):
+        self.copies, self.held, self.outs = copies, held, outs
+        self.first, self.z, self.s, self.z_first = ids[0] == 0, ids[1], ids[2], z_first
+
+    def at(self, s, z):
+        s = slice(None) if s is None else s ^ self.s
+        z = slice(None) if z is None else z ^ self.z
+        return (z, s) if self.z_first else (s, z)
+
+    def put(self, s, z, at, even, odd):
+        rows = slice(at, at + even.shape[0])
+        self.held[0][*self.at(s, z), rows] = jnp.where(self.first, even, odd)
+        self.held[1][*self.at(s, z), rows] = jnp.where(self.first, odd, even)
+
+    def send(self, s, z, at):
+        for ref, out in zip(self.held, self.outs):
+            index = *self.at(s, z), pl.ds(at, 64)
+            self.copies.send(ref.at[index], out.at[index])
+
+
+def feed_tiles(place, z1, e2, eu, h, at):
     for step in range(4):
         tile = tn(z1[...], eu[:, step * CHUNK : (step + 1) * CHUNK]).astype(BF)
-        s = step ^ ids[2]
         for z in range(4):
-            even, odd = tile[128 * z : 128 * z + 64], tile[128 * z + 64 : 128 * z + 128]
-            held[0][s, z ^ ids[1], at : at + 64] = jnp.where(first, even, odd)
-            held[1][s, z ^ ids[1], at : at + 64] = jnp.where(first, odd, even)
-        for ref, out in zip(held, outs):
-            copies.send(ref.at[s, :, pl.ds(at, 64)], out.at[s, :, pl.ds(at, 64)])
+            row = 128 * z
+            place.put(step, z, at, tile[row : row + 64], tile[row + 64 : row + 128])
+        place.send(step, None, at)
     at = at + 64
     for step in range(4):
         tile = tn(e2[...], h[:, step * CHUNK : (step + 1) * CHUNK]).astype(BF)
-        z = step ^ ids[1]
         for s in range(4):
             upper, lower = tile[128 * s : 128 * s + 64], tile[128 * s + 64 : 128 * s + 128]
             even = jnp.concatenate([upper[:, :256], lower[:, :256]], axis=1)
             odd = jnp.concatenate([upper[:, 256:], lower[:, 256:]], axis=1)
-            held[0][s ^ ids[2], z, at : at + 64] = jnp.where(first, even, odd)
-            held[1][s ^ ids[2], z, at : at + 64] = jnp.where(first, odd, even)
-        for ref, out in zip(held, outs):
-            copies.send(ref.at[:, z, pl.ds(at, 64)], out.at[:, z, pl.ds(at, 64)])
-
-
-def attend_tiles(copies, ids, z0, o, gqkv, e1, at, held, outs, depth):
-    first = ids[0] == 0
+            place.put(s, step, at, even, odd)
+        place.send(None, step, at)
+
+
+def attend_tiles(place, z0, o, gqkv, e1, at, depth):
     for step in range(4):
         if step == 3:
             tile = tn(o[...], e1[...])
@@ -529,22 +512,20 @@
             rows = gqkv.shape[0] if step == 2 else depth
             tile = tn(z0[:rows], gqkv[:rows, step * CHUNK : (step + 1) * CHUNK])
         tile = tile.astype(BF)
-        here = at + 16 * step
         for z in range(4):
             for s in range(4):
                 row = 128 * z + 16 * s
                 even, odd = tile[row : row + 16], tile[row + 64 : row + 80]
-                held[0][s ^ ids[2], z ^ ids[1], here : here + 16] = jnp.where(first, even, odd)
-                held[1][s ^ ids[2], z ^ ids[1], here : here + 16] = jnp.where(first, odd, even)
-    for ref, out in zip(held, outs):
-        copies.send(ref.at[:, :, pl.ds(at, 64)], out.at[:, :, pl.ds(at, 64)])
+                place.put(s, z, at + 16 * step, even, odd)
+    place.send(None, None, at)
 
 
 def time_weights_kernel(ids, *rest):
     names = 8
     shared, one, outs, scratch = rest[:names], rest[names : 2 * names], rest[16:18], rest[18:]
     z1, eu, e2, h, z0, gqkv, o, e1 = scratch[:names]
-    held, copies = scratch[8:10], Copies(scratch[-1])
+    copies = Copies(scratch[-1])
+    place = Halves(copies, ids, scratch[8:10], outs)
     packs, tokens, _ = shared[0].shape
     have = packs * tokens
     got = []
@@ -557,9 +538,9 @@
             + [copies.fetch(single.at[0], wide_target)]
         )
     wait(*got[0], *got[1], *got[2], *got[3])
-    feed_tiles(copies, ids, z1, e2, eu, h, 0, held, outs)
+    feed_tiles(place, z1, e2, eu, h, 0)
     wait(*got[4], *got[5], *got[6], *got[7])
-    attend_tiles(copies, ids, z0, o, gqkv, e1, 128, held, outs, have)
+    attend_tiles(place, z0, o, gqkv, e1, 128, have)
     copies.finish()
 
 
@@ -576,7 +557,7 @@
         + [pltpu.SemaphoreType.DMA((semaphores,))],
         compiler_params=pltpu.CompilerParams(vmem_limit_bytes=VMEM),
         cost_estimate=pl.CostEstimate(
-            flops=int(flops), bytes_accessed=sum(a.size * 2 for a in args), transcendentals=0
+            flops=int(flops * COST), bytes_accessed=0, transcendentals=0
         ),
     )(ids, *args, *after)
 
@@ -592,25 +573,131 @@
     return total.astype(BF)
 
 
-def core_sum(mine, other):
-    got = swap(other, "tm", 8, 1)
-    return [add(mine[d], got[d]) for d in range(1, 4)], (mine[0], got[0])
-
-
-def rest_sum(parts, own):
+def core_sum(mine, got, *note):
+    return [add(mine[d], got[d], *note) for d in range(1, 4)], (mine[0], got[0])
+
+
+def stream_total(parts, own):
+    return add(*own, *[swap(part, "stream", 4, d + 1) for d, part in enumerate(parts)])
+
+
+def stream_sum(parts, own):
     got = [swap(part, "stream", 4, d + 1) for d, part in enumerate(parts)]
-    rows = [add(*[term[d] for term in (*own, *got)]) for d in range(4)]
-    got = [swap(rows[d], "tm", 8, 2 * d) for d in range(1, 4)]
-    final = add(rows[0], *got)
+    return [add(*[term[d] for term in (*own, *got)]) for d in range(4)]
+
+
+def z_sum(rows):
+    return add(rows[0], *[swap(rows[d], "tm", 8, 2 * d) for d in range(1, 4)])
+
+
+def gather_parts(final):
     return [final] + [swap(final, "stream", 4, d) for d in range(1, 4)]
 
 
-def column(row):
-    size = row.shape[1]
-    eye = lax.broadcasted_iota(jnp.int32, (size, size), 0) == lax.broadcasted_iota(
-        jnp.int32, (size, size), 1
+def marker(array):
+    def kernel(source, out):
+        out[...] = jnp.zeros_like(out)
+
+    return pl.pallas_call(
+        kernel,
+        out_shape=jax.ShapeDtypeStruct((1, CHUNK), F32),
+        in_specs=[pl.BlockSpec(memory_space=pl.ANY)],
+        out_specs=pl.BlockSpec(memory_space=pltpu.VMEM),
+        cost_estimate=pl.CostEstimate(flops=10**12, bytes_accessed=10**8, transcendentals=0),
+    )(array)
+
+
+def z_scatter(rows):
+    groups = [[0, 2, 4, 6], [1, 3, 5, 7]]
+    got = lax.all_to_all(
+        rows, "tm", split_axis=0, concat_axis=0, tiled=True, axis_index_groups=groups
     )
-    return jnp.sum(jnp.where(eye, row, 0.0), axis=1, keepdims=True)
+    return add(*[got[z] for z in range(4)])
+
+
+def stream_total(parts, own):
+    return add(*own, *[swap(part, "stream", 4, d + 1) for d, part in enumerate(parts)])
+
+
+def stream_sum(parts, own):
+    got = [swap(part, "stream", 4, d + 1) for d, part in enumerate(parts)]
+    return [add(*[term[d] for term in (*own, *got)]) for d in range(4)]
+
+
+def z_sum(rows):
+    return add(rows[0], *[swap(rows[d], "tm", 8, 2 * d) for d in range(1, 4)])
+
+
+def gather_parts(final):
+    return [final] + [swap(final, "stream", 4, d) for d in range(1, 4)]
+
+
+def marker(array):
+    def kernel(source, out):
+        out[...] = jnp.zeros_like(out)
+
+    return pl.pallas_call(
+        kernel,
+        out_shape=jax.ShapeDtypeStruct((1, CHUNK), F32),
+        in_specs=[pl.BlockSpec(memory_space=pl.ANY)],
+        out_specs=pl.BlockSpec(memory_space=pltpu.VMEM),
+        cost_estimate=pl.CostEstimate(flops=10**12, bytes_accessed=10**8, transcendentals=0),
+    )(array)
+
+
+def stream_total(parts, own):
+    return add(*own, *[swap(part, "stream", 4, d + 1) for d, part in enumerate(parts)])
+
+
+def stream_total(parts, own):
+    return add(*own, *[swap(part, "stream", 4, d + 1) for d, part in enumerate(parts)])
+
+
+def stream_sum(parts, own):
+    got = [swap(part, "stream", 4, d + 1) for d, part in enumerate(parts)]
+    return [add(*[term[d] for term in (*own, *got)]) for d in range(4)]
+
+
+def z_sum(rows):
+    return add(rows[0], *[swap(rows[d], "tm", 8, 2 * d) for d in range(1, 4)])
+
+
+def gather_parts(final):
+    return [final] + [swap(final, "stream", 4, d) for d in range(1, 4)]
+
+
+def marker(array):
+    def kernel(source, out):
+        out[...] = jnp.zeros_like(out)
+
+    return pl.pallas_call(
+        kernel,
+        out_shape=jax.ShapeDtypeStruct((1, CHUNK), F32),
+        in_specs=[pl.BlockSpec(memory_space=pl.ANY)],
+        out_specs=pl.BlockSpec(memory_space=pltpu.VMEM),
+        cost_estimate=pl.CostEstimate(flops=10**12, bytes_accessed=10**8, transcendentals=0),
+    )(array)
+
+
+def add_call(mine, got, after):
+    def kernel(a, b, out):
+        out[...] = (a[...].astype(F32) + b[...].astype(F32)).astype(BF)
+
+    block = pl.BlockSpec((1,) + mine.shape[1:], lambda i: (i,) + (0,) * (mine.ndim - 1))
+    return pl.pallas_call(
+        without(kernel, 2, len(after)),
+        out_shape=jax.ShapeDtypeStruct(mine.shape, BF),
+        grid=(mine.shape[0],),
+        in_specs=[block, block] + [pl.BlockSpec(memory_space=pl.ANY)] * len(after),
+        out_specs=block,
+        compiler_params=pltpu.CompilerParams(vmem_limit_bytes=VMEM),
+    )(mine, got, *after)
+
+
+def scatter_sum(total):
+    share = lax.psum_scatter(total, "stream", scatter_dimension=0)
+    groups = [[0, 2, 4, 6], [1, 3, 5, 7]]
+    return lax.psum_scatter(share, "tm", scatter_dimension=0, axis_index_groups=groups)
 
 
 def as_row(col):
@@ -622,8 +709,10 @@
 
 
 def own_rows(ids, vector):
-    rank = 2 * ids[1] + ids[0]
-    return column(vector[pl.ds(rank, 1), :])
+    shape = 64, vector.shape[1]
+    row = lax.broadcasted_iota(jnp.int32, shape, 0) + 64 * (2 * ids[1] + ids[0])
+    lane = lax.broadcasted_iota(jnp.int32, shape, 1)
+    return jnp.sum(jnp.where(row == lane, vector[...], 0.0), axis=1, keepdims=True)
 
 
 def finish_feed(ids, pieces, at, w_up, scale, scale_grad, up_grad, down_grad):
@@ -653,17 +742,14 @@
     in_grad[...] = total * factor
 
 
-def finish_feed_kernel(ids, p0, p1, p2, p3, w_up, scale, *outs):
-    finish_feed(ids, (p0, p1, p2, p3), 0, w_up, scale, *outs)
-
-
-def finish_attend_kernel(ids, p0, p1, p2, p3, w_in, gain, *outs):
-    finish_attend(ids, (p0, p1, p2, p3), 0, w_in, gain, *outs)
-
-
-def finish_all_kernel(ids, p0, p1, p2, p3, w_up, scale, w_in, gain, *outs):
-    finish_feed(ids, (p0, p1, p2, p3), 0, w_up, scale, *outs[:3])
-    finish_attend(ids, (p0, p1, p2, p3), 128, w_in, gain, *outs[3:])
+def finish_space_kernel(ids, p0, p1, p2, p3, *rest):
+    pieces, outs = (p0, p1, p2, p3), rest[4:]
+    finish_feed(ids, pieces, 0, *rest[0:2], *outs[0:3])
+    finish_attend(ids, pieces, 128, *rest[2:4], *outs[3:6])
+
+
+def finish_time_kernel(ids, p0, p1, p2, p3, *rest):
+    finish_space_kernel(ids, p0, p1, p2, p3, *rest)
 
 
 def finish_call(kernel, ids, pieces, pairs, outs):
@@ -673,9 +759,9 @@
         height = weight.shape[0] // 8
         specs += [
             pl.BlockSpec((height, weight.shape[1]), lambda i, s: (2 * s[1] + s[0], 0)),
-            pl.BlockSpec((8, height), lambda i, *s: (0, 0)),
+            pl.BlockSpec((1, vector.size), lambda i, *s: (0, 0)),
         ]
-        operands += [weight, vector.reshape(8, height)]
+        operands += [weight, vector.reshape(1, -1)]
     results = pl.pallas_call(
         kernel,
         out_shape=[jax.ShapeDtypeStruct(shape, F32) for shape in outs],
@@ -685,7 +771,7 @@
             in_specs=[whole] * 4 + specs,
             out_specs=[pl.BlockSpec(shape, lambda i, *s: (0, 0)) for shape in outs],
         ),
-        compiler_params=pltpu.CompilerParams(vmem_limit_bytes=VMEM),
+        compiler_params=pltpu.CompilerParams(vmem_limit_bytes=SMALL_VMEM),
     )(ids, *pieces, *operands)
     return [a.reshape(-1) if a.shape[0] == 1 else a for a in results]
 
@@ -835,123 +921,63 @@
     out, g0_moved = lax.optimization_barrier((out, g0_moved))
     out_moved = exchange(out)
 
+    held_back = ()
     everything = packs * tokens
     feed_shapes = [(1, width // 8), (width // 8, hidden), (hidden // 8, width)]
     attend_shapes = [(1, width // 8), (width // 8, 3 * width), (width // 8, width)]
     time_shared = [tz1, teu, te2, th, tz0, tgqkv, to, te1]
     time_one = [tz1_one, teu_one, te2_one, th_one, tz0_one, tgv_one, to_one, te1_one]
-    time_parts = ()
     if hierarchical:
         parts_shape = ((4, 4, 192, CHUNK), BF)
         mine, other = manual_call(
             time_weights_kernel,
-            ids,
+            jnp.stack([ids[0], jnp.int32(0), ids[2]]),
             time_shared + time_one,
             [parts_shape] * 2,
             [((everything, a.shape[2]), BF) for a in time_shared] + [parts_shape] * 2,
             8 * packs + 18,
             flops=packs * flops,
         )
-        time_parts, own = core_sum(mine, other)
-        time_grads = finish_call(
-            finish_all_kernel,
-            ids,
-            rest_sum(time_parts, own),
-            [(time_up, time_scale), (time_input, time_gain)],
-            feed_shapes + attend_shapes,
-        )
+        time_parts, time_own = core_sum(mine, swap(other, "tm", 8, 1), marker(g0_moved))
+        held_back = tuple(time_parts)
     else:
         grad_one = jnp.pad(tgv_one, ((0, 0), (0, 0), (2 * width, 0)))
         joined = [joint(a, b) for a, b in zip(time_shared, time_one[:5] + [grad_one] + time_one[6:])]
         time_grads = plain_grads(joined[0], joined[1], joined[3], joined[2], time_up, time_scale)
         time_grads += plain_grads(joined[4], joined[5], joined[6], joined[7], time_input, time_gain)
 
-    shared_w, shared_h = (some,) + rows_w, (some,) + rows_h
-    feed_args = [row(space_scale), sinv1, g0_moved, sslope, sz1, space_output, space_up, space_down]
-    feed_args += [sh, sz1_one, sh_one, seu_one, se2_one]
-    parts_shape = ((4, 4, 128, CHUNK), BF)
-    state_shapes = [((everything, hidden), BF), ((everything, width), BF)]
-    se1, sgo, sg1, *weights = manual_call(
-        functools.partial(space_feed_kernel, hierarchical),
+    shared_w, shared_3 = (some,) + rows_w, (some,) + rows_3
+    space_one = [sz1_one, seu_one, sh_one, se2_one, sz0_one, sgqkv_one, so_one, se1_one]
+    whole_shapes = [((everything, a.shape[2]), BF) for a in space_one]
+    parts_shapes = [((4, 4, 128, CHUNK), BF)] * 2 + [((4, 4, 64, CHUNK), BF)] * 2
+    sg1, sgqkv, *weights = manual_call(
+        functools.partial(space_kernel, hierarchical),
         ids,
-        feed_args,
-        [(shared_w, BF), (shared_w, BF), (shared_w, F32)]
-        + ([parts_shape] * 2 if hierarchical else state_shapes),
+        [row(space_scale), sinv1, g0_moved, sslope, sz1, space_output, space_up, space_down]
+        + [sqkv, sp, sh, sz0, so]
+        + space_one,
+        [(shared_w, F32), (shared_3, BF)]
+        + (parts_shapes if hierarchical else [whole_shapes[i] for i in (1, 3, 7)]),
         [
             (g0_moved.shape, BF),
-            (shared_h, BF),
-            ((everything, width), BF),
+            (sslope.shape, BF),
             (space_output.shape, BF),
             (space_up.shape, BF),
             (space_down.shape, BF),
-            ((everything, hidden), BF),
-            *state_shapes,
-            (shared_w, BF),
+            (sqkv.shape, BF),
+            (sp.shape, BF),
             (shared_w, BF),
             (shared_w, F32),
-        ]
-        + ([parts_shape] * 2 if hierarchical else []),
-        64,
-        small=2,
-        after=time_parts,
-        flops=packs * flops,
-    )
-    parts = ()
-    if hierarchical:
-        parts, own = core_sum(*weights)
-        feed_grads = finish_call(
-            finish_feed_kernel, ids, rest_sum(parts, own), [(space_up, space_scale)], feed_shapes
-        )
-    else:
-        have = some * tokens
-        seu, se2 = [a[:have].reshape(some, tokens, -1) for a in weights]
-        feed_grads = plain_grads(
-            joint(sz1, sz1_one),
-            joint(seu, seu_one),
-            joint(sh, sh_one),
-            joint(se2, se2_one),
-            space_up,
-            space_scale,
-        )
-    parts_shape = ((4, 4, 64, CHUNK), BF)
-    sgqkv, *weights = manual_call(
-        functools.partial(space_attend_kernel, hierarchical),
-        ids,
-        [sqkv, sp, sgo, sz0, so, se1, sz0_one, so_one, se1_one, sgqkv_one],
-        [((some,) + rows_3, BF)] + ([parts_shape] * 2 if hierarchical else []),
-        [
-            ((some,) + rows_3, BF),
-            (sp.shape, BF),
-            (shared_w, BF),
-            ((everything, width), BF),
-            ((everything, width), BF),
-            ((everything, width), BF),
-            ((everything, 3 * width), BF),
             ((4, tokens, tokens), BF),
             ((HEADS, tokens, tokens), BF),
         ]
-        + ([parts_shape] * 2 if hierarchical else []),
-        64,
-        after=parts,
-        flops=packs * flops,
+        + whole_shapes
+        + (parts_shapes if hierarchical else []),
+        80,
+        small=2,
+        after=held_back,
+        flops=2 * packs * flops,
     )
-    if hierarchical:
-        attend_grads = finish_call(
-            finish_attend_kernel,
-            ids,
-            rest_sum(*core_sum(*weights)),
-            [(space_input, space_gain)],
-            attend_shapes,
-        )
-    else:
-        attend_grads = plain_grads(
-            joint(sz0, sz0_one),
-            joint(sgqkv, sgqkv_one),
-            joint(so, so_one),
-            joint(se1, se1_one),
-            space_input,
-            space_gain,
-        )
     input_grad, result = shared.call(
         space_back_in,
         [
@@ -966,6 +992,58 @@
         [("pack", frames.shape, F32, input_grad), ("pack", frames.shape, F32, result)],
         flops=flops // 4,
     )
+    if hierarchical:
+        feed, feed_other, attend_mine, attend_other = weights
+        feed_got = swap(feed_other, "tm", 8, 1)
+        attend_got = swap(attend_other, "tm", 8, 1)
+        time_own, input_grad = lax.optimization_barrier((time_own, input_grad))
+        time_rows = stream_total(time_parts, time_own)
+        note = marker(time_rows)
+        feed_parts = [add(feed[d], feed_got[d], note) for d in range(1, 4)]
+        attend_got, feed_parts[0] = lax.optimization_barrier((attend_got, feed_parts[0]))
+        attend_part = add(attend_mine[2:], attend_got[2:])
+        rows = stream_sum(feed_parts, (feed[0], feed_got[0]))
+        half = swap(attend_part, "stream", 4, 2)
+        got, rows[1] = lax.optimization_barrier((attend_got[1], rows[1]))
+        near = swap(add(attend_mine[1], got, half[1]), "stream", 4, 1)
+        feed_final = z_sum(rows)
+        own, feed_final = lax.optimization_barrier(((attend_mine[0], attend_got[0]), feed_final))
+        attend_rows = [add(*[term[d] for term in (*own, half[0], near)]) for d in range(4)]
+        final = jnp.concatenate([feed_final, z_sum(attend_rows)])
+        grads = finish_call(
+            finish_space_kernel,
+            ids,
+            gather_parts(final),
+            [(space_up, space_scale), (space_input, space_gain)],
+            feed_shapes + attend_shapes,
+        )
+        feed_grads, attend_grads = grads[:3], grads[3:]
+        time_grads = finish_call(
+            finish_time_kernel,
+            ids,
+            gather_parts(z_scatter(time_rows)),
+            [(time_up, time_scale), (time_input, time_gain)],
+            feed_shapes + attend_shapes,
+        )
+    else:
+        have = some * tokens
+        seu, se2, se1 = [a[:have].reshape(some, tokens, -1) for a in weights]
+        feed_grads = plain_grads(
+            joint(sz1, sz1_one),
+            joint(seu, seu_one),
+            joint(sh, sh_one),
+            joint(se2, se2_one),
+            space_up,
+            space_scale,
+        )
+        attend_grads = plain_grads(
+            joint(sz0, sz0_one),
+            joint(sgqkv, sgqkv_one),
+            joint(so, so_one),
+            joint(se1, se1_one),
+            space_input,
+            space_gain,
+        )
     grads = attend_grads + feed_grads + time_grads[3:] + time_grads[:3]
     return (result, input_grad, *grads)
 

time: 282 us -> 250 us (0.89)
  blocking collectives: 24.7 us -> 0 us
  Pallas kernels: 122 us -> 114 us
    all_to_all x1 -> x0, blocking collectives: 24.7 us -> none  [exchange(): return lax.all_to_all(array, 'tm', split_axis=0, concat_axis=0, tiled=True)]
    ppermute x30 -> x23, starting transfers between devices: 36.2 us -> 27.1 us  [swap(): return lax.ppermute(array, axis, [(i, i ^ mask) for i in range(size)])]
    ppermute x30 -> x23, waiting for transfers between devices: 50.6 us -> 45 us  [swap(): return lax.ppermute(array, axis, [(i, i ^ mask) for i in range(size)])]
    pallas_call x3 -> x2, Pallas kernels: 9.21 us -> 3.96 us  [finish_call(): pl.pallas_call(kernel, out_shape=[jax.ShapeDtypeStruct(shape, F32) for sh...]
    all_to_all x0 -> x1, starting transfers between devices: none -> 4.98 us  [z_scatter(): lax.all_to_all(rows, 'tm', split_axis=0, concat_axis=0, tiled=True, axis_...]
    squeeze x0 -> x4, local copies, waits for them, and re-layouts: none -> 4.51 us  [the longest x1 2.08 us: core_sum(): mine[0]]
    all_to_all x3 -> x4, waiting for transfers between devices: 5.44 us -> 9.93 us  [exchange(): return lax.all_to_all(array, 'tm', split_axis=0, concat_axis=0, tiled=True)]
    all_to_all x3 -> x4, starting transfers between devices: 13.6 us -> 17.6 us  [exchange(): return lax.all_to_all(array, 'tm', split_axis=0, concat_axis=0, tiled=True)]
  transfers between devices with their start and end apart: 33 -> 28, of which waited for: 12 -> 17; matrix products, arithmetic and copies ran while one was open for 6% -> 9% of each run, Pallas kernels for 22% -> 33%
where the time goes in v3:
time: 250 us; the launch traced here: 246 us
  Pallas kernels  114 us (46%)
  waiting for transfers between devices  55 us (22%)
  starting transfers between devices  49.6 us (20%)
  other arithmetic  18.7 us (7%)
  local copies, waits for them, and re-layouts  7.29 us (3%)
    pallas_call x4, Pallas kernels, call(): pl.pallas_call(without(kernel, len(scalars) + len(args), unread), out_sha...  70.6 us
    ppermute x23, waiting for transfers between devices, swap(): return lax.ppermute(array, axis, [(i, i ^ mask) for i in range(size)])  45 us
    pallas_call x2, Pallas kernels, manual_call(): pl.pallas_call(without(kernel, 1 + len(args), len(after)), out_shape=[jax...  35.4 us
    ppermute x23, starting transfers between devices, swap(): return lax.ppermute(array, axis, [(i, i ^ mask) for i in range(size)])  27.1 us
    all_to_all x4, starting transfers between devices, exchange(): return lax.all_to_all(array, 'tm', split_axis=0, concat_axis=0, tiled=True)  17.6 us
    convert_element_type x9, other arithmetic, add(): return total.astype(BF)  17.4 us
    all_to_all x4, waiting for transfers between devices, exchange(): return lax.all_to_all(array, 'tm', split_axis=0, concat_axis=0, tiled=True)  9.93 us
  transfers between devices with their start and end apart: 28, of which 17 were waited for; matrix products, arithmetic and copies ran while one was open for 9% of the time, Pallas kernels for 33%

profile of v3, /device:TPU:0, one launch (start us, length us, event | category | flops | bytes accessed | tf_op | source)
XLA Modules:
  0.0 245.6 jit_solution(3221471236164213769)
XLA Ops:
  0.6 2.8 %shard_map.254.refs_8_ = bf16[8,3,32,512]{3,2,1,0:T(8,128)(2,1)} custom-call(s32[4,8]{1,0:T(4,128)} %refs_0_.7, bf16[4,1,256,512]{3,2,1,0:T(8,128)(2,1)} %refs_2_.2), custom_call_target="tpu_custom_call" | custom-call | tf_op jit(solution)/shard_map/pallas_call | solution.py:791
  3.5 6.3 %all-to-all-start = ((bf16[8,3,32,512]{3,2,1,0:T(8,128)(2,1)}), bf16[8,3,32,512]{3,2,1,0:T(8,128)(2,1)S(1)}, u32[]{:S(2)}, u32[]{:S(2)}) async-start(bf16[8,3,32,512]{3,2,1,0:T(8,128)(2,1)} %shard_map.254.refs_8_), calls=%async_computation | async-start | bytes 1572864 | tf_op jit(solution)/shard_map/all_to_all | solution.py:838
  9.8 17.0 %shard_map.255 = (bf16[8,3,32,512]{3,2,1,0:T(8,128)(2,1)}, bf16[3,256,512]{2,1,0:T(8,128)(2,1)}, f32[3,256,128]{2,1,0:T(8,128)}, bf16[3,256,1536]{2,1,0:T(8,128)...) custom-call(s32[4,8]{1,0:T(4,128)} %refs_0_.7, ...), custom_call_target="tpu_custom_call" | custom-call | flops 4831838208 | bytes 8130560 | tf_op jit(solution)/shard_map/pallas_call | solution.py:448
  26.8 4.0 %all-to-all-done.refs_2_ = bf16[8,3,32,512]{3,2,1,0:T(8,128)(2,1)S(1)} async-done(((bf16[8,3,32,512]{3,2,1,0:T(8,128)(2,1)}), bf16[8,3,32,512]{3,2,1,0:T(8,128)(2,1)S(1)}, u32[]{:S(2)}, u32[]{:S(2)}) %all-to-all-start) | async-done | bytes 786464 | tf_op jit(solution)/shard_map/all_to_all | solution.py:838
  30.8 3.7 %all-to-all-start.1 = ((bf16[8,3,32,512]{3,2,1,0:T(8,128)(2,1)}), bf16[8,3,32,512]{3,2,1,0:T(8,128)(2,1)S(1)}, u32[]{:S(2)}, u32[]{:S(2)}) async-start(bf16[8,3,32,512]{3,2,1,0:T(8,128)(2,1)} %get-tuple-element.90.refs_15_), calls=%async_computation.1 | async-start | bytes 1572864 | tf_op jit(solution)/shard_map/all_to_all | solution.py:838
  34.5 18.9 %shard_map.256 = (f32[4,1,256,512]{3,2,1,0:T(8,128)}, f32[4,1,256,512]{3,2,1,0:T(8,128)}, bf16[1,256,512]{2,1,0:T(8,128)(2,1)}, bf16[1,256,512]{2,1,0:T(8,128)(2...) custom-call(s32[4,8]{1,0:T(4,128)} %refs_0_.7, ...), custom_call_target="tpu_custom_call" | custom-call | flops 9663676416 | bytes 15474688 | tf_op jit(solution)/shard_map/pallas_call | solution.py:448
  56.3 27.3 %shard_map.257 = (bf16[8,3,32,512]{3,2,1,0:T(8,128)(2,1)}, bf16[8,3,32,512]{3,2,1,0:T(8,128)(2,1)}, bf16[3,256,512]{2,1,0:T(8,128)(2,1)}, bf16[3,256,1536]{2,1,0...) custom-call(s32[4,8]{1,0:T(4,128)} %refs_0_.7, ...), custom_call_target="tpu_custom_call" | custom-call | flops 14495514624 | bytes 8130560 | tf_op jit(solution)/shard_map/pallas_call | solution.py:448
  83.6 3.6 %all-to-all-start.2 = ((bf16[8,3,32,512]{3,2,1,0:T(8,128)(2,1)}), bf16[8,3,32,512]{3,2,1,0:T(8,128)(2,1)S(1)}, u32[]{:S(2)}, u32[]{:S(2)}) async-start(bf16[8,3,32,512]{3,2,1,0:T(8,128)(2,1)} %get-tuple-element.94), calls=%async_computation.2 | async-start | bytes 1572864 | tf_op jit(solution)/shard_map/all_to_all | solution.py:838
  88.4 13.2 %shard_map.258 = (bf16[4,4,192,512]{3,2,1,0:T(8,128)(2,1)}, bf16[4,4,192,512]{3,2,1,0:T(8,128)(2,1)}) custom-call(s32[3]{0:T(128)} %add_add_fusion.1.refs_0_, bf16[3,256,512]{2,1,0:T(8,128)(2,1)} %get-tuple-element.110.refs_1_, bf16[3,256,2048]{2,1,0:T(8,128)(2,1)} %get-tuple-element.111.refs_2_, bf16[3,256,512]{2,1,0:T(8,128)(2,1)} %get-tuple-element.112.refs_3_, ...), custom_call_target="tpu_custom_call" | custom-call | flops 6442450944 | tf_op jit(solution)/shard_map/pallas_call | solution.py:549
  102.1 2.1 slice_bitcast_fusion.1
  104.1 4.0 %all-to-all-done.2.source.refs_3_ = bf16[8,3,32,512]{3,2,1,0:T(8,128)(2,1)S(1)} async-done(((bf16[8,3,32,512]{3,2,1,0:T(8,128)(2,1)}), bf16[8,3,32,512]{3,2,1,0:T(8,128)(2,1)S(1)}, u32[]{:S(2)}, u32[]{:S(2)}) %all-to-all-start.2) | async-done | bytes 786464 | tf_op jit(solution)/shard_map/all_to_all | solution.py:838
  109.6 4.0 %all-to-all-start.3 = ((bf16[8,3,32,512]{3,2,1,0:T(8,128)(2,1)}), bf16[8,3,32,512]{3,2,1,0:T(8,128)(2,1)S(1)}, u32[]{:S(2)}, u32[]{:S(2)}) async-start(bf16[8,3,32,512]{3,2,1,0:T(8,128)(2,1)} %get-tuple-element.131), calls=%async_computation.3 | async-start | bytes 1572864 | tf_op jit(solution)/shard_map/all_to_all | solution.py:838
  113.6 4.2 %fusion = (bf16[4,192,512]{2,1,0:T(8,128)(2,1)}, bf16[4,192,512]{2,1,0:T(8,128)(2,1)}, bf16[4,192,512]{2,1,0:T(8,128)(2,1)}) fusion(bf16[4,4,192,512]{3,2,1,0:T(8,128)(2,1)} %collective-permute-done, bf16[4,4,192,512]{3,2,1,0:T(8,128)(2,1)} %get-tuple-element.126, f32[512]{0:T(512)} %bitcast.192), kind=kLoop, calls=%fused_computation.1 | loop fusion | flops 5898240 | bytes 7079936 | tf_op jit(solution)/shard_map/convert_element_type | solution.py:573
  117.8 2.5 %collective-permute-start.5 = (bf16[4,192,512]{2,1,0:T(8,128)(2,1)}, bf16[4,192,512]{2,1,0:T(8,128)(2,1)S(1)}, u32[]{:S(2)}, u32[]{:S(2)}) collective-permute-start(bf16[4,192,512]{2,1,0:T(8,128)(2,1)} %get-tuple-element.162.refs_24_), channel_id=1, source_target_pairs={{0,24},{8,16},{16,8},{24,0},{1,25},{9,17},{17,9},{25,1},{2,26},{10... | collective-permute-start | bytes 2359304 | tf_op jit(solution)/shard_map/ppermute | solution.py:566
  121.3 22.2 %shard_map.260 = (f32[3,256,512]{2,1,0:T(8,128)}, bf16[3,256,1536]{2,1,0:T(8,128)(2,1)}, bf16[4,4,128,512]{3,2,1,0:T(8,128)(2,1)}, bf16[4,4,128,512]{3,2,1,0:T(8...) custom-call(s32[3]{0:T(128)} %add_add_fusion.refs_0_.ids, f32[1,512]{1,0:T(1,128)} %bitcast.189, ...), custom_call_target="tpu_custom_call" | custom-call | flops 12884901888 | tf_op jit(solution)/shard_map/pallas_call | solution.py:549
  144.4 7.3 %shard_map.261 = (f32[4,1,256,512]{3,2,1,0:T(8,128)}, f32[4,1,256,512]{3,2,1,0:T(8,128)}) custom-call(s32[4,8]{1,0:T(4,128)} %refs_0_.7, bf16[3,256,1536]{2,1,0:T(8,128)(2,1)} %get-tuple-element.128.refs_1_, bf16[512,1536]{1,0:T(8,128)(2,1)} %rest_2_.2, f32[1,512]{1,0:T(1,128)} %bitcast.179, ...), custom_call_target="tpu_custom_call", output_to_operand_aliasing={{0}: (8, {}), {1}: (9, {})} | custom-call | flops 1207959552 | bytes 11667456 | tf_op jit(solution)/shard_map/pallas_call | solution.py:448
  153.6 2.0 collective-permute-done.4
  159.1 2.9 %fusion.4 = (bf16[4,128,512]{2,1,0:T(8,128)(2,1)}, bf16[4,128,512]{2,1,0:T(8,128)(2,1)}, bf16[4,128,512]{2,1,0:T(8,128)(2,1)}) fusion(bf16[4,4,128,512]{3,2,1,0:T(8,128)(2,1)} %collective-permute-done.2, bf16[4,4,128,512]{3,2,1,0:T(8,128)(2,1)S(1)} %copy-done.11, f32[512]{0:T(512)} %bitcast.191), kind=kLoop, calls=%fused_computation.10 | loop fusion | flops 3932160 | bytes 4720640 | tf_op jit(solution)/shard_map/convert_element_type | solution.py:573
  162.0 2.4 collective-permute-start.8
  169.0 5.0 %all-to-all-start.4 = ((bf16[4,192,512]{2,1,0:T(8,128)(2,1)}), bf16[4,192,512]{2,1,0:T(8,128)(2,1)S(1)}, u32[]{:S(2)}, u32[]{:S(2)}) async-start(bf16[4,192,512]{2,1,0:T(8,128)(2,1)} %add_convert_fusion.source), calls=%async_computation.4 | async-start | bytes 1572864 | tf_op jit(solution)/shard_map/all_to_all | solution.py:612
  175.1 2.9 %collective-permute-done.8 = bf16[4,128,512]{2,1,0:T(8,128)(2,1)} collective-permute-done((bf16[4,128,512]{2,1,0:T(8,128)(2,1)}, bf16[4,128,512]{2,1,0:T(8,128)(2,1)}, u32[]{:S(2)}, u32[]{:S(2)}) %collective-permute-start.8) | collective-permute-done | bytes 524320 | tf_op jit(solution)/shard_map/ppermute | solution.py:566
  178.0 10.5 %collective-permute-done.7 = bf16[4,128,512]{2,1,0:T(8,128)(2,1)} collective-permute-done((bf16[4,128,512]{2,1,0:T(8,128)(2,1)}, bf16[4,128,512]{2,1,0:T(8,128)(2,1)}, u32[]{:S(2)}, u32[]{:S(2)}) %collective-permute-start.7) | collective-permute-done | bytes 524320 | tf_op jit(solution)/shard_map/ppermute | solution.py:566
  190.2 9.4 %collective-permute-done.12 = bf16[2,4,64,512]{3,2,1,0:T(8,128)(2,1)} collective-permute-done((bf16[2,4,64,512]{3,2,1,0:T(8,128)(2,1)}, bf16[2,4,64,512]{3,2,1,0:T(8,128)(2,1)}, u32[]{:S(2)}, u32[]{:S(2)}) %collective-permute-start.12) | collective-permute-done | bytes 524320 | tf_op jit(solution)/shard_map/ppermute | solution.py:566
  202.3 3.7 %collective-permute-start.11 = (bf16[128,512]{1,0:T(8,128)(2,1)S(1)}, bf16[128,512]{1,0:T(8,128)(2,1)S(1)}, u32[]{:S(2)}, u32[]{:S(2)}) collective-permute-start(bf16[128,512]{1,0:T(8,128)(2,1)S(1)} %get-tuple-element.166), channel_id=1, source_target_pairs={{0,6},{1,7},{2,4},{3,5},{4,2},{5,3},{6,0},{7,1},{8,14},{9,15},{10,... | collective-permute-start | bytes 393224 | tf_op jit(solution)/shard_map/ppermute | solution.py:566
  206.7 3.8 %collective-permute-done.11 = bf16[128,512]{1,0:T(8,128)(2,1)S(1)} collective-permute-done((bf16[128,512]{1,0:T(8,128)(2,1)S(1)}, bf16[128,512]{1,0:T(8,128)(2,1)S(1)}, u32[]{:S(2)}, u32[]{:S(2)}) %collective-permute-start.11) | collective-permute-done | bytes 131104 | tf_op jit(solution)/shard_map/ppermute | solution.py:566
  210.5 6.7 %collective-permute-done.10 = bf16[128,512]{1,0:T(8,128)(2,1)S(1)} collective-permute-done((bf16[128,512]{1,0:T(8,128)(2,1)S(1)}, bf16[128,512]{1,0:T(8,128)(2,1)S(1)}, u32[]{:S(2)}, u32[]{:S(2)}) %collective-permute-start.10) | collective-permute-done | bytes 131104 | tf_op jit(solution)/shard_map/ppermute | solution.py:566
  220.2 2.4 collective-permute-start.16
  222.6 2.0 collective-permute-start.14
  236.5 2.0 shard_map.264
  238.5 2.2 collective-permute-done.17.p1
  240.6 2.7 %collective-permute-done.18.p2 = bf16[192,512]{1,0:T(8,128)(2,1)S(1)} collective-permute-done((bf16[192,512]{1,0:T(8,128)(2,1)S(1)}, bf16[192,512]{1,0:T(8,128)(2,1)S(1)}, u32[]{:S(2)}, u32[]{:S(2)}) %collective-permute-start.18) | collective-permute-done | bytes 196640 | tf_op jit(solution)/shard_map/ppermute | solution.py:566
  243.4 2.0 shard_map.263
  (88 shorter events, 38.8 us)
Async XLA Ops:
  3.5 27.3 %all-to-all-start = ((bf16[8,3,32,512]{3,2,1,0:T(8,128)(2,1)}), bf16[8,3,32,512]{3,2,1,0:T(8,128)(2,1)S(1)}, u32[]{:S(2)}, u32[]{:S(2)}) async-start(bf16[8,3,32,512]{3,2,1,0:T(8,128)(2,1)} %shard_map.254.refs_8_), calls=%async_computation | async-start | bytes 1572864 | tf_op jit(solution)/shard_map/all_to_all | solution.py:838
  30.8 24.6 %all-to-all-start.1 = ((bf16[8,3,32,512]{3,2,1,0:T(8,128)(2,1)}), bf16[8,3,32,512]{3,2,1,0:T(8,128)(2,1)S(1)}, u32[]{:S(2)}, u32[]{:S(2)}) async-start(bf16[8,3,32,512]{3,2,1,0:T(8,128)(2,1)} %get-tuple-element.90.refs_15_), calls=%async_computation.1 | async-start | bytes 1572864 | tf_op jit(solution)/shard_map/all_to_all | solution.py:838
  83.6 24.5 %all-to-all-start.2 = ((bf16[8,3,32,512]{3,2,1,0:T(8,128)(2,1)}), bf16[8,3,32,512]{3,2,1,0:T(8,128)(2,1)S(1)}, u32[]{:S(2)}, u32[]{:S(2)}) async-start(bf16[8,3,32,512]{3,2,1,0:T(8,128)(2,1)} %get-tuple-element.94), calls=%async_computation.2 | async-start | bytes 1572864 | tf_op jit(solution)/shard_map/all_to_all | solution.py:838
  101.6 11.9 %collective-permute-start = (bf16[4,4,192,512]{3,2,1,0:T(8,128)(2,1)}, bf16[4,4,192,512]{3,2,1,0:T(8,128)(2,1)}, u32[]{:S(2)}, u32[]{:S(2)}) collective-permute-start(bf16[4,4,192,512]{3,2,1,0:T(8,128)(2,1)} %get-tuple-element.127), channel_id=1, source_target_pairs={{0,1},{1,0},{2,3},{3,2},{4,5},{5,4},{6,7},{7,6},{8,9},{9,8},{10,11... | collective-permute-start | bytes 9437192 | tf_op jit(solution)/shard_map/ppermute | solution.py:566
  109.6 33.9 %all-to-all-start.3 = ((bf16[8,3,32,512]{3,2,1,0:T(8,128)(2,1)}), bf16[8,3,32,512]{3,2,1,0:T(8,128)(2,1)S(1)}, u32[]{:S(2)}, u32[]{:S(2)}) async-start(bf16[8,3,32,512]{3,2,1,0:T(8,128)(2,1)} %get-tuple-element.131), calls=%async_computation.3 | async-start | bytes 1572864 | tf_op jit(solution)/shard_map/all_to_all | solution.py:838
  117.8 35.8 %collective-permute-start.5 = (bf16[4,192,512]{2,1,0:T(8,128)(2,1)}, bf16[4,192,512]{2,1,0:T(8,128)(2,1)S(1)}, u32[]{:S(2)}, u32[]{:S(2)}) collective-permute-start(bf16[4,192,512]{2,1,0:T(8,128)(2,1)} %get-tuple-element.162.refs_24_), channel_id=1, source_target_pairs={{0,24},{8,16},{16,8},{24,0},{1,25},{9,17},{17,9},{25,1},{2,26},{10... | collective-permute-start | bytes 2359304 | tf_op jit(solution)/shard_map/ppermute | solution.py:566
  120.3 35.3 %collective-permute-start.4 = (bf16[4,192,512]{2,1,0:T(8,128)(2,1)}, bf16[4,192,512]{2,1,0:T(8,128)(2,1)S(1)}, u32[]{:S(2)}, u32[]{:S(2)}) collective-permute-start(bf16[4,192,512]{2,1,0:T(8,128)(2,1)} %get-tuple-element.163.refs_23_), channel_id=1, source_target_pairs={{0,16},{8,24},{16,0},{24,8},{1,17},{9,25},{17,1},{25,9},{2,18},{10... | collective-permute-start | bytes 2359304 | tf_op jit(solution)/shard_map/ppermute | solution.py:566
  120.8 34.9 %collective-permute-start.3 = (bf16[4,192,512]{2,1,0:T(8,128)(2,1)}, bf16[4,192,512]{2,1,0:T(8,128)(2,1)S(1)}, u32[]{:S(2)}, u32[]{:S(2)}) collective-permute-start(bf16[4,192,512]{2,1,0:T(8,128)(2,1)} %get-tuple-element.164.refs_22_), channel_id=1, source_target_pairs={{0,8},{8,0},{16,24},{24,16},{1,9},{9,1},{17,25},{25,17},{2,10},{10... | collective-permute-start | bytes 2359304 | tf_op jit(solution)/shard_map/ppermute | solution.py:566
  153.0 9.0 %collective-permute-start.1 = (bf16[4,4,64,512]{3,2,1,0:T(8,128)(2,1)}, bf16[4,4,64,512]{3,2,1,0:T(8,128)(2,1)}, u32[]{:S(2)}, u32[]{:S(2)}) collective-permute-start(bf16[4,4,64,512]{3,2,1,0:T(8,128)(2,1)} %get-tuple-element.138), channel_id=1, source_target_pairs={{0,1},{1,0},{2,3},{3,2},{4,5},{5,4},{6,7},{7,6},{8,9},{9,8},{10,11... | collective-permute-start | bytes 3145736 | tf_op jit(solution)/shard_map/ppermute | solution.py:566
  153.1 6.0 %collective-permute-start.2 = (bf16[4,4,128,512]{3,2,1,0:T(8,128)(2,1)}, bf16[4,4,128,512]{3,2,1,0:T(8,128)(2,1)}, u32[]{:S(2)}, u32[]{:S(2)}) collective-permute-start(bf16[4,4,128,512]{3,2,1,0:T(8,128)(2,1)} %get-tuple-element.140), channel_id=1, source_target_pairs={{0,1},{1,0},{2,3},{3,2},{4,5},{5,4},{6,7},{7,6},{8,9},{9,8},{10,11... | collective-permute-start | bytes 6291464 | tf_op jit(solution)/shard_map/ppermute | solution.py:566
  162.0 16.0 %collective-permute-start.8 = (bf16[4,128,512]{2,1,0:T(8,128)(2,1)}, bf16[4,128,512]{2,1,0:T(8,128)(2,1)}, u32[]{:S(2)}, u32[]{:S(2)}) collective-permute-start(bf16[4,128,512]{2,1,0:T(8,128)(2,1)} %get-tuple-element.169), channel_id=1, source_target_pairs={{0,24},{8,16},{16,8},{24,0},{1,25},{9,17},{17,9},{25,1},{2,26},{10... | collective-permute-start | bytes 1572872 | tf_op jit(solution)/shard_map/ppermute | solution.py:566
  164.4 24.1 %collective-permute-start.7 = (bf16[4,128,512]{2,1,0:T(8,128)(2,1)}, bf16[4,128,512]{2,1,0:T(8,128)(2,1)}, u32[]{:S(2)}, u32[]{:S(2)}) collective-permute-start(bf16[4,128,512]{2,1,0:T(8,128)(2,1)} %get-tuple-element.168), channel_id=1, source_target_pairs={{0,16},{8,24},{16,0},{24,8},{1,17},{9,25},{17,1},{25,9},{2,18},{10... | collective-permute-start | bytes 1572872 | tf_op jit(solution)/shard_map/ppermute | solution.py:566
  165.0 23.6 %collective-permute-start.6 = (bf16[4,128,512]{2,1,0:T(8,128)(2,1)}, bf16[4,128,512]{2,1,0:T(8,128)(2,1)}, u32[]{:S(2)}, u32[]{:S(2)}) collective-permute-start(bf16[4,128,512]{2,1,0:T(8,128)(2,1)} %get-tuple-element.144), channel_id=1, source_target_pairs={{0,8},{8,0},{16,24},{24,16},{1,9},{9,1},{17,25},{25,17},{2,10},{10... | collective-permute-start | bytes 1572872 | tf_op jit(solution)/shard_map/ppermute | solution.py:566
  167.5 32.2 %collective-permute-start.12 = (bf16[2,4,64,512]{3,2,1,0:T(8,128)(2,1)}, bf16[2,4,64,512]{3,2,1,0:T(8,128)(2,1)}, u32[]{:S(2)}, u32[]{:S(2)}) collective-permute-start(bf16[2,4,64,512]{3,2,1,0:T(8,128)(2,1)} %add_convert_fusion.1), channel_id=1, source_target_pairs={{0,16},{8,24},{16,0},{24,8},{1,17},{9,25},{17,1},{25,9},{2,18},{10... | collective-permute-start | bytes 1572872 | tf_op jit(solution)/shard_map/ppermute | solution.py:566
  169.0 55.7 %all-to-all-start.4 = ((bf16[4,192,512]{2,1,0:T(8,128)(2,1)}), bf16[4,192,512]{2,1,0:T(8,128)(2,1)S(1)}, u32[]{:S(2)}, u32[]{:S(2)}) async-start(bf16[4,192,512]{2,1,0:T(8,128)(2,1)} %add_convert_fusion.source), calls=%async_computation.4 | async-start | bytes 1572864 | tf_op jit(solution)/shard_map/all_to_all | solution.py:612
  200.7 17.8 %collective-permute-start.13 = (bf16[4,64,512]{2,1,0:T(8,128)(2,1)S(1)}, bf16[4,64,512]{2,1,0:T(8,128)(2,1)S(1)}, u32[]{:S(2)}, u32[]{:S(2)}) collective-permute-start(bf16[4,64,512]{2,1,0:T(8,128)(2,1)S(1)} %fusion.6), channel_id=1, source_target_pairs={{0,8},{8,0},{16,24},{24,16},{1,9},{9,1},{17,25},{25,17},{2,10},{10... | collective-permute-start | bytes 786440 | tf_op jit(solution)/shard_map/ppermute | solution.py:566
  202.3 8.2 %collective-permute-start.11 = (bf16[128,512]{1,0:T(8,128)(2,1)S(1)}, bf16[128,512]{1,0:T(8,128)(2,1)S(1)}, u32[]{:S(2)}, u32[]{:S(2)}) collective-permute-start(bf16[128,512]{1,0:T(8,128)(2,1)S(1)} %get-tuple-element.166), channel_id=1, source_target_pairs={{0,6},{1,7},{2,4},{3,5},{4,2},{5,3},{6,0},{7,1},{8,14},{9,15},{10,... | collective-permute-start | bytes 393224 | tf_op jit(solution)/shard_map/ppermute | solution.py:566
  206.0 11.2 %collective-permute-start.10 = (bf16[128,512]{1,0:T(8,128)(2,1)S(1)}, bf16[128,512]{1,0:T(8,128)(2,1)S(1)}, u32[]{:S(2)}, u32[]{:S(2)}) collective-permute-start(bf16[128,512]{1,0:T(8,128)(2,1)S(1)} %get-tuple-element.165), channel_id=1, source_target_pairs={{0,4},{1,5},{2,6},{3,7},{4,0},{5,1},{6,2},{7,3},{8,12},{9,13},{10,... | collective-permute-start | bytes 393224 | tf_op jit(solution)/shard_map/ppermute | solution.py:566
  206.0 11.2 %collective-permute-start.9 = (bf16[128,512]{1,0:T(8,128)(2,1)S(1)}, bf16[128,512]{1,0:T(8,128)(2,1)S(1)}, u32[]{:S(2)}, u32[]{:S(2)}) collective-permute-start(bf16[128,512]{1,0:T(8,128)(2,1)S(1)} %get-tuple-element.145), channel_id=1, source_target_pairs={{0,2},{1,3},{2,0},{3,1},{4,6},{5,7},{6,4},{7,5},{8,10},{9,11},{10,... | collective-permute-start | bytes 393224 | tf_op jit(solution)/shard_map/ppermute | solution.py:566
  206.7 29.8 %copy-start.1 = (bf16[512,2048]{1,0:T(8,128)(2,1)S(1)}, bf16[512,2048]{1,0:T(8,128)(2,1)}, u32[]{:S(2)}) copy-start(bf16[512,2048]{1,0:T(8,128)(2,1)} %rest_0_.3) | copy-start | bytes 6291460
  206.7 29.8 %copy-start.5 = (s32[3]{0:T(128)S(1)}, s32[3]{0:T(128)}, u32[]{:S(2)}) copy-start(s32[3]{0:T(128)} %add_add_fusion.refs_0_.ids) | copy-start | bytes 40
  206.7 29.8 %copy-start.6 = (f32[512]{0:T(512)S(1)}, f32[512]{0:T(512)}, u32[]{:S(2)}) copy-start(f32[512]{0:T(512)} %param.22) | copy-start | bytes 6148
  206.7 29.8 %copy-start.7 = (f32[512]{0:T(512)S(1)}, f32[512]{0:T(512)}, u32[]{:S(2)}) copy-start(f32[512]{0:T(512)} %param.25) | copy-start | bytes 6148
  220.2 6.9 %collective-permute-start.16 = (bf16[64,512]{1,0:T(8,128)(2,1)}, bf16[64,512]{1,0:T(8,128)(2,1)}, u32[]{:S(2)}, u32[]{:S(2)}) collective-permute-start(bf16[64,512]{1,0:T(8,128)(2,1)} %get-tuple-element.172), channel_id=1, source_target_pairs={{0,6},{1,7},{2,4},{3,5},{4,2},{5,3},{6,0},{7,1},{8,14},{9,15},{10,... | collective-permute-start | bytes 196616 | tf_op jit(solution)/shard_map/ppermute | solution.py:566
  222.6 6.0 %collective-permute-start.15 = (bf16[64,512]{1,0:T(8,128)(2,1)}, bf16[64,512]{1,0:T(8,128)(2,1)}, u32[]{:S(2)}, u32[]{:S(2)}) collective-permute-start(bf16[64,512]{1,0:T(8,128)(2,1)} %get-tuple-element.173), channel_id=1, source_target_pairs={{0,4},{1,5},{2,6},{3,7},{4,0},{5,1},{6,2},{7,3},{8,12},{9,13},{10,... | collective-permute-start | bytes 196616 | tf_op jit(solution)/shard_map/ppermute | solution.py:566
  222.6 6.0 %collective-permute-start.14 = (bf16[64,512]{1,0:T(8,128)(2,1)}, bf16[64,512]{1,0:T(8,128)(2,1)}, u32[]{:S(2)}, u32[]{:S(2)}) collective-permute-start(bf16[64,512]{1,0:T(8,128)(2,1)} %get-tuple-element.171), channel_id=1, source_target_pairs={{0,2},{1,3},{2,0},{3,1},{4,6},{5,7},{6,4},{7,5},{8,10},{9,11},{10,... | collective-permute-start | bytes 196616 | tf_op jit(solution)/shard_map/ppermute | solution.py:566
  224.7 7.9 %collective-permute-start.20 = (bf16[192,512]{1,0:T(8,128)(2,1)S(1)}, bf16[192,512]{1,0:T(8,128)(2,1)S(1)}, u32[]{:S(2)}, u32[]{:S(2)}) collective-permute-start(bf16[192,512]{1,0:T(8,128)(2,1)S(1)} %fusion.11.p0), channel_id=1, source_target_pairs={{0,8},{8,0},{16,24},{24,16},{1,9},{9,1},{17,25},{25,17},{2,10},{10... | collective-permute-start | bytes 589832 | tf_op jit(solution)/shard_map/ppermute | solution.py:566
  225.3 9.9 %collective-permute-start.21 = (bf16[192,512]{1,0:T(8,128)(2,1)S(1)}, bf16[192,512]{1,0:T(8,128)(2,1)S(1)}, u32[]{:S(2)}, u32[]{:S(2)}) collective-permute-start(bf16[192,512]{1,0:T(8,128)(2,1)S(1)} %fusion.11.p0), channel_id=1, source_target_pairs={{0,16},{8,24},{16,0},{24,8},{1,17},{9,25},{17,1},{25,9},{2,18},{10... | collective-permute-start | bytes 589832 | tf_op jit(solution)/shard_map/ppermute | solution.py:566
  227.1 9.4 %collective-permute-start.22 = (bf16[192,512]{1,0:T(8,128)(2,1)S(1)}, bf16[192,512]{1,0:T(8,128)(2,1)S(1)}, u32[]{:S(2)}, u32[]{:S(2)}) collective-permute-start(bf16[192,512]{1,0:T(8,128)(2,1)S(1)} %fusion.11.p0), channel_id=1, source_target_pairs={{0,24},{8,16},{16,8},{24,0},{1,25},{9,17},{17,9},{25,1},{2,26},{10... | collective-permute-start | bytes 589832 | tf_op jit(solution)/shard_map/ppermute | solution.py:566
  229.7 10.9 %collective-permute-start.17 = (bf16[192,512]{1,0:T(8,128)(2,1)S(1)}, bf16[192,512]{1,0:T(8,128)(2,1)S(1)}, u32[]{:S(2)}, u32[]{:S(2)}) collective-permute-start(bf16[192,512]{1,0:T(8,128)(2,1)S(1)} %pad_maximum_fusion.p0), channel_id=1, source_target_pairs={{0,8},{8,0},{16,24},{24,16},{1,9},{9,1},{17,25},{25,17},{2,10},{10... | collective-permute-start | bytes 589832 | tf_op jit(solution)/shard_map/ppermute | solution.py:566
  230.3 13.0 %collective-permute-start.18 = (bf16[192,512]{1,0:T(8,128)(2,1)S(1)}, bf16[192,512]{1,0:T(8,128)(2,1)S(1)}, u32[]{:S(2)}, u32[]{:S(2)}) collective-permute-start(bf16[192,512]{1,0:T(8,128)(2,1)S(1)} %pad_maximum_fusion.p0), channel_id=1, source_target_pairs={{0,16},{8,24},{16,0},{24,8},{1,17},{9,25},{17,1},{25,9},{2,18},{10... | collective-permute-start | bytes 589832 | tf_op jit(solution)/shard_map/ppermute | solution.py:566
  232.6 10.7 %collective-permute-start.19 = (bf16[192,512]{1,0:T(8,128)(2,1)S(1)}, bf16[192,512]{1,0:T(8,128)(2,1)S(1)}, u32[]{:S(2)}, u32[]{:S(2)}) collective-permute-start(bf16[192,512]{1,0:T(8,128)(2,1)S(1)} %pad_maximum_fusion.p0), channel_id=1, source_target_pairs={{0,24},{8,16},{16,8},{24,0},{1,25},{9,17},{17,9},{25,1},{2,26},{10... | collective-permute-start | bytes 589832 | tf_op jit(solution)/shard_map/ppermute | solution.py:566
  (14 other events, 134.1 us)

commit v4 on v3

--- a/solution.py
+++ b/solution.py
@@ -16,6 +16,7 @@
 CHUNK = 512
 LANES = 128
 COST = 1
+ROWS = (0, 96, 64, 80, 160, 176)
 VMEM = 60 * 1024 * 1024
 SMALL_VMEM = 24 * 1024 * 1024
 
@@ -371,9 +372,11 @@
         copies.send(gqkv.at[rows], gqkv_out.at[pack])
     if hierarchical:
         wait(*got_rest)
-        feed_tiles(Halves(copies, ids, scratch[19:21], outs[:2]), z1, e2, eu, h, 0)
-        place = Halves(copies, ids, scratch[21:23], outs[2:])
-        attend_tiles(place, z0, o, gqkv, e1, 0, gqkv.shape[0])
+        one = Halves(copies, ids, scratch[19:21], outs[:2], x_high=True)
+        two = Halves(copies, ids, scratch[21:23], outs[2:])
+        up_tiles(one, z1, eu, 0)
+        down_tiles(two, e2, h, 0)
+        attend_tiles([one, one, two, two], z0, o, gqkv, e1, [64, 80, 64, 80], gqkv.shape[0])
     else:
         for source, target in zip((eu, e2, e1), outs):
             copies.send(source, target)
@@ -466,34 +469,37 @@
 
 
 class Halves:
-    def __init__(self, copies, ids, held, outs, z_first=False):
+    def __init__(self, copies, ids, held, outs, x_high=False):
         self.copies, self.held, self.outs = copies, held, outs
-        self.first, self.z, self.s, self.z_first = ids[0] == 0, ids[1], ids[2], z_first
-
-    def at(self, s, z):
-        s = slice(None) if s is None else s ^ self.s
-        z = slice(None) if z is None else z ^ self.z
-        return (z, s) if self.z_first else (s, z)
+        self.first, self.z, self.s, self.x_high = ids[0] == 0, ids[1], ids[2], x_high
+
+    def part(self, s):
+        if s is None:
+            return slice(None)
+        part = s ^ self.s
+        return (part & 1) * 2 + (part >> 1) if self.x_high else part
 
     def put(self, s, z, at, even, odd):
         rows = slice(at, at + even.shape[0])
-        self.held[0][*self.at(s, z), rows] = jnp.where(self.first, even, odd)
-        self.held[1][*self.at(s, z), rows] = jnp.where(self.first, odd, even)
-
-    def send(self, s, z, at):
+        self.held[0][self.part(s), z ^ self.z, rows] = jnp.where(self.first, even, odd)
+        self.held[1][self.part(s), z ^ self.z, rows] = jnp.where(self.first, odd, even)
+
+    def send(self, s, z, at, rows):
+        index = self.part(s), slice(None) if z is None else z ^ self.z, pl.ds(at, rows)
         for ref, out in zip(self.held, self.outs):
-            index = *self.at(s, z), pl.ds(at, 64)
             self.copies.send(ref.at[index], out.at[index])
 
 
-def feed_tiles(place, z1, e2, eu, h, at):
+def up_tiles(place, z1, eu, at):
     for step in range(4):
         tile = tn(z1[...], eu[:, step * CHUNK : (step + 1) * CHUNK]).astype(BF)
         for z in range(4):
             row = 128 * z
             place.put(step, z, at, tile[row : row + 64], tile[row + 64 : row + 128])
-        place.send(step, None, at)
-    at = at + 64
+        place.send(step, None, at, 64)
+
+
+def down_tiles(place, e2, h, at):
     for step in range(4):
         tile = tn(e2[...], h[:, step * CHUNK : (step + 1) * CHUNK]).astype(BF)
         for s in range(4):
@@ -501,11 +507,11 @@
             even = jnp.concatenate([upper[:, :256], lower[:, :256]], axis=1)
             odd = jnp.concatenate([upper[:, 256:], lower[:, 256:]], axis=1)
             place.put(s, step, at, even, odd)
-        place.send(None, step, at)
-
-
-def attend_tiles(place, z0, o, gqkv, e1, at, depth):
-    for step in range(4):
+        place.send(None, step, at, 64)
+
+
+def attend_tiles(places, z0, o, gqkv, e1, ats, depth):
+    for step, (place, at) in enumerate(zip(places, ats)):
         if step == 3:
             tile = tn(o[...], e1[...])
         else:
@@ -515,32 +521,34 @@
         for z in range(4):
             for s in range(4):
                 row = 128 * z + 16 * s
-                even, odd = tile[row : row + 16], tile[row + 64 : row + 80]
-                place.put(s, z, at + 16 * step, even, odd)
-    place.send(None, None, at)
+                place.put(s, z, at, tile[row : row + 16], tile[row + 64 : row + 80])
+        if step % 2:
+            place.send(None, None, at - 16, 32)
 
 
 def time_weights_kernel(ids, *rest):
     names = 8
-    shared, one, outs, scratch = rest[:names], rest[names : 2 * names], rest[16:18], rest[18:]
+    shared, single, outs, scratch = rest[:names], rest[names : 2 * names], rest[16:20], rest[20:]
     z1, eu, e2, h, z0, gqkv, o, e1 = scratch[:names]
     copies = Copies(scratch[-1])
-    place = Halves(copies, ids, scratch[8:10], outs)
+    one = Halves(copies, ids, scratch[8:10], outs[:2], x_high=True)
+    two = Halves(copies, ids, scratch[10:12], outs[2:])
     packs, tokens, _ = shared[0].shape
     have = packs * tokens
     got = []
-    for source, single, target in zip(shared, one, scratch):
+    for source, last, target in zip(shared, single, scratch):
         wide_target = target.at[pl.ds(have, tokens)]
-        if single.shape[2] < target.shape[1]:
-            wide_target = target.at[pl.ds(have, tokens), pl.ds(target.shape[1] - single.shape[2], single.shape[2])]
+        if last.shape[2] < target.shape[1]:
+            wide_target = target.at[pl.ds(have, tokens), pl.ds(target.shape[1] - last.shape[2], last.shape[2])]
         got.append(
             [copies.fetch(source.at[pack], target.at[pl.ds(pack * tokens, tokens)]) for pack in range(packs)]
-            + [copies.fetch(single.at[0], wide_target)]
+            + [copies.fetch(last.at[0], wide_target)]
         )
     wait(*got[0], *got[1], *got[2], *got[3])
-    feed_tiles(place, z1, e2, eu, h, 0)
+    up_tiles(one, z1, eu, 0)
+    down_tiles(two, e2, h, 0)
     wait(*got[4], *got[5], *got[6], *got[7])
-    attend_tiles(place, z0, o, gqkv, e1, 128, have)
+    attend_tiles([one, one, two, two], z0, o, gqkv, e1, [64, 80, 64, 80], have)
     copies.finish()
 
 
@@ -573,17 +581,22 @@
     return total.astype(BF)
 
 
-def core_sum(mine, got, *note):
-    return [add(mine[d], got[d], *note) for d in range(1, 4)], (mine[0], got[0])
-
-
-def stream_total(parts, own):
-    return add(*own, *[swap(part, "stream", 4, d + 1) for d, part in enumerate(parts)])
-
-
-def stream_sum(parts, own):
-    got = [swap(part, "stream", 4, d + 1) for d, part in enumerate(parts)]
-    return [add(*[term[d] for term in (*own, *got)]) for d in range(4)]
+def far_parts(mine, got, note):
+    return [add(a[2:], b[2:], note) for a, b in zip(mine, got)]
+
+
+def near_parts(mine, got, far):
+    halves = [swap(far[0], "stream", 4, 1), swap(far[1], "stream", 4, 2)]
+    return halves, [add(a[1], b[1], half[1]) for a, b, half in zip(mine, got, halves)]
+
+
+def stream_rows(mine, got, halves, near):
+    last = [swap(near[0], "stream", 4, 2), swap(near[1], "stream", 4, 1)]
+    terms = list(zip(mine, got, halves, last))
+    return [
+        jnp.concatenate([add(a[0][d], b[0][d], half[0][d], end[d]) for a, b, half, end in terms])
+        for d in range(4)
+    ]
 
 
 def z_sum(rows):
@@ -607,12 +620,8 @@
     )(array)
 
 
-def z_scatter(rows):
-    groups = [[0, 2, 4, 6], [1, 3, 5, 7]]
-    got = lax.all_to_all(
-        rows, "tm", split_axis=0, concat_axis=0, tiled=True, axis_index_groups=groups
-    )
-    return add(*[got[z] for z in range(4)])
+def stream_total(parts, own):
+    return add(*own, *[swap(part, "stream", 4, d + 1) for d, part in enumerate(parts)])
 
 
 def stream_total(parts, own):
@@ -624,38 +633,10 @@
     return [add(*[term[d] for term in (*own, *got)]) for d in range(4)]
 
 
-def z_sum(rows):
-    return add(rows[0], *[swap(rows[d], "tm", 8, 2 * d) for d in range(1, 4)])
-
-
-def gather_parts(final):
-    return [final] + [swap(final, "stream", 4, d) for d in range(1, 4)]
-
-
-def marker(array):
-    def kernel(source, out):
-        out[...] = jnp.zeros_like(out)
-
-    return pl.pallas_call(
-        kernel,
-        out_shape=jax.ShapeDtypeStruct((1, CHUNK), F32),
-        in_specs=[pl.BlockSpec(memory_space=pl.ANY)],
-        out_specs=pl.BlockSpec(memory_space=pltpu.VMEM),
-        cost_estimate=pl.CostEstimate(flops=10**12, bytes_accessed=10**8, transcendentals=0),
-    )(array)
-
-
-def stream_total(parts, own):
-    return add(*own, *[swap(part, "stream", 4, d + 1) for d, part in enumerate(parts)])
-
-
-def stream_total(parts, own):
-    return add(*own, *[swap(part, "stream", 4, d + 1) for d, part in enumerate(parts)])
-
-
-def stream_sum(parts, own):
-    got = [swap(part, "stream", 4, d + 1) for d, part in enumerate(parts)]
-    return [add(*[term[d] for term in (*own, *got)]) for d in range(4)]
+def halved_sum(mine, got, far, first, second):
+    half = swap(far, "stream", 4, first)
+    near = swap(add(mine[1], got[1], half[1]), "stream", 4, second)
+    return [(mine[0][d], got[0][d], half[0][d], near[d]) for d in range(4)]
 
 
 def z_sum(rows):
@@ -715,41 +696,26 @@
     return jnp.sum(jnp.where(row == lane, vector[...], 0.0), axis=1, keepdims=True)
 
 
-def finish_feed(ids, pieces, at, w_up, scale, scale_grad, up_grad, down_grad):
-    factor = own_rows(ids, scale)
-    for d, piece in enumerate(pieces):
+def finish_kernel(ids, p0, p1, p2, p3, w_up, scale, w_in, gain, *outs):
+    scale_grad, up_grad, down_grad, gain_grad, in_grad, out_grad = outs
+    up_at, down_at, *in_at, out_at = ROWS
+    for d, piece in enumerate((p0, p1, p2, p3)):
         s = ids[2] ^ d
-        up_grad[:, pl.ds(pl.multiple_of(512 * s, 512), 512)] = piece[at : at + 64].astype(F32)
-        lower = piece[at + 64 : at + 128].astype(F32)
+        up_grad[:, pl.ds(pl.multiple_of(512 * s, 512), 512)] = piece[up_at : up_at + 64].astype(F32)
+        lower = piece[down_at : down_at + 64].astype(F32)
         whole = jnp.concatenate([lower[:, :256], lower[:, 256:]], axis=0)
         down_grad[:, pl.ds(pl.multiple_of(128 * s, 128), 128)] = whole.T
-    total = up_grad[...]
-    scale_grad[...] = as_row(jnp.sum(total * w_up[...].astype(F32), axis=1, keepdims=True))
-    up_grad[...] = total * factor
-
-
-def finish_attend(ids, pieces, at, w_in, gain, gain_grad, in_grad, out_grad):
-    factor = own_rows(ids, gain)
-    for d, piece in enumerate(pieces):
-        rows = pl.ds(pl.multiple_of(16 * (ids[2] ^ d), 16), 16)
-        for third in range(3):
-            in_grad[rows, 512 * third : 512 * third + 512] = piece[
-                at + 16 * third : at + 16 * third + 16
-            ].astype(F32)
-        out_grad[rows, :] = piece[at + 48 : at + 64].astype(F32)
-    total = in_grad[...]
-    gain_grad[...] = as_row(jnp.sum(total * w_in[...].astype(F32), axis=1, keepdims=True))
-    in_grad[...] = total * factor
-
-
-def finish_space_kernel(ids, p0, p1, p2, p3, *rest):
-    pieces, outs = (p0, p1, p2, p3), rest[4:]
-    finish_feed(ids, pieces, 0, *rest[0:2], *outs[0:3])
-    finish_attend(ids, pieces, 128, *rest[2:4], *outs[3:6])
-
-
-def finish_time_kernel(ids, p0, p1, p2, p3, *rest):
-    finish_space_kernel(ids, p0, p1, p2, p3, *rest)
+        rows = pl.ds(pl.multiple_of(16 * s, 16), 16)
+        for third, at in enumerate(in_at):
+            in_grad[rows, 512 * third : 512 * third + 512] = piece[at : at + 16].astype(F32)
+        out_grad[rows, :] = piece[out_at : out_at + 16].astype(F32)
+    for grad, weight, factor, vector_grad in (
+        (up_grad, w_up, scale, scale_grad),
+        (in_grad, w_in, gain, gain_grad),
+    ):
+        total = grad[...]
+        vector_grad[...] = as_row(jnp.sum(total * weight[...].astype(F32), axis=1, keepdims=True))
+        grad[...] = total * own_rows(ids, factor)
 
 
 def finish_call(kernel, ids, pieces, pairs, outs):
@@ -928,18 +894,19 @@
     time_shared = [tz1, teu, te2, th, tz0, tgqkv, to, te1]
     time_one = [tz1_one, teu_one, te2_one, th_one, tz0_one, tgv_one, to_one, te1_one]
     if hierarchical:
-        parts_shape = ((4, 4, 192, CHUNK), BF)
-        mine, other = manual_call(
+        parts_shapes = [((4, 4, 96, CHUNK), BF)] * 4
+        time_terms = manual_call(
             time_weights_kernel,
-            jnp.stack([ids[0], jnp.int32(0), ids[2]]),
+            ids,
             time_shared + time_one,
-            [parts_shape] * 2,
-            [((everything, a.shape[2]), BF) for a in time_shared] + [parts_shape] * 2,
-            8 * packs + 18,
+            parts_shapes,
+            [((everything, a.shape[2]), BF) for a in time_shared] + parts_shapes,
+            8 * packs + 20,
             flops=packs * flops,
         )
-        time_parts, time_own = core_sum(mine, swap(other, "tm", 8, 1), marker(g0_moved))
-        held_back = tuple(time_parts)
+        time_got = [swap(other, "tm", 8, 1) for other in time_terms[1::2]]
+        time_far = far_parts(time_terms[::2], time_got, marker(g0_moved))
+        held_back = time_far
     else:
         grad_one = jnp.pad(tgv_one, ((0, 0), (0, 0), (2 * width, 0)))
         joined = [joint(a, b) for a, b in zip(time_shared, time_one[:5] + [grad_one] + time_one[6:])]
@@ -949,7 +916,7 @@
     shared_w, shared_3 = (some,) + rows_w, (some,) + rows_3
     space_one = [sz1_one, seu_one, sh_one, se2_one, sz0_one, sgqkv_one, so_one, se1_one]
     whole_shapes = [((everything, a.shape[2]), BF) for a in space_one]
-    parts_shapes = [((4, 4, 128, CHUNK), BF)] * 2 + [((4, 4, 64, CHUNK), BF)] * 2
+    parts_shapes = [((4, 4, 96, CHUNK), BF)] * 4
     sg1, sgqkv, *weights = manual_call(
         functools.partial(space_kernel, hierarchical),
         ids,
@@ -978,6 +945,16 @@
         after=held_back,
         flops=2 * packs * flops,
     )
+    held_back = ()
+    if hierarchical:
+        time_got, sgqkv = lax.optimization_barrier((time_got, sgqkv))
+        time_mine = time_terms[::2]
+        time_halves, time_near = near_parts(time_mine, time_got, time_far)
+        mine = weights[::2]
+        got = [swap(other, "tm", 8, 1) for other in weights[1::2]]
+        far = far_parts(mine, got, marker(time_near[1]))
+        far, time_halves = lax.optimization_barrier((far, time_halves))
+        held_back = far
     input_grad, result = shared.call(
         space_back_in,
         [
@@ -991,27 +968,15 @@
         ],
         [("pack", frames.shape, F32, input_grad), ("pack", frames.shape, F32, result)],
         flops=flops // 4,
+        after=held_back,
     )
     if hierarchical:
-        feed, feed_other, attend_mine, attend_other = weights
-        feed_got = swap(feed_other, "tm", 8, 1)
-        attend_got = swap(attend_other, "tm", 8, 1)
-        time_own, input_grad = lax.optimization_barrier((time_own, input_grad))
-        time_rows = stream_total(time_parts, time_own)
-        note = marker(time_rows)
-        feed_parts = [add(feed[d], feed_got[d], note) for d in range(1, 4)]
-        attend_got, feed_parts[0] = lax.optimization_barrier((attend_got, feed_parts[0]))
-        attend_part = add(attend_mine[2:], attend_got[2:])
-        rows = stream_sum(feed_parts, (feed[0], feed_got[0]))
-        half = swap(attend_part, "stream", 4, 2)
-        got, rows[1] = lax.optimization_barrier((attend_got[1], rows[1]))
-        near = swap(add(attend_mine[1], got, half[1]), "stream", 4, 1)
-        feed_final = z_sum(rows)
-        own, feed_final = lax.optimization_barrier(((attend_mine[0], attend_got[0]), feed_final))
-        attend_rows = [add(*[term[d] for term in (*own, half[0], near)]) for d in range(4)]
-        final = jnp.concatenate([feed_final, z_sum(attend_rows)])
+        time_rows = stream_rows(time_mine, time_got, time_halves, time_near)
+        time_final = z_sum(time_rows)
+        got, time_final, input_grad = lax.optimization_barrier((got, time_final, input_grad))
+        final = z_sum(stream_rows(mine, got, *near_parts(mine, got, far)))
         grads = finish_call(
-            finish_space_kernel,
+            finish_kernel,
             ids,
             gather_parts(final),
             [(space_up, space_scale), (space_input, space_gain)],
@@ -1019,9 +984,9 @@
         )
         feed_grads, attend_grads = grads[:3], grads[3:]
         time_grads = finish_call(
-            finish_time_kernel,
+            finish_kernel,
             ids,
-            gather_parts(z_scatter(time_rows)),
+            gather_parts(time_final),
             [(time_up, time_scale), (time_input, time_gain)],
             feed_shapes + attend_shapes,
         )

time: 250 us -> 231 us (0.924)
  the two profiles are of different devices: /device:TPU:0 before, /device:TPU:16 now
where the time goes in v4:
time: 231 us; the launch traced here: 227 us
  Pallas kernels  113 us (49%)
  starting transfers between devices  50 us (22%)
  waiting for transfers between devices  38.2 us (17%)
  other arithmetic  20.6 us (9%)
  local copies, waits for them, and re-layouts  3.16 us (1%)
    pallas_call x4, Pallas kernels, call(): pl.pallas_call(without(kernel, len(scalars) + len(args), unread), out_sha...  70.5 us
    pallas_call x2, Pallas kernels, manual_call(): pl.pallas_call(without(kernel, 1 + len(args), len(after)), out_shape=[jax...  35 us
    ppermute x24, waiting for transfers between devices, swap(): return lax.ppermute(array, axis, [(i, i ^ mask) for i in range(size)])  34 us
    all_to_all x4, starting transfers between devices, exchange(): return lax.all_to_all(array, 'tm', split_axis=0, concat_axis=0, tiled=True)  25.5 us
    ppermute x24, starting transfers between devices, swap(): return lax.ppermute(array, axis, [(i, i ^ mask) for i in range(size)])  24.5 us
    convert_element_type x12, other arithmetic, add(): return total.astype(BF)  18.6 us
  transfers between devices with their start and end apart: 28, of which 11 were waited for; matrix products, arithmetic and copies ran while one was open for 8% of the time, Pallas kernels for 36%

profile of v4, /device:TPU:16, one launch (start us, length us, event | category | flops | bytes accessed | tf_op | source)
XLA Modules:
  0.0 226.7 jit_solution(14122002495951220234)
XLA Ops:
  0.6 2.8 %shard_map.254.refs_8_ = bf16[8,3,32,512]{3,2,1,0:T(8,128)(2,1)} custom-call(s32[4,8]{1,0:T(4,128)} %refs_0_.7, bf16[4,1,256,512]{3,2,1,0:T(8,128)(2,1)} %refs_2_.2), custom_call_target="tpu_custom_call" | custom-call | tf_op jit(solution)/shard_map/pallas_call | solution.py:757
  3.5 5.2 %all-to-all-start = ((bf16[8,3,32,512]{3,2,1,0:T(8,128)(2,1)}), bf16[8,3,32,512]{3,2,1,0:T(8,128)(2,1)S(1)}, u32[]{:S(2)}, u32[]{:S(2)}) async-start(bf16[8,3,32,512]{3,2,1,0:T(8,128)(2,1)} %shard_map.254.refs_8_), calls=%async_computation | async-start | bytes 1572864 | tf_op jit(solution)/shard_map/all_to_all | solution.py:804
  8.7 16.9 %shard_map.255 = (bf16[8,3,32,512]{3,2,1,0:T(8,128)(2,1)}, bf16[3,256,512]{2,1,0:T(8,128)(2,1)}, f32[3,256,128]{2,1,0:T(8,128)}, bf16[3,256,1536]{2,1,0:T(8,128)...) custom-call(s32[4,8]{1,0:T(4,128)} %refs_0_.7, ...), custom_call_target="tpu_custom_call" | custom-call | flops 4831838208 | bytes 8130560 | tf_op jit(solution)/shard_map/pallas_call | solution.py:451
  26.4 6.9 %all-to-all-start.1 = ((bf16[8,3,32,512]{3,2,1,0:T(8,128)(2,1)}), bf16[8,3,32,512]{3,2,1,0:T(8,128)(2,1)S(1)}, u32[]{:S(2)}, u32[]{:S(2)}) async-start(bf16[8,3,32,512]{3,2,1,0:T(8,128)(2,1)} %get-tuple-element.92.refs_15_), calls=%async_computation.1 | async-start | bytes 1572864 | tf_op jit(solution)/shard_map/all_to_all | solution.py:804
  33.4 18.9 %shard_map.256 = (f32[4,1,256,512]{3,2,1,0:T(8,128)}, f32[4,1,256,512]{3,2,1,0:T(8,128)}, bf16[1,256,512]{2,1,0:T(8,128)(2,1)}, bf16[1,256,512]{2,1,0:T(8,128)(2...) custom-call(s32[4,8]{1,0:T(4,128)} %refs_0_.7, ...), custom_call_target="tpu_custom_call" | custom-call | flops 9663676416 | bytes 15474688 | tf_op jit(solution)/shard_map/pallas_call | solution.py:451
  53.2 27.3 %shard_map.257 = (bf16[8,3,32,512]{3,2,1,0:T(8,128)(2,1)}, bf16[8,3,32,512]{3,2,1,0:T(8,128)(2,1)}, bf16[3,256,512]{2,1,0:T(8,128)(2,1)}, bf16[3,256,1536]{2,1,0...) custom-call(s32[4,8]{1,0:T(4,128)} %refs_0_.7, ...), custom_call_target="tpu_custom_call" | custom-call | flops 14495514624 | bytes 8130560 | tf_op jit(solution)/shard_map/pallas_call | solution.py:451
  80.5 5.5 %all-to-all-start.2 = ((bf16[8,3,32,512]{3,2,1,0:T(8,128)(2,1)}), bf16[8,3,32,512]{3,2,1,0:T(8,128)(2,1)S(1)}, u32[]{:S(2)}, u32[]{:S(2)}) async-start(bf16[8,3,32,512]{3,2,1,0:T(8,128)(2,1)} %get-tuple-element.115), calls=%async_computation.2 | async-start | bytes 1572864 | tf_op jit(solution)/shard_map/all_to_all | solution.py:804
  86.6 13.1 %shard_map.258 = (bf16[4,4,96,512]{3,2,1,0:T(8,128)(2,1)}, bf16[4,4,96,512]{3,2,1,0:T(8,128)(2,1)}, bf16[4,4,96,512]{3,2,1,0:T(8,128)(2,1)}, bf16[4,4,96,512]{3,2,1,0:T(8,128)(2,1)}) custom-call(s32[3]{0:T(128)} %pad_add_fusion.refs_0_.ids, bf16[3,256,512]{2,1,0:T(8,128)(2,1)} %get-tuple-element.95.refs_1_, bf16[3,256,2048]{2,1,0:T(8,128)(2,1)} %get-tuple-element.96.refs_2_, ...), custom_call_target="tpu_custom_call" | custom-call | flops 6442450944 | tf_op jit(solution)/shard_map/pallas_call | solution.py:557
  100.2 3.5 %all-to-all-done.2.source.refs_3_ = bf16[8,3,32,512]{3,2,1,0:T(8,128)(2,1)S(1)} async-done(((bf16[8,3,32,512]{3,2,1,0:T(8,128)(2,1)}), bf16[8,3,32,512]{3,2,1,0:T(8,128)(2,1)S(1)}, u32[]{:S(2)}, u32[]{:S(2)}) %all-to-all-start.2) | async-done | bytes 786464 | tf_op jit(solution)/shard_map/all_to_all | solution.py:804
  105.2 7.9 %all-to-all-start.3 = ((bf16[8,3,32,512]{3,2,1,0:T(8,128)(2,1)}), bf16[8,3,32,512]{3,2,1,0:T(8,128)(2,1)}, u32[]{:S(2)}, u32[]{:S(2)}) async-start(bf16[8,3,32,512]{3,2,1,0:T(8,128)(2,1)} %get-tuple-element.137), calls=%async_computation.3 | async-start | bytes 1572864 | tf_op jit(solution)/shard_map/all_to_all | solution.py:804
  113.1 3.0 %add_convert_fusion.2 = (bf16[2,4,96,512]{3,2,1,0:T(8,128)(2,1)S(1)}, bf16[2,4,96,512]{3,2,1,0:T(8,128)(2,1)}) fusion(bf16[4,4,96,512]{3,2,1,0:T(8,128)(2,1)} %collective-permute-done.1, bf16[4,4,96,512]{3,2,1,0:T(8,128)(2,1)} %get-tuple-element.132, f32[512]{0:T(512)S(1)} %bitcast.148, bf16[4,4,96,512]{3,2,1,0:T(8,128)(2,1)} %collective-permute-done, ...), kind=kLoop, calls=%fused_computation.2 | loop fusion | flops 3932160 | bytes 4720640 | tf_op jit(solution)/shard_map/convert_element_type | solution.py:581
  119.1 21.9 %shard_map.260 = (f32[3,256,512]{2,1,0:T(8,128)}, bf16[3,256,1536]{2,1,0:T(8,128)(2,1)}, bf16[4,4,96,512]{3,2,1,0:T(8,128)(2,1)}, bf16[4,4,96,512]{3,2,1,0:T(8,1...) custom-call(s32[3]{0:T(128)} %pad_add_fusion.refs_0_.ids, f32[1,512]{1,0:T(1,128)} %bitcast.145, ...), custom_call_target="tpu_custom_call" | custom-call | flops 12884901888 | tf_op jit(solution)/shard_map/pallas_call | solution.py:557
  142.5 2.0 fusion.source
  148.1 2.2 add_convert_fusion
  150.3 1.6 collective-permute-start.11
  151.9 5.7 %collective-permute-done.7 = bf16[4,96,512]{2,1,0:T(8,128)(2,1)S(1)} collective-permute-done((bf16[4,96,512]{2,1,0:T(8,128)(2,1)S(1)}, bf16[4,96,512]{2,1,0:T(8,128)(2,1)S(1)}, u32[]{:S(2)}, u32[]{:S(2)}) %collective-permute-start.7) | collective-permute-done | bytes 393248 | tf_op jit(solution)/shard_map/ppermute | solution.py:574
  159.0 1.5 fusion.19
  160.5 1.5 collective-permute-start.8
  166.0 7.3 %shard_map.262 = (f32[4,1,256,512]{3,2,1,0:T(8,128)}, f32[4,1,256,512]{3,2,1,0:T(8,128)}) custom-call(s32[4,8]{1,0:T(4,128)} %refs_0_.7, bf16[3,256,1536]{2,1,0:T(8,128)(2,1)} %get-tuple-element.134.refs_1_, bf16[512,1536]{1,0:T(8,128)(2,1)} %w_in.2, f32[1,512]{1,0:T(1,128)} %bitcast.135, ...), custom_call_target="tpu_custom_call", output_to_operand_aliasing={{0}: (8, {}), {1}: (9, {})} | custom-call | flops 1207959552 | bytes 13240320 | tf_op jit(solution)/shard_map/pallas_call | solution.py:451
  173.3 3.0 %collective-permute-done.9 = bf16[192,512]{1,0:T(8,128)(2,1)} collective-permute-done((bf16[192,512]{1,0:T(8,128)(2,1)}, bf16[192,512]{1,0:T(8,128)(2,1)}, u32[]{:S(2)}, u32[]{:S(2)}) %collective-permute-start.9) | collective-permute-done | bytes 196640 | tf_op jit(solution)/shard_map/ppermute | solution.py:574
  176.4 4.5 %collective-permute-done.10 = bf16[192,512]{1,0:T(8,128)(2,1)} collective-permute-done((bf16[192,512]{1,0:T(8,128)(2,1)}, bf16[192,512]{1,0:T(8,128)(2,1)}, u32[]{:S(2)}, u32[]{:S(2)}) %collective-permute-start.10) | collective-permute-done | bytes 196640 | tf_op jit(solution)/shard_map/ppermute | solution.py:574
  186.7 6.1 %collective-permute-done.12 = bf16[4,96,512]{2,1,0:T(8,128)(2,1)S(1)} collective-permute-done((bf16[4,96,512]{2,1,0:T(8,128)(2,1)S(1)}, bf16[4,96,512]{2,1,0:T(8,128)(2,1)S(1)}, u32[]{:S(2)}, u32[]{:S(2)}) %collective-permute-start.12) | collective-permute-done | bytes 393248 | tf_op jit(solution)/shard_map/ppermute | solution.py:574
  192.8 1.5 fusion.11
  194.4 1.5 fusion.10
  196.1 2.2 collective-permute-start.16
  199.7 2.5 %collective-permute-start.23 = (bf16[192,512]{1,0:T(8,128)(2,1)S(1)}, bf16[192,512]{1,0:T(8,128)(2,1)S(1)}, u32[]{:S(2)}, u32[]{:S(2)}) collective-permute-start(bf16[192,512]{1,0:T(8,128)(2,1)S(1)} %add_convert_fusion.9.p0), channel_id=1, source_target_pairs={{0,24},{8,16},{16,8},{24,0},{1,25},{9,17},{17,9},{25,1},{2,26},{10... | collective-permute-start | bytes 589832 | tf_op jit(solution)/shard_map/ppermute | solution.py:574
  205.4 4.8 %collective-permute-done.16 = bf16[192,512]{1,0:T(8,128)(2,1)S(1)} collective-permute-done((bf16[192,512]{1,0:T(8,128)(2,1)S(1)}, bf16[192,512]{1,0:T(8,128)(2,1)S(1)}, u32[]{:S(2)}, u32[]{:S(2)}) %collective-permute-start.16) | collective-permute-done | bytes 196640 | tf_op jit(solution)/shard_map/ppermute | solution.py:574
  210.2 3.9 %collective-permute-done.17 = bf16[192,512]{1,0:T(8,128)(2,1)S(1)} collective-permute-done((bf16[192,512]{1,0:T(8,128)(2,1)S(1)}, bf16[192,512]{1,0:T(8,128)(2,1)S(1)}, u32[]{:S(2)}, u32[]{:S(2)}) %collective-permute-start.17) | collective-permute-done | bytes 196640 | tf_op jit(solution)/shard_map/ppermute | solution.py:574
  214.3 2.5 %collective-permute-start.20 = (bf16[192,512]{1,0:T(8,128)(2,1)S(1)}, bf16[192,512]{1,0:T(8,128)(2,1)S(1)}, u32[]{:S(2)}, u32[]{:S(2)}) collective-permute-start(bf16[192,512]{1,0:T(8,128)(2,1)S(1)} %add_convert_fusion.8.p0), channel_id=1, source_target_pairs={{0,24},{8,16},{16,8},{24,0},{1,25},{9,17},{17,9},{25,1},{2,26},{10... | collective-permute-start | bytes 589832 | tf_op jit(solution)/shard_map/ppermute | solution.py:574
  217.9 2.0 shard_map.264
  219.8 3.1 %collective-permute-done.20.p3 = bf16[192,512]{1,0:T(8,128)(2,1)S(1)} collective-permute-done((bf16[192,512]{1,0:T(8,128)(2,1)S(1)}, bf16[192,512]{1,0:T(8,128)(2,1)S(1)}, u32[]{:S(2)}, u32[]{:S(2)}) %collective-permute-start.20) | collective-permute-done | bytes 196640 | tf_op jit(solution)/shard_map/ppermute | solution.py:574
  224.5 1.9 shard_map.263
  (98 shorter events, 31.0 us)
Async XLA Ops:
  3.5 22.9 %all-to-all-start = ((bf16[8,3,32,512]{3,2,1,0:T(8,128)(2,1)}), bf16[8,3,32,512]{3,2,1,0:T(8,128)(2,1)S(1)}, u32[]{:S(2)}, u32[]{:S(2)}) async-start(bf16[8,3,32,512]{3,2,1,0:T(8,128)(2,1)} %shard_map.254.refs_8_), calls=%async_computation | async-start | bytes 1572864 | tf_op jit(solution)/shard_map/all_to_all | solution.py:804
  26.4 25.9 %copy-start.14 = (bf16[8,3,32,512]{3,2,1,0:T(8,128)(2,1)}, bf16[8,3,32,512]{3,2,1,0:T(8,128)(2,1)S(1)}, u32[]{:S(2)}) copy-start(bf16[8,3,32,512]{3,2,1,0:T(8,128)(2,1)S(1)} %all-to-all-done.refs_2_) | copy-start | bytes 2359300
  26.4 25.9 %all-to-all-start.1 = ((bf16[8,3,32,512]{3,2,1,0:T(8,128)(2,1)}), bf16[8,3,32,512]{3,2,1,0:T(8,128)(2,1)S(1)}, u32[]{:S(2)}, u32[]{:S(2)}) async-start(bf16[8,3,32,512]{3,2,1,0:T(8,128)(2,1)} %get-tuple-element.92.refs_15_), calls=%async_computation.1 | async-start | bytes 1572864 | tf_op jit(solution)/shard_map/all_to_all | solution.py:804
  80.5 23.2 %all-to-all-start.2 = ((bf16[8,3,32,512]{3,2,1,0:T(8,128)(2,1)}), bf16[8,3,32,512]{3,2,1,0:T(8,128)(2,1)S(1)}, u32[]{:S(2)}, u32[]{:S(2)}) async-start(bf16[8,3,32,512]{3,2,1,0:T(8,128)(2,1)} %get-tuple-element.115), calls=%async_computation.2 | async-start | bytes 1572864 | tf_op jit(solution)/shard_map/all_to_all | solution.py:804
  99.7 13.4 %collective-permute-start = (bf16[4,4,96,512]{3,2,1,0:T(8,128)(2,1)}, bf16[4,4,96,512]{3,2,1,0:T(8,128)(2,1)}, u32[]{:S(2)}, u32[]{:S(2)}) collective-permute-start(bf16[4,4,96,512]{3,2,1,0:T(8,128)(2,1)} %get-tuple-element.111), channel_id=1, source_target_pairs={{0,1},{1,0},{2,3},{3,2},{4,5},{5,4},{6,7},{7,6},{8,9},{9,8},{10,11... | collective-permute-start | bytes 4718600 | tf_op jit(solution)/shard_map/ppermute | solution.py:574
  99.9 13.2 %collective-permute-start.1 = (bf16[4,4,96,512]{3,2,1,0:T(8,128)(2,1)}, bf16[4,4,96,512]{3,2,1,0:T(8,128)(2,1)}, u32[]{:S(2)}, u32[]{:S(2)}) collective-permute-start(bf16[4,4,96,512]{3,2,1,0:T(8,128)(2,1)} %get-tuple-element.112), channel_id=1, source_target_pairs={{0,1},{1,0},{2,3},{3,2},{4,5},{5,4},{6,7},{7,6},{8,9},{9,8},{10,11... | collective-permute-start | bytes 4718600 | tf_op jit(solution)/shard_map/ppermute | solution.py:574
  105.2 60.8 %all-to-all-start.3 = ((bf16[8,3,32,512]{3,2,1,0:T(8,128)(2,1)}), bf16[8,3,32,512]{3,2,1,0:T(8,128)(2,1)}, u32[]{:S(2)}, u32[]{:S(2)}) async-start(bf16[8,3,32,512]{3,2,1,0:T(8,128)(2,1)} %get-tuple-element.137), calls=%async_computation.3 | async-start | bytes 1572864 | tf_op jit(solution)/shard_map/all_to_all | solution.py:804
  116.1 25.5 %collective-permute-start.3 = (bf16[2,4,96,512]{3,2,1,0:T(8,128)(2,1)S(1)}, bf16[2,4,96,512]{3,2,1,0:T(8,128)(2,1)S(1)}, u32[]{:S(2)}, u32[]{:S(2)}) collective-permute-start(bf16[2,4,96,512]{3,2,1,0:T(8,128)(2,1)S(1)} %get-tuple-element.186.refs_23_), channel_id=1, source_target_pairs={{0,16},{8,24},{16,0},{24,8},{1,17},{9,25},{17,1},{25,9},{2,18},{10... | collective-permute-start | bytes 2359304 | tf_op jit(solution)/shard_map/ppermute | solution.py:574
  117.6 28.5 %collective-permute-start.5 = (bf16[2,4,96,512]{3,2,1,0:T(8,128)(2,1)}, bf16[2,4,96,512]{3,2,1,0:T(8,128)(2,1)}, u32[]{:S(2)}, u32[]{:S(2)}) collective-permute-start(bf16[2,4,96,512]{3,2,1,0:T(8,128)(2,1)} %get-tuple-element.187.refs_22_), channel_id=1, source_target_pairs={{0,8},{8,0},{16,24},{24,16},{1,9},{9,1},{17,25},{25,17},{2,10},{10... | collective-permute-start | bytes 2359304 | tf_op jit(solution)/shard_map/ppermute | solution.py:574
  141.1 7.0 %collective-permute-start.2 = (bf16[4,4,96,512]{3,2,1,0:T(8,128)(2,1)}, bf16[4,4,96,512]{3,2,1,0:T(8,128)(2,1)}, u32[]{:S(2)}, u32[]{:S(2)}) collective-permute-start(bf16[4,4,96,512]{3,2,1,0:T(8,128)(2,1)} %get-tuple-element.141), channel_id=1, source_target_pairs={{0,1},{1,0},{2,3},{3,2},{4,5},{5,4},{6,7},{7,6},{8,9},{9,8},{10,11... | collective-permute-start | bytes 4718600 | tf_op jit(solution)/shard_map/ppermute | solution.py:574
  141.2 6.9 %collective-permute-start.4 = (bf16[4,4,96,512]{3,2,1,0:T(8,128)(2,1)}, bf16[4,4,96,512]{3,2,1,0:T(8,128)(2,1)}, u32[]{:S(2)}, u32[]{:S(2)}) collective-permute-start(bf16[4,4,96,512]{3,2,1,0:T(8,128)(2,1)} %get-tuple-element.144), channel_id=1, source_target_pairs={{0,1},{1,0},{2,3},{3,2},{4,5},{5,4},{6,7},{7,6},{8,9},{9,8},{10,11... | collective-permute-start | bytes 4718600 | tf_op jit(solution)/shard_map/ppermute | solution.py:574
  145.6 12.0 %collective-permute-start.7 = (bf16[4,96,512]{2,1,0:T(8,128)(2,1)S(1)}, bf16[4,96,512]{2,1,0:T(8,128)(2,1)S(1)}, u32[]{:S(2)}, u32[]{:S(2)}) collective-permute-start(bf16[4,96,512]{2,1,0:T(8,128)(2,1)S(1)} %copy-done.19), channel_id=1, source_target_pairs={{0,8},{8,0},{16,24},{24,16},{1,9},{9,1},{17,25},{25,17},{2,10},{10... | collective-permute-start | bytes 1179656 | tf_op jit(solution)/shard_map/ppermute | solution.py:574
  147.5 11.5 %collective-permute-start.6 = (bf16[4,96,512]{2,1,0:T(8,128)(2,1)S(1)}, bf16[4,96,512]{2,1,0:T(8,128)(2,1)S(1)}, u32[]{:S(2)}, u32[]{:S(2)}) collective-permute-start(bf16[4,96,512]{2,1,0:T(8,128)(2,1)S(1)} %fusion.1), channel_id=1, source_target_pairs={{0,16},{8,24},{16,0},{24,8},{1,17},{9,25},{17,1},{25,9},{2,18},{10... | collective-permute-start | bytes 1179656 | tf_op jit(solution)/shard_map/ppermute | solution.py:574
  150.3 31.7 %collective-permute-start.11 = (bf16[2,4,96,512]{3,2,1,0:T(8,128)(2,1)S(1)}, bf16[2,4,96,512]{3,2,1,0:T(8,128)(2,1)}, u32[]{:S(2)}, u32[]{:S(2)}) collective-permute-start(bf16[2,4,96,512]{3,2,1,0:T(8,128)(2,1)S(1)} %get-tuple-element.145.refs_10_), channel_id=1, source_target_pairs={{0,8},{8,0},{16,24},{24,16},{1,9},{9,1},{17,25},{25,17},{2,10},{10... | collective-permute-start | bytes 2359304 | tf_op jit(solution)/shard_map/ppermute | solution.py:574
  160.5 12.8 %collective-permute-start.8 = (bf16[192,512]{1,0:T(8,128)(2,1)S(1)}, bf16[192,512]{1,0:T(8,128)(2,1)}, u32[]{:S(2)}, u32[]{:S(2)}) collective-permute-start(bf16[192,512]{1,0:T(8,128)(2,1)S(1)} %pad_maximum_fusion), channel_id=1, source_target_pairs={{0,2},{1,3},{2,0},{3,1},{4,6},{5,7},{6,4},{7,5},{8,10},{9,11},{10,... | collective-permute-start | bytes 589832 | tf_op jit(solution)/shard_map/ppermute | solution.py:574
  162.8 13.6 %collective-permute-start.9 = (bf16[192,512]{1,0:T(8,128)(2,1)}, bf16[192,512]{1,0:T(8,128)(2,1)}, u32[]{:S(2)}, u32[]{:S(2)}) collective-permute-start(bf16[192,512]{1,0:T(8,128)(2,1)} %pad_maximum_fusion.1), channel_id=1, source_target_pairs={{0,4},{1,5},{2,6},{3,7},{4,0},{5,1},{6,2},{7,3},{8,12},{9,13},{10,... | collective-permute-start | bytes 589832 | tf_op jit(solution)/shard_map/ppermute | solution.py:574
  163.3 20.7 %collective-permute-start.13 = (bf16[2,4,96,512]{3,2,1,0:T(8,128)(2,1)S(1)}, bf16[2,4,96,512]{3,2,1,0:T(8,128)(2,1)}, u32[]{:S(2)}, u32[]{:S(2)}) collective-permute-start(bf16[2,4,96,512]{3,2,1,0:T(8,128)(2,1)S(1)} %get-tuple-element.146.refs_11_), channel_id=1, source_target_pairs={{0,16},{8,24},{16,0},{24,8},{1,17},{9,25},{17,1},{25,9},{2,18},{10... | collective-permute-start | bytes 2359304 | tf_op jit(solution)/shard_map/ppermute | solution.py:574
  164.5 16.3 %collective-permute-start.10 = (bf16[192,512]{1,0:T(8,128)(2,1)}, bf16[192,512]{1,0:T(8,128)(2,1)}, u32[]{:S(2)}, u32[]{:S(2)}) collective-permute-start(bf16[192,512]{1,0:T(8,128)(2,1)} %pad_maximum_fusion.2), channel_id=1, source_target_pairs={{0,6},{1,7},{2,4},{3,5},{4,2},{5,3},{6,0},{7,1},{8,14},{9,15},{10,... | collective-permute-start | bytes 589832 | tf_op jit(solution)/shard_map/ppermute | solution.py:574
  183.4 9.4 %collective-permute-start.12 = (bf16[4,96,512]{2,1,0:T(8,128)(2,1)S(1)}, bf16[4,96,512]{2,1,0:T(8,128)(2,1)S(1)}, u32[]{:S(2)}, u32[]{:S(2)}) collective-permute-start(bf16[4,96,512]{2,1,0:T(8,128)(2,1)S(1)} %fusion.2), channel_id=1, source_target_pairs={{0,16},{8,24},{16,0},{24,8},{1,17},{9,25},{17,1},{25,9},{2,18},{10... | collective-permute-start | bytes 1179656 | tf_op jit(solution)/shard_map/ppermute | solution.py:574
  185.3 9.1 %collective-permute-start.14 = (bf16[4,96,512]{2,1,0:T(8,128)(2,1)S(1)}, bf16[4,96,512]{2,1,0:T(8,128)(2,1)S(1)}, u32[]{:S(2)}, u32[]{:S(2)}) collective-permute-start(bf16[4,96,512]{2,1,0:T(8,128)(2,1)S(1)} %fusion.3), channel_id=1, source_target_pairs={{0,8},{8,0},{16,24},{24,16},{1,9},{9,1},{17,25},{25,17},{2,10},{10... | collective-permute-start | bytes 1179656 | tf_op jit(solution)/shard_map/ppermute | solution.py:574
  194.4 23.5 %copy-start.3 = (bf16[512,1536]{1,0:T(8,128)(2,1)S(1)}, bf16[512,1536]{1,0:T(8,128)(2,1)}, u32[]{:S(2)}) copy-start(bf16[512,1536]{1,0:T(8,128)(2,1)} %w_in.3) | copy-start | bytes 4718596
  195.9 21.9 %copy-start.1 = (bf16[512,2048]{1,0:T(8,128)(2,1)S(1)}, bf16[512,2048]{1,0:T(8,128)(2,1)}, u32[]{:S(2)}) copy-start(bf16[512,2048]{1,0:T(8,128)(2,1)} %w_up.3) | copy-start | bytes 6291460
  195.9 21.9 %copy-start.5 = (s32[3]{0:T(128)S(1)}, s32[3]{0:T(128)}, u32[]{:S(2)}) copy-start(s32[3]{0:T(128)} %pad_add_fusion.refs_0_.ids) | copy-start | bytes 40
  196.0 7.9 %collective-permute-start.15 = (bf16[192,512]{1,0:T(8,128)(2,1)S(1)}, bf16[192,512]{1,0:T(8,128)(2,1)S(1)}, u32[]{:S(2)}, u32[]{:S(2)}) collective-permute-start(bf16[192,512]{1,0:T(8,128)(2,1)S(1)} %pad_maximum_fusion.3), channel_id=1, source_target_pairs={{0,2},{1,3},{2,0},{3,1},{4,6},{5,7},{6,4},{7,5},{8,10},{9,11},{10,... | collective-permute-start | bytes 589832 | tf_op jit(solution)/shard_map/ppermute | solution.py:574
  196.1 14.1 %collective-permute-start.16 = (bf16[192,512]{1,0:T(8,128)(2,1)S(1)}, bf16[192,512]{1,0:T(8,128)(2,1)S(1)}, u32[]{:S(2)}, u32[]{:S(2)}) collective-permute-start(bf16[192,512]{1,0:T(8,128)(2,1)S(1)} %pad_maximum_fusion.4), channel_id=1, source_target_pairs={{0,4},{1,5},{2,6},{3,7},{4,0},{5,1},{6,2},{7,3},{8,12},{9,13},{10,... | collective-permute-start | bytes 589832 | tf_op jit(solution)/shard_map/ppermute | solution.py:574
  198.3 15.8 %collective-permute-start.17 = (bf16[192,512]{1,0:T(8,128)(2,1)S(1)}, bf16[192,512]{1,0:T(8,128)(2,1)S(1)}, u32[]{:S(2)}, u32[]{:S(2)}) collective-permute-start(bf16[192,512]{1,0:T(8,128)(2,1)S(1)} %pad_maximum_fusion.5), channel_id=1, source_target_pairs={{0,6},{1,7},{2,4},{3,5},{4,2},{5,3},{6,0},{7,1},{8,14},{9,15},{10,... | collective-permute-start | bytes 589832 | tf_op jit(solution)/shard_map/ppermute | solution.py:574
  199.7 17.8 %collective-permute-start.23 = (bf16[192,512]{1,0:T(8,128)(2,1)S(1)}, bf16[192,512]{1,0:T(8,128)(2,1)S(1)}, u32[]{:S(2)}, u32[]{:S(2)}) collective-permute-start(bf16[192,512]{1,0:T(8,128)(2,1)S(1)} %add_convert_fusion.9.p0), channel_id=1, source_target_pairs={{0,24},{8,16},{16,8},{24,0},{1,25},{9,17},{17,9},{25,1},{2,26},{10... | collective-permute-start | bytes 589832 | tf_op jit(solution)/shard_map/ppermute | solution.py:574
  202.2 15.7 %collective-permute-start.22 = (bf16[192,512]{1,0:T(8,128)(2,1)S(1)}, bf16[192,512]{1,0:T(8,128)(2,1)S(1)}, u32[]{:S(2)}, u32[]{:S(2)}) collective-permute-start(bf16[192,512]{1,0:T(8,128)(2,1)S(1)} %add_convert_fusion.9.p0), channel_id=1, source_target_pairs={{0,16},{8,24},{16,0},{24,8},{1,17},{9,25},{17,1},{25,9},{2,18},{10... | collective-permute-start | bytes 589832 | tf_op jit(solution)/shard_map/ppermute | solution.py:574
  203.9 13.9 %collective-permute-start.21 = (bf16[192,512]{1,0:T(8,128)(2,1)S(1)}, bf16[192,512]{1,0:T(8,128)(2,1)S(1)}, u32[]{:S(2)}, u32[]{:S(2)}) collective-permute-start(bf16[192,512]{1,0:T(8,128)(2,1)S(1)} %add_convert_fusion.9.p0), channel_id=1, source_target_pairs={{0,8},{8,0},{16,24},{24,16},{1,9},{9,1},{17,25},{25,17},{2,10},{10... | collective-permute-start | bytes 589832 | tf_op jit(solution)/shard_map/ppermute | solution.py:574
  214.3 8.7 %collective-permute-start.20 = (bf16[192,512]{1,0:T(8,128)(2,1)S(1)}, bf16[192,512]{1,0:T(8,128)(2,1)S(1)}, u32[]{:S(2)}, u32[]{:S(2)}) collective-permute-start(bf16[192,512]{1,0:T(8,128)(2,1)S(1)} %add_convert_fusion.8.p0), channel_id=1, source_target_pairs={{0,24},{8,16},{16,8},{24,0},{1,25},{9,17},{17,9},{25,1},{2,26},{10... | collective-permute-start | bytes 589832 | tf_op jit(solution)/shard_map/ppermute | solution.py:574
  216.7 7.8 %collective-permute-start.19 = (bf16[192,512]{1,0:T(8,128)(2,1)S(1)}, bf16[192,512]{1,0:T(8,128)(2,1)S(1)}, u32[]{:S(2)}, u32[]{:S(2)}) collective-permute-start(bf16[192,512]{1,0:T(8,128)(2,1)S(1)} %add_convert_fusion.8.p0), channel_id=1, source_target_pairs={{0,16},{8,24},{16,0},{24,8},{1,17},{9,25},{17,1},{25,9},{2,18},{10... | collective-permute-start | bytes 589832 | tf_op jit(solution)/shard_map/ppermute | solution.py:574
  217.5 7.0 %collective-permute-start.18 = (bf16[192,512]{1,0:T(8,128)(2,1)S(1)}, bf16[192,512]{1,0:T(8,128)(2,1)S(1)}, u32[]{:S(2)}, u32[]{:S(2)}) collective-permute-start(bf16[192,512]{1,0:T(8,128)(2,1)S(1)} %add_convert_fusion.8.p0), channel_id=1, source_target_pairs={{0,8},{8,0},{16,24},{24,16},{1,9},{9,1},{17,25},{25,17},{2,10},{10... | collective-permute-start | bytes 589832 | tf_op jit(solution)/shard_map/ppermute | solution.py:574
  (18 other events, 145.1 us)

commit v5 on v4

--- a/solution.py
+++ b/solution.py
@@ -63,7 +63,7 @@
     return low, (low.astype(F32).astype(BF), (1.0 - low.astype(F32)).astype(BF))
 
 
-def attend(qkv_ref, p_ref, o_ref, bias_ref, s_ref):
+def attend_steps(qkv_ref, p_ref, o_ref, bias_ref, s_ref):
     width = qkv_ref.shape[1] // 3
     size = width // HEADS
     _, masks = head_masks(size)
@@ -91,13 +91,15 @@
             score(head + 3)
         soften(head)
         soften(head + 1)
+        yield
     for head in range(0, HEADS, 2):
         v = lanes(2, head).T
         both = jnp.concatenate([nn(v[:size], p_ref[head]), nn(v[size:], p_ref[head + 1])], axis=0)
         o_ref[:, head * size : (head + 2) * size] = both.T.astype(BF)
-
-
-def attend_backward(qkv_ref, p_ref, go_ref, out_ref, gp_ref, gs_ref):
+        yield
+
+
+def attend_backward_steps(qkv_ref, p_ref, go_ref, out_ref, gp_ref, gs_ref):
     width = qkv_ref.shape[1] // 3
     size = width // HEADS
     _, masks = head_masks(size)
@@ -133,6 +135,7 @@
         put(0, head, both.T)
 
     start(0)
+    yield
     for head in range(0, HEADS, 2):
         middle(head)
         middle(head + 1)
@@ -140,10 +143,11 @@
             start(head + 2)
         if head > 0:
             finish(head - 2)
+        yield
     finish(HEADS - 2)
 
 
-def feed_up(m, up_ref, down_ref, h_ref, slope_ref, u_ref):
+def feed_up_steps(m, up_ref, down_ref, h_ref, slope_ref, u_ref):
     steps = up_ref.shape[1] // CHUNK
 
     def before(step):
@@ -155,14 +159,47 @@
             before(step + 1)
         at = step * CHUNK
         h_ref[:, at : at + CHUNK], slope_ref[:, at : at + CHUNK] = gelu_parts(u_ref[step % 2])
+        yield
     return nn(h_ref[...], down_ref[...])
 
 
-def feed_back(e2, up_ref, down_ref, slope_ref, eu_ref):
+def feed_back_steps(e2, up_ref, down_ref, slope_ref, eu_ref, up_copy=None):
     for at in range(0, up_ref.shape[1], CHUNK):
         gh = nt(e2, down_ref[at : at + CHUNK, :]).astype(BF)
         eu_ref[:, at : at + CHUNK] = gh * slope_ref[:, at : at + CHUNK]
+        yield
+    if up_copy is not None:
+        wait(up_copy)
     return nt(eu_ref[...], up_ref[...])
+
+
+def whole(steps):
+    while True:
+        try:
+            next(steps)
+        except StopIteration as end:
+            return end.value
+
+
+def together(runs):
+    while runs:
+        runs = [run for run in runs if next(run, "end") != "end"]
+
+
+def attend(*args):
+    whole(attend_steps(*args))
+
+
+def attend_backward(*args):
+    whole(attend_backward_steps(*args))
+
+
+def feed_up(*args):
+    return whole(feed_up_steps(*args))
+
+
+def feed_back(*args):
+    return whole(feed_back_steps(*args))
 
 
 def rows_of(block):
@@ -227,31 +264,72 @@
     bias[...] = jnp.where(allowed, 0.0, -1e30)
 
 
-def time_both(labels, x2, grad, *rest):
-    gain, w_in, w_out, scale, w_up, w_down = rest[:6]
-    g0, out, z0, gqkv, o, e1, z1, eu, h, e2 = rest[6:16]
-    qkv, p, slope, bias, *work = rest[16:]
-    slots, _, patches, _ = x2.shape
-    build_bias(labels, pack_at(labels, pl.program_id(0)), slots, patches, bias)
-    x = rows_of(x2[...])
-    unit0, inverse0 = unit(x)
-    z0[0] = unit0.astype(BF)
-    qkv[...] = nn((unit0 * gain[...]).astype(BF), w_in[...]).astype(BF)
-    attend(qkv, p, o.at[0], bias, work[0])
-    r1 = x + nn(o[0], w_out[...])
-    unit1, inverse1 = unit(r1)
-    z1[0] = unit1.astype(BF)
-    m = (unit1 * scale[...]).astype(BF)
-    block_of(r1 + feed_up(m, w_up, w_down, h.at[0], slope, work[1]), out)
-    g2 = rows_of(grad[...])
-    e2[0] = g2.astype(BF)
-    gm = feed_back(e2[0], w_up, w_down, slope, eu.at[0])
-    g1 = g2 + unit_backward(gm * scale[...], unit1, inverse1)
-    e1[0] = g1.astype(BF)
-    slope[:, : g1.shape[1]] = nt(e1[0], w_out[...]).astype(BF)
-    attend_backward(qkv, p, slope, gqkv.at[0], work[2], work[3])
-    gn = nt(gqkv[0], w_in[...])
-    block_of(g1 + unit_backward(gn * gain[...], unit0, inverse0), g0)
+def time_kernel(labels, gain, scale, x2_in, grad_in, w_in_in, w_out_in, w_up_in, w_down_in, *rest):
+    outs, rest = rest[:10], rest[10:]
+    x2, grad, w_in, w_out, w_up, w_down = rest[:6]
+    held = rest[6:16]
+    g0, out, z0, gqkv, o, e1, z1, eu, h, e2 = held
+    qkv, p, slope, bias, go, scores, u, gp, gs = rest[16:25]
+    copies = Copies(rest[-1])
+    slots, packs, patches, _ = x2.shape
+    got_x2, got_in = copies.fetch(x2_in, x2), copies.fetch(w_in_in, w_in)
+    got_out, got_up = copies.fetch(w_out_in, w_out), copies.fetch(w_up_in, w_up)
+    got_down, got_grad = copies.fetch(w_down_in, w_down), copies.fetch(grad_in, grad)
+
+    def send(index, pack):
+        copies.send(held[index].at[pack], outs[index].at[pack])
+
+    def run(pack):
+        if pack == 0:
+            wait(got_x2)
+        build_bias(labels, pack_at(labels, pack), slots, patches, bias.at[pack])
+        x = rows_of(x2[:, pack : pack + 1])
+        unit0, inverse0 = unit(x)
+        z0[pack] = unit0.astype(BF)
+        send(2, pack)
+        if pack == 0:
+            wait(got_in)
+        qkv[pack] = nn((unit0 * gain[...]).astype(BF), w_in[...]).astype(BF)
+        yield
+        yield from attend_steps(qkv.at[pack], p.at[pack], o.at[pack], bias.at[pack], scores.at[pack])
+        send(4, pack)
+        if pack == 0:
+            wait(got_out)
+        r1 = x + nn(o[pack], w_out[...])
+        unit1, inverse1 = unit(r1)
+        z1[pack] = unit1.astype(BF)
+        send(6, pack)
+        m = (unit1 * scale[...]).astype(BF)
+        yield
+        if pack == 0:
+            wait(got_up, got_down)
+        total = yield from feed_up_steps(m, w_up, w_down, h.at[pack], slope.at[pack], u.at[pack])
+        send(8, pack)
+        block_of(r1 + total, out.at[:, pl.ds(pack, 1)])
+        if pack == 0:
+            wait(got_grad)
+        g2 = rows_of(grad[:, pack : pack + 1])
+        e2[pack] = g2.astype(BF)
+        send(9, pack)
+        yield
+        gm = yield from feed_back_steps(e2[pack], w_up, w_down, slope.at[pack], eu.at[pack])
+        send(7, pack)
+        g1 = g2 + unit_backward(gm * scale[...], unit1, inverse1)
+        e1[pack] = g1.astype(BF)
+        send(5, pack)
+        go[pack] = nt(e1[pack], w_out[...]).astype(BF)
+        yield
+        yield from attend_backward_steps(
+            qkv.at[pack], p.at[pack], go.at[pack], gqkv.at[pack], gp.at[pack], gs.at[pack]
+        )
+        send(3, pack)
+        gn = nt(gqkv[pack], w_in[...])
+        block_of(g1 + unit_backward(gn * gain[...], unit0, inverse0), g0.at[:, pl.ds(pack, 1)])
+
+    together([run(pack) for pack in range(packs)])
+    copies.send(g0, outs[0])
+    copies.send(out, outs[1])
+    copies.finish()
 
 
 def alone_both(labels, frames, grad, *rest):
@@ -350,13 +428,14 @@
         for source, target in zip(one, whole):
             got_rest.append(copies.fetch(source.at[0], target.at[pl.ds(have, tokens)]))
     wait(got_g2)
-    for pack in range(packs):
+
+    def run(pack):
         rows = slice(pack * tokens, (pack + 1) * tokens)
         e2[rows] = rows_of(g2[:, pack : pack + 1]).astype(BF)
+        if pack == 0:
+            wait(got_down)
         wait(got_slope[pack])
-        if pack == 0:
-            wait(got_down, got_up)
-        gm = feed_back(e2[rows], w_up, w_down, slope.at[pack], eu.at[rows])
+        gm = yield from feed_back_steps(e2[rows], w_up, w_down, slope.at[pack], eu.at[rows], got_up if pack == 0 else None)
         if pack == 0:
             wait(*got_z1, got_out)
         grad = unit_backward(gm * scale[...], z1[rows].astype(F32), inv1[pack, :, :1])
@@ -365,11 +444,15 @@
         e1[rows] = total.astype(BF)
         go[pack] = nt(e1[rows], w_out[...]).astype(BF)
         copies.send(g1.at[pack], g1_out.at[pack])
-    for pack in range(packs):
+        yield
         wait(*got_attend[pack])
         rows = pl.ds(pack * tokens, tokens)
-        attend_backward(qkv.at[pack], p.at[pack], go.at[pack], gqkv.at[rows], gp, gs)
+        yield from attend_backward_steps(
+            qkv.at[pack], p.at[pack], go.at[pack], gqkv.at[rows], gp.at[pack], gs.at[pack]
+        )
         copies.send(gqkv.at[rows], gqkv_out.at[pack])
+
+    together([run(pack) for pack in range(packs)])
     if hierarchical:
         wait(*got_rest)
         one = Halves(copies, ids, scratch[19:21], outs[:2], x_high=True)
@@ -869,19 +952,36 @@
     sz0_one, so_one, se1_one, sgqkv_one, sz1_one, seu_one, sh_one, se2_one = alone[:8]
     tz0_one, to_one, te1_one, tgv_one, tz1_one, teu_one, th_one, te2_one = alone[8:]
 
-    g0, out, tz0, tgqkv, to, te1, tz1, teu, th, te2 = shared.call(
-        time_both,
-        [("moved", x2_moved), ("moved", grad_moved)] + time_args,
-        [moved, moved] + steps(some, rows_w, rows_3, rows_w, rows_w, rows_w, rows_h, rows_h, rows_w),
-        scratch=[
-            pltpu.VMEM(rows_3, BF),
-            pltpu.VMEM((HEADS, tokens, tokens), BF),
-            pltpu.VMEM(rows_h, BF),
-            pltpu.VMEM((tokens, tokens), F32),
-        ]
-        + work_shapes(tokens),
-        flops=3 * flops,
+    shared_w, shared_3, shared_h = [(some,) + tail for tail in (rows_w, rows_3, rows_h)]
+    time_outs = [(x2.shape, BF)] * 2 + [
+        (shape, BF)
+        for shape in (shared_w, shared_3, shared_w, shared_w, shared_w, shared_h, shared_h, shared_w)
+    ]
+    square = (some, HEADS, tokens, tokens)
+    g0, out, tz0, tgqkv, to, te1, tz1, teu, th, te2 = manual_call(
+        time_kernel,
+        clip_labels,
+        [row(time_gain), row(time_scale), x2_moved, grad_moved]
+        + [time_input, time_output, time_up, time_down],
+        time_outs,
+        [(x2.shape, BF)] * 2
+        + [(w.shape, BF) for w in (time_input, time_output, time_up, time_down)]
+        + time_outs
+        + [
+            (shared_3, BF),
+            (square, BF),
+            (shared_h, BF),
+            ((some, tokens, tokens), F32),
+            (shared_w, BF),
+            ((some, 4, tokens, tokens), F32),
+            ((some, 2, tokens, CHUNK), BF),
+            ((some, 4, tokens, tokens), BF),
+            (square, BF),
+        ],
+        6 + 8 * some + 2,
+        small=2,
         after=(sz0_one,),
+        flops=3 * some * flops,
     )
     g0_moved = exchange(g0)
     out, g0_moved = lax.optimization_barrier((out, g0_moved))
@@ -913,7 +1013,6 @@
         time_grads = plain_grads(joined[0], joined[1], joined[3], joined[2], time_up, time_scale)
         time_grads += plain_grads(joined[4], joined[5], joined[6], joined[7], time_input, time_gain)
 
-    shared_w, shared_3 = (some,) + rows_w, (some,) + rows_3
     space_one = [sz1_one, seu_one, sh_one, se2_one, sz0_one, sgqkv_one, so_one, se1_one]
     whole_shapes = [((everything, a.shape[2]), BF) for a in space_one]
     parts_shapes = [((4, 4, 96, CHUNK), BF)] * 4
@@ -935,8 +1034,8 @@
             (sp.shape, BF),
             (shared_w, BF),
             (shared_w, F32),
-            ((4, tokens, tokens), BF),
-            ((HEADS, tokens, tokens), BF),
+            ((some, 4, tokens, tokens), BF),
+            (square, BF),
         ]
         + whole_shapes
         + (parts_shapes if hierarchical else []),

time: 231 us -> 226 us (0.978)
  Pallas kernels: 113 us -> 108 us
    pallas_call x4 -> x3, Pallas kernels: 70.5 us -> 43.2 us  [call(): pl.pallas_call(without(kernel, len(scalars) + len(args), unread), out_sha...]
    pallas_call x2 -> x3, Pallas kernels: 35 us -> 57.3 us  [manual_call(): pl.pallas_call(without(kernel, 1 + len(args), len(after)), out_shape=[jax...]
  transfers between devices with their start and end apart: 28 -> 28, of which waited for: 11 -> 12; matrix products, arithmetic and copies ran while one was open for 8% -> 9% of each run, Pallas kernels for 36% -> 36%
where the time goes in v5:
time: 226 us; the launch traced here: 221 us
  Pallas kernels  108 us (48%)
  starting transfers between devices  49.6 us (22%)
  waiting for transfers between devices  38.3 us (17%)
  other arithmetic  20.6 us (9%)
  local copies, waits for them, and re-layouts  3.16 us (1%)
    pallas_call x3, Pallas kernels, manual_call(): pl.pallas_call(without(kernel, 1 + len(args), len(after)), out_shape=[jax...  57.3 us
    pallas_call x3, Pallas kernels, call(): pl.pallas_call(without(kernel, len(scalars) + len(args), unread), out_sha...  43.2 us
    ppermute x24, waiting for transfers between devices, swap(): return lax.ppermute(array, axis, [(i, i ^ mask) for i in range(size)])  34.1 us
    all_to_all x4, starting transfers between devices, exchange(): return lax.all_to_all(array, 'tm', split_axis=0, concat_axis=0, tiled=True)  25.2 us
    ppermute x24, starting transfers between devices, swap(): return lax.ppermute(array, axis, [(i, i ^ mask) for i in range(size)])  24.4 us
    convert_element_type x12, other arithmetic, add(): return total.astype(BF)  18.6 us
  transfers between devices with their start and end apart: 28, of which 12 were waited for; matrix products, arithmetic and copies ran while one was open for 9% of the time, Pallas kernels for 36%

profile of v5, /device:TPU:16, one launch (start us, length us, event | category | flops | bytes accessed | tf_op | source)
XLA Modules:
  0.0 221.3 jit_solution(8468244192634106334)
XLA Ops:
  0.6 2.8 %shard_map.254.refs_8_ = bf16[8,3,32,512]{3,2,1,0:T(8,128)(2,1)} custom-call(s32[4,8]{1,0:T(4,128)} %refs_0_.7, bf16[4,1,256,512]{3,2,1,0:T(8,128)(2,1)} %refs_2_.2), custom_call_target="tpu_custom_call" | custom-call | tf_op jit(solution)/shard_map/pallas_call | solution.py:840
  3.5 5.2 %all-to-all-start = ((bf16[8,3,32,512]{3,2,1,0:T(8,128)(2,1)}), bf16[8,3,32,512]{3,2,1,0:T(8,128)(2,1)S(1)}, u32[]{:S(2)}, u32[]{:S(2)}) async-start(bf16[8,3,32,512]{3,2,1,0:T(8,128)(2,1)} %shard_map.254.refs_8_), calls=%async_computation | async-start | bytes 1572864 | tf_op jit(solution)/shard_map/all_to_all | solution.py:887
  8.7 16.9 %shard_map.255 = (bf16[8,3,32,512]{3,2,1,0:T(8,128)(2,1)}, bf16[3,256,512]{2,1,0:T(8,128)(2,1)}, f32[3,256,128]{2,1,0:T(8,128)}, bf16[3,256,1536]{2,1,0:T(8,128)...) custom-call(s32[4,8]{1,0:T(4,128)} %refs_0_.7, ...), custom_call_target="tpu_custom_call" | custom-call | flops 4831838208 | bytes 8130560 | tf_op jit(solution)/shard_map/pallas_call | solution.py:534
  26.4 7.0 %all-to-all-start.1 = ((bf16[8,3,32,512]{3,2,1,0:T(8,128)(2,1)}), bf16[8,3,32,512]{3,2,1,0:T(8,128)(2,1)S(1)}, u32[]{:S(2)}, u32[]{:S(2)}) async-start(bf16[8,3,32,512]{3,2,1,0:T(8,128)(2,1)} %get-tuple-element.92.refs_15_), calls=%async_computation.1 | async-start | bytes 1572864 | tf_op jit(solution)/shard_map/all_to_all | solution.py:887
  33.4 18.9 %shard_map.256 = (f32[4,1,256,512]{3,2,1,0:T(8,128)}, f32[4,1,256,512]{3,2,1,0:T(8,128)}, bf16[1,256,512]{2,1,0:T(8,128)(2,1)}, bf16[1,256,512]{2,1,0:T(8,128)(2...) custom-call(s32[4,8]{1,0:T(4,128)} %refs_0_.7, ...), custom_call_target="tpu_custom_call" | custom-call | flops 9663676416 | bytes 15474688 | tf_op jit(solution)/shard_map/pallas_call | solution.py:534
  53.3 23.3 %shard_map.257 = (bf16[8,3,32,512]{3,2,1,0:T(8,128)(2,1)}, bf16[8,3,32,512]{3,2,1,0:T(8,128)(2,1)}, bf16[3,256,512]{2,1,0:T(8,128)(2,1)}, bf16[3,256,1536]{2,1,0...) custom-call(s32[4,8]{1,0:T(4,128)} %refs_0_.7, ...), custom_call_target="tpu_custom_call" | custom-call | flops 14495514624 | tf_op jit(solution)/shard_map/pallas_call | solution.py:640
  76.5 5.2 %all-to-all-start.2 = ((bf16[8,3,32,512]{3,2,1,0:T(8,128)(2,1)}), bf16[8,3,32,512]{3,2,1,0:T(8,128)(2,1)S(1)}, u32[]{:S(2)}, u32[]{:S(2)}) async-start(bf16[8,3,32,512]{3,2,1,0:T(8,128)(2,1)} %get-tuple-element.115), calls=%async_computation.2 | async-start | bytes 1572864 | tf_op jit(solution)/shard_map/all_to_all | solution.py:887
  82.4 13.1 %shard_map.258 = (bf16[4,4,96,512]{3,2,1,0:T(8,128)(2,1)}, bf16[4,4,96,512]{3,2,1,0:T(8,128)(2,1)}, bf16[4,4,96,512]{3,2,1,0:T(8,128)(2,1)}, bf16[4,4,96,512]{3,2,1,0:T(8,128)(2,1)}) custom-call(s32[3]{0:T(128)} %pad_add_fusion.refs_0_.ids, bf16[3,256,512]{2,1,0:T(8,128)(2,1)} %get-tuple-element.95.refs_1_, bf16[3,256,2048]{2,1,0:T(8,128)(2,1)} %get-tuple-element.96.refs_2_, ...), custom_call_target="tpu_custom_call" | custom-call | flops 6442450944 | tf_op jit(solution)/shard_map/pallas_call | solution.py:640
  96.0 3.5 %all-to-all-done.2.source.refs_3_ = bf16[8,3,32,512]{3,2,1,0:T(8,128)(2,1)S(1)} async-done(((bf16[8,3,32,512]{3,2,1,0:T(8,128)(2,1)}), bf16[8,3,32,512]{3,2,1,0:T(8,128)(2,1)S(1)}, u32[]{:S(2)}, u32[]{:S(2)}) %all-to-all-start.2) | async-done | bytes 786464 | tf_op jit(solution)/shard_map/all_to_all | solution.py:887
  101.0 7.7 %all-to-all-start.3 = ((bf16[8,3,32,512]{3,2,1,0:T(8,128)(2,1)}), bf16[8,3,32,512]{3,2,1,0:T(8,128)(2,1)}, u32[]{:S(2)}, u32[]{:S(2)}) async-start(bf16[8,3,32,512]{3,2,1,0:T(8,128)(2,1)} %get-tuple-element.137), calls=%async_computation.3 | async-start | bytes 1572864 | tf_op jit(solution)/shard_map/all_to_all | solution.py:887
  108.7 3.0 %add_convert_fusion.2 = (bf16[2,4,96,512]{3,2,1,0:T(8,128)(2,1)S(1)}, bf16[2,4,96,512]{3,2,1,0:T(8,128)(2,1)}) fusion(bf16[4,4,96,512]{3,2,1,0:T(8,128)(2,1)} %collective-permute-done.1, bf16[4,4,96,512]{3,2,1,0:T(8,128)(2,1)} %get-tuple-element.132, f32[512]{0:T(512)S(1)} %bitcast.148, bf16[4,4,96,512]{3,2,1,0:T(8,128)(2,1)} %collective-permute-done, ...), kind=kLoop, calls=%fused_computation.2 | loop fusion | flops 3932160 | bytes 4720640 | tf_op jit(solution)/shard_map/convert_element_type | solution.py:664
  114.7 21.0 %shard_map.260 = (f32[3,256,512]{2,1,0:T(8,128)}, bf16[3,256,1536]{2,1,0:T(8,128)(2,1)}, bf16[4,4,96,512]{3,2,1,0:T(8,128)(2,1)}, bf16[4,4,96,512]{3,2,1,0:T(8,1...) custom-call(s32[3]{0:T(128)} %pad_add_fusion.refs_0_.ids, f32[1,512]{1,0:T(1,128)} %bitcast.145, ...), custom_call_target="tpu_custom_call" | custom-call | flops 12884901888 | tf_op jit(solution)/shard_map/pallas_call | solution.py:640
  137.1 2.0 fusion.source
  142.7 2.2 add_convert_fusion
  144.9 1.5 collective-permute-start.11
  146.5 5.7 %collective-permute-done.7 = bf16[4,96,512]{2,1,0:T(8,128)(2,1)S(1)} collective-permute-done((bf16[4,96,512]{2,1,0:T(8,128)(2,1)S(1)}, bf16[4,96,512]{2,1,0:T(8,128)(2,1)S(1)}, u32[]{:S(2)}, u32[]{:S(2)}) %collective-permute-start.7) | collective-permute-done | bytes 393248 | tf_op jit(solution)/shard_map/ppermute | solution.py:657
  153.6 1.5 fusion.19
  155.1 1.5 collective-permute-start.8
  160.6 7.3 %shard_map.262 = (f32[4,1,256,512]{3,2,1,0:T(8,128)}, f32[4,1,256,512]{3,2,1,0:T(8,128)}) custom-call(s32[4,8]{1,0:T(4,128)} %refs_0_.7, bf16[3,256,1536]{2,1,0:T(8,128)(2,1)} %get-tuple-element.134.refs_1_, bf16[512,1536]{1,0:T(8,128)(2,1)} %w_in.2, f32[1,512]{1,0:T(1,128)} %bitcast.135, ...), custom_call_target="tpu_custom_call", output_to_operand_aliasing={{0}: (8, {}), {1}: (9, {})} | custom-call | flops 1207959552 | bytes 13240320 | tf_op jit(solution)/shard_map/pallas_call | solution.py:534
  167.9 3.0 %collective-permute-done.9 = bf16[192,512]{1,0:T(8,128)(2,1)} collective-permute-done((bf16[192,512]{1,0:T(8,128)(2,1)}, bf16[192,512]{1,0:T(8,128)(2,1)}, u32[]{:S(2)}, u32[]{:S(2)}) %collective-permute-start.9) | collective-permute-done | bytes 196640 | tf_op jit(solution)/shard_map/ppermute | solution.py:657
  171.0 4.5 %collective-permute-done.10 = bf16[192,512]{1,0:T(8,128)(2,1)} collective-permute-done((bf16[192,512]{1,0:T(8,128)(2,1)}, bf16[192,512]{1,0:T(8,128)(2,1)}, u32[]{:S(2)}, u32[]{:S(2)}) %collective-permute-start.10) | collective-permute-done | bytes 196640 | tf_op jit(solution)/shard_map/ppermute | solution.py:657
  181.3 6.1 %collective-permute-done.12 = bf16[4,96,512]{2,1,0:T(8,128)(2,1)S(1)} collective-permute-done((bf16[4,96,512]{2,1,0:T(8,128)(2,1)S(1)}, bf16[4,96,512]{2,1,0:T(8,128)(2,1)S(1)}, u32[]{:S(2)}, u32[]{:S(2)}) %collective-permute-start.12) | collective-permute-done | bytes 393248 | tf_op jit(solution)/shard_map/ppermute | solution.py:657
  187.4 1.5 fusion.11
  189.0 1.5 fusion.10
  190.7 2.2 collective-permute-start.16
  194.4 2.4 %collective-permute-start.23 = (bf16[192,512]{1,0:T(8,128)(2,1)S(1)}, bf16[192,512]{1,0:T(8,128)(2,1)S(1)}, u32[]{:S(2)}, u32[]{:S(2)}) collective-permute-start(bf16[192,512]{1,0:T(8,128)(2,1)S(1)} %add_convert_fusion.9.p0), channel_id=1, source_target_pairs={{0,24},{8,16},{16,8},{24,0},{1,25},{9,17},{17,9},{25,1},{2,26},{10... | collective-permute-start | bytes 589832 | tf_op jit(solution)/shard_map/ppermute | solution.py:657
  200.0 4.8 %collective-permute-done.16 = bf16[192,512]{1,0:T(8,128)(2,1)S(1)} collective-permute-done((bf16[192,512]{1,0:T(8,128)(2,1)S(1)}, bf16[192,512]{1,0:T(8,128)(2,1)S(1)}, u32[]{:S(2)}, u32[]{:S(2)}) %collective-permute-start.16) | collective-permute-done | bytes 196640 | tf_op jit(solution)/shard_map/ppermute | solution.py:657
  204.8 3.9 %collective-permute-done.17 = bf16[192,512]{1,0:T(8,128)(2,1)S(1)} collective-permute-done((bf16[192,512]{1,0:T(8,128)(2,1)S(1)}, bf16[192,512]{1,0:T(8,128)(2,1)S(1)}, u32[]{:S(2)}, u32[]{:S(2)}) %collective-permute-start.17) | collective-permute-done | bytes 196640 | tf_op jit(solution)/shard_map/ppermute | solution.py:657
  208.9 2.5 %collective-permute-start.20 = (bf16[192,512]{1,0:T(8,128)(2,1)S(1)}, bf16[192,512]{1,0:T(8,128)(2,1)S(1)}, u32[]{:S(2)}, u32[]{:S(2)}) collective-permute-start(bf16[192,512]{1,0:T(8,128)(2,1)S(1)} %add_convert_fusion.8.p0), channel_id=1, source_target_pairs={{0,24},{8,16},{16,8},{24,0},{1,25},{9,17},{17,9},{25,1},{2,26},{10... | collective-permute-start | bytes 589832 | tf_op jit(solution)/shard_map/ppermute | solution.py:657
  212.5 2.0 shard_map.264
  214.4 3.1 %collective-permute-done.20.p3 = bf16[192,512]{1,0:T(8,128)(2,1)S(1)} collective-permute-done((bf16[192,512]{1,0:T(8,128)(2,1)S(1)}, bf16[192,512]{1,0:T(8,128)(2,1)S(1)}, u32[]{:S(2)}, u32[]{:S(2)}) %collective-permute-start.20) | collective-permute-done | bytes 196640 | tf_op jit(solution)/shard_map/ppermute | solution.py:657
  219.1 1.9 shard_map.263
  (98 shorter events, 31.1 us)
Async XLA Ops:
  3.5 22.9 %all-to-all-start = ((bf16[8,3,32,512]{3,2,1,0:T(8,128)(2,1)}), bf16[8,3,32,512]{3,2,1,0:T(8,128)(2,1)S(1)}, u32[]{:S(2)}, u32[]{:S(2)}) async-start(bf16[8,3,32,512]{3,2,1,0:T(8,128)(2,1)} %shard_map.254.refs_8_), calls=%async_computation | async-start | bytes 1572864 | tf_op jit(solution)/shard_map/all_to_all | solution.py:887
  26.4 26.0 %copy-start.14 = (bf16[8,3,32,512]{3,2,1,0:T(8,128)(2,1)}, bf16[8,3,32,512]{3,2,1,0:T(8,128)(2,1)S(1)}, u32[]{:S(2)}) copy-start(bf16[8,3,32,512]{3,2,1,0:T(8,128)(2,1)S(1)} %all-to-all-done.refs_4_) | copy-start | bytes 2359300
  26.4 26.0 %all-to-all-start.1 = ((bf16[8,3,32,512]{3,2,1,0:T(8,128)(2,1)}), bf16[8,3,32,512]{3,2,1,0:T(8,128)(2,1)S(1)}, u32[]{:S(2)}, u32[]{:S(2)}) async-start(bf16[8,3,32,512]{3,2,1,0:T(8,128)(2,1)} %get-tuple-element.92.refs_15_), calls=%async_computation.1 | async-start | bytes 1572864 | tf_op jit(solution)/shard_map/all_to_all | solution.py:887
  76.5 22.9 %all-to-all-start.2 = ((bf16[8,3,32,512]{3,2,1,0:T(8,128)(2,1)}), bf16[8,3,32,512]{3,2,1,0:T(8,128)(2,1)S(1)}, u32[]{:S(2)}, u32[]{:S(2)}) async-start(bf16[8,3,32,512]{3,2,1,0:T(8,128)(2,1)} %get-tuple-element.115), calls=%async_computation.2 | async-start | bytes 1572864 | tf_op jit(solution)/shard_map/all_to_all | solution.py:887
  95.4 13.2 %collective-permute-start = (bf16[4,4,96,512]{3,2,1,0:T(8,128)(2,1)}, bf16[4,4,96,512]{3,2,1,0:T(8,128)(2,1)}, u32[]{:S(2)}, u32[]{:S(2)}) collective-permute-start(bf16[4,4,96,512]{3,2,1,0:T(8,128)(2,1)} %get-tuple-element.111), channel_id=1, source_target_pairs={{0,1},{1,0},{2,3},{3,2},{4,5},{5,4},{6,7},{7,6},{8,9},{9,8},{10,11... | collective-permute-start | bytes 4718600 | tf_op jit(solution)/shard_map/ppermute | solution.py:657
  95.7 13.0 %collective-permute-start.1 = (bf16[4,4,96,512]{3,2,1,0:T(8,128)(2,1)}, bf16[4,4,96,512]{3,2,1,0:T(8,128)(2,1)}, u32[]{:S(2)}, u32[]{:S(2)}) collective-permute-start(bf16[4,4,96,512]{3,2,1,0:T(8,128)(2,1)} %get-tuple-element.112), channel_id=1, source_target_pairs={{0,1},{1,0},{2,3},{3,2},{4,5},{5,4},{6,7},{7,6},{8,9},{9,8},{10,11... | collective-permute-start | bytes 4718600 | tf_op jit(solution)/shard_map/ppermute | solution.py:657
  101.0 59.6 %all-to-all-start.3 = ((bf16[8,3,32,512]{3,2,1,0:T(8,128)(2,1)}), bf16[8,3,32,512]{3,2,1,0:T(8,128)(2,1)}, u32[]{:S(2)}, u32[]{:S(2)}) async-start(bf16[8,3,32,512]{3,2,1,0:T(8,128)(2,1)} %get-tuple-element.137), calls=%async_computation.3 | async-start | bytes 1572864 | tf_op jit(solution)/shard_map/all_to_all | solution.py:887
  111.7 24.6 %collective-permute-start.3 = (bf16[2,4,96,512]{3,2,1,0:T(8,128)(2,1)S(1)}, bf16[2,4,96,512]{3,2,1,0:T(8,128)(2,1)S(1)}, u32[]{:S(2)}, u32[]{:S(2)}) collective-permute-start(bf16[2,4,96,512]{3,2,1,0:T(8,128)(2,1)S(1)} %get-tuple-element.186.refs_23_), channel_id=1, source_target_pairs={{0,16},{8,24},{16,0},{24,8},{1,17},{9,25},{17,1},{25,9},{2,18},{10... | collective-permute-start | bytes 2359304 | tf_op jit(solution)/shard_map/ppermute | solution.py:657
  113.2 27.5 %collective-permute-start.5 = (bf16[2,4,96,512]{3,2,1,0:T(8,128)(2,1)}, bf16[2,4,96,512]{3,2,1,0:T(8,128)(2,1)}, u32[]{:S(2)}, u32[]{:S(2)}) collective-permute-start(bf16[2,4,96,512]{3,2,1,0:T(8,128)(2,1)} %get-tuple-element.187.refs_22_), channel_id=1, source_target_pairs={{0,8},{8,0},{16,24},{24,16},{1,9},{9,1},{17,25},{25,17},{2,10},{10... | collective-permute-start | bytes 2359304 | tf_op jit(solution)/shard_map/ppermute | solution.py:657
  135.7 7.0 %collective-permute-start.2 = (bf16[4,4,96,512]{3,2,1,0:T(8,128)(2,1)}, bf16[4,4,96,512]{3,2,1,0:T(8,128)(2,1)}, u32[]{:S(2)}, u32[]{:S(2)}) collective-permute-start(bf16[4,4,96,512]{3,2,1,0:T(8,128)(2,1)} %get-tuple-element.141), channel_id=1, source_target_pairs={{0,1},{1,0},{2,3},{3,2},{4,5},{5,4},{6,7},{7,6},{8,9},{9,8},{10,11... | collective-permute-start | bytes 4718600 | tf_op jit(solution)/shard_map/ppermute | solution.py:657
  135.8 6.9 %collective-permute-start.4 = (bf16[4,4,96,512]{3,2,1,0:T(8,128)(2,1)}, bf16[4,4,96,512]{3,2,1,0:T(8,128)(2,1)}, u32[]{:S(2)}, u32[]{:S(2)}) collective-permute-start(bf16[4,4,96,512]{3,2,1,0:T(8,128)(2,1)} %get-tuple-element.144), channel_id=1, source_target_pairs={{0,1},{1,0},{2,3},{3,2},{4,5},{5,4},{6,7},{7,6},{8,9},{9,8},{10,11... | collective-permute-start | bytes 4718600 | tf_op jit(solution)/shard_map/ppermute | solution.py:657
  140.2 12.0 %collective-permute-start.7 = (bf16[4,96,512]{2,1,0:T(8,128)(2,1)S(1)}, bf16[4,96,512]{2,1,0:T(8,128)(2,1)S(1)}, u32[]{:S(2)}, u32[]{:S(2)}) collective-permute-start(bf16[4,96,512]{2,1,0:T(8,128)(2,1)S(1)} %copy-done.19), channel_id=1, source_target_pairs={{0,8},{8,0},{16,24},{24,16},{1,9},{9,1},{17,25},{25,17},{2,10},{10... | collective-permute-start | bytes 1179656 | tf_op jit(solution)/shard_map/ppermute | solution.py:657
  142.1 11.5 %collective-permute-start.6 = (bf16[4,96,512]{2,1,0:T(8,128)(2,1)S(1)}, bf16[4,96,512]{2,1,0:T(8,128)(2,1)S(1)}, u32[]{:S(2)}, u32[]{:S(2)}) collective-permute-start(bf16[4,96,512]{2,1,0:T(8,128)(2,1)S(1)} %fusion.1), channel_id=1, source_target_pairs={{0,16},{8,24},{16,0},{24,8},{1,17},{9,25},{17,1},{25,9},{2,18},{10... | collective-permute-start | bytes 1179656 | tf_op jit(solution)/shard_map/ppermute | solution.py:657
  144.9 31.7 %collective-permute-start.11 = (bf16[2,4,96,512]{3,2,1,0:T(8,128)(2,1)S(1)}, bf16[2,4,96,512]{3,2,1,0:T(8,128)(2,1)}, u32[]{:S(2)}, u32[]{:S(2)}) collective-permute-start(bf16[2,4,96,512]{3,2,1,0:T(8,128)(2,1)S(1)} %get-tuple-element.145.refs_10_), channel_id=1, source_target_pairs={{0,8},{8,0},{16,24},{24,16},{1,9},{9,1},{17,25},{25,17},{2,10},{10... | collective-permute-start | bytes 2359304 | tf_op jit(solution)/shard_map/ppermute | solution.py:657
  155.1 12.8 %collective-permute-start.8 = (bf16[192,512]{1,0:T(8,128)(2,1)S(1)}, bf16[192,512]{1,0:T(8,128)(2,1)}, u32[]{:S(2)}, u32[]{:S(2)}) collective-permute-start(bf16[192,512]{1,0:T(8,128)(2,1)S(1)} %pad_maximum_fusion), channel_id=1, source_target_pairs={{0,2},{1,3},{2,0},{3,1},{4,6},{5,7},{6,4},{7,5},{8,10},{9,11},{10,... | collective-permute-start | bytes 589832 | tf_op jit(solution)/shard_map/ppermute | solution.py:657
  157.4 13.6 %collective-permute-start.9 = (bf16[192,512]{1,0:T(8,128)(2,1)}, bf16[192,512]{1,0:T(8,128)(2,1)}, u32[]{:S(2)}, u32[]{:S(2)}) collective-permute-start(bf16[192,512]{1,0:T(8,128)(2,1)} %pad_maximum_fusion.1), channel_id=1, source_target_pairs={{0,4},{1,5},{2,6},{3,7},{4,0},{5,1},{6,2},{7,3},{8,12},{9,13},{10,... | collective-permute-start | bytes 589832 | tf_op jit(solution)/shard_map/ppermute | solution.py:657
  157.9 20.8 %collective-permute-start.13 = (bf16[2,4,96,512]{3,2,1,0:T(8,128)(2,1)S(1)}, bf16[2,4,96,512]{3,2,1,0:T(8,128)(2,1)}, u32[]{:S(2)}, u32[]{:S(2)}) collective-permute-start(bf16[2,4,96,512]{3,2,1,0:T(8,128)(2,1)S(1)} %get-tuple-element.146.refs_11_), channel_id=1, source_target_pairs={{0,16},{8,24},{16,0},{24,8},{1,17},{9,25},{17,1},{25,9},{2,18},{10... | collective-permute-start | bytes 2359304 | tf_op jit(solution)/shard_map/ppermute | solution.py:657
  159.1 16.3 %collective-permute-start.10 = (bf16[192,512]{1,0:T(8,128)(2,1)}, bf16[192,512]{1,0:T(8,128)(2,1)}, u32[]{:S(2)}, u32[]{:S(2)}) collective-permute-start(bf16[192,512]{1,0:T(8,128)(2,1)} %pad_maximum_fusion.2), channel_id=1, source_target_pairs={{0,6},{1,7},{2,4},{3,5},{4,2},{5,3},{6,0},{7,1},{8,14},{9,15},{10,... | collective-permute-start | bytes 589832 | tf_op jit(solution)/shard_map/ppermute | solution.py:657
  178.0 9.4 %collective-permute-start.12 = (bf16[4,96,512]{2,1,0:T(8,128)(2,1)S(1)}, bf16[4,96,512]{2,1,0:T(8,128)(2,1)S(1)}, u32[]{:S(2)}, u32[]{:S(2)}) collective-permute-start(bf16[4,96,512]{2,1,0:T(8,128)(2,1)S(1)} %fusion.2), channel_id=1, source_target_pairs={{0,16},{8,24},{16,0},{24,8},{1,17},{9,25},{17,1},{25,9},{2,18},{10... | collective-permute-start | bytes 1179656 | tf_op jit(solution)/shard_map/ppermute | solution.py:657
  179.9 9.1 %collective-permute-start.14 = (bf16[4,96,512]{2,1,0:T(8,128)(2,1)S(1)}, bf16[4,96,512]{2,1,0:T(8,128)(2,1)S(1)}, u32[]{:S(2)}, u32[]{:S(2)}) collective-permute-start(bf16[4,96,512]{2,1,0:T(8,128)(2,1)S(1)} %fusion.3), channel_id=1, source_target_pairs={{0,8},{8,0},{16,24},{24,16},{1,9},{9,1},{17,25},{25,17},{2,10},{10... | collective-permute-start | bytes 1179656 | tf_op jit(solution)/shard_map/ppermute | solution.py:657
  189.0 23.4 %copy-start.3 = (bf16[512,1536]{1,0:T(8,128)(2,1)S(1)}, bf16[512,1536]{1,0:T(8,128)(2,1)}, u32[]{:S(2)}) copy-start(bf16[512,1536]{1,0:T(8,128)(2,1)} %w_in.3) | copy-start | bytes 4718596
  190.6 21.9 %copy-start.1 = (bf16[512,2048]{1,0:T(8,128)(2,1)S(1)}, bf16[512,2048]{1,0:T(8,128)(2,1)}, u32[]{:S(2)}) copy-start(bf16[512,2048]{1,0:T(8,128)(2,1)} %w_up.3) | copy-start | bytes 6291460
  190.6 21.9 %copy-start.5 = (s32[3]{0:T(128)S(1)}, s32[3]{0:T(128)}, u32[]{:S(2)}) copy-start(s32[3]{0:T(128)} %pad_add_fusion.refs_0_.ids) | copy-start | bytes 40
  190.6 7.9 %collective-permute-start.15 = (bf16[192,512]{1,0:T(8,128)(2,1)S(1)}, bf16[192,512]{1,0:T(8,128)(2,1)S(1)}, u32[]{:S(2)}, u32[]{:S(2)}) collective-permute-start(bf16[192,512]{1,0:T(8,128)(2,1)S(1)} %pad_maximum_fusion.3), channel_id=1, source_target_pairs={{0,2},{1,3},{2,0},{3,1},{4,6},{5,7},{6,4},{7,5},{8,10},{9,11},{10,... | collective-permute-start | bytes 589832 | tf_op jit(solution)/shard_map/ppermute | solution.py:657
  190.7 14.0 %collective-permute-start.16 = (bf16[192,512]{1,0:T(8,128)(2,1)S(1)}, bf16[192,512]{1,0:T(8,128)(2,1)S(1)}, u32[]{:S(2)}, u32[]{:S(2)}) collective-permute-start(bf16[192,512]{1,0:T(8,128)(2,1)S(1)} %pad_maximum_fusion.4), channel_id=1, source_target_pairs={{0,4},{1,5},{2,6},{3,7},{4,0},{5,1},{6,2},{7,3},{8,12},{9,13},{10,... | collective-permute-start | bytes 589832 | tf_op jit(solution)/shard_map/ppermute | solution.py:657
  192.9 15.8 %collective-permute-start.17 = (bf16[192,512]{1,0:T(8,128)(2,1)S(1)}, bf16[192,512]{1,0:T(8,128)(2,1)S(1)}, u32[]{:S(2)}, u32[]{:S(2)}) collective-permute-start(bf16[192,512]{1,0:T(8,128)(2,1)S(1)} %pad_maximum_fusion.5), channel_id=1, source_target_pairs={{0,6},{1,7},{2,4},{3,5},{4,2},{5,3},{6,0},{7,1},{8,14},{9,15},{10,... | collective-permute-start | bytes 589832 | tf_op jit(solution)/shard_map/ppermute | solution.py:657
  194.4 17.7 %collective-permute-start.23 = (bf16[192,512]{1,0:T(8,128)(2,1)S(1)}, bf16[192,512]{1,0:T(8,128)(2,1)S(1)}, u32[]{:S(2)}, u32[]{:S(2)}) collective-permute-start(bf16[192,512]{1,0:T(8,128)(2,1)S(1)} %add_convert_fusion.9.p0), channel_id=1, source_target_pairs={{0,24},{8,16},{16,8},{24,0},{1,25},{9,17},{17,9},{25,1},{2,26},{10... | collective-permute-start | bytes 589832 | tf_op jit(solution)/shard_map/ppermute | solution.py:657
  196.8 15.7 %collective-permute-start.22 = (bf16[192,512]{1,0:T(8,128)(2,1)S(1)}, bf16[192,512]{1,0:T(8,128)(2,1)S(1)}, u32[]{:S(2)}, u32[]{:S(2)}) collective-permute-start(bf16[192,512]{1,0:T(8,128)(2,1)S(1)} %add_convert_fusion.9.p0), channel_id=1, source_target_pairs={{0,16},{8,24},{16,0},{24,8},{1,17},{9,25},{17,1},{25,9},{2,18},{10... | collective-permute-start | bytes 589832 | tf_op jit(solution)/shard_map/ppermute | solution.py:657
  198.5 13.9 %collective-permute-start.21 = (bf16[192,512]{1,0:T(8,128)(2,1)S(1)}, bf16[192,512]{1,0:T(8,128)(2,1)S(1)}, u32[]{:S(2)}, u32[]{:S(2)}) collective-permute-start(bf16[192,512]{1,0:T(8,128)(2,1)S(1)} %add_convert_fusion.9.p0), channel_id=1, source_target_pairs={{0,8},{8,0},{16,24},{24,16},{1,9},{9,1},{17,25},{25,17},{2,10},{10... | collective-permute-start | bytes 589832 | tf_op jit(solution)/shard_map/ppermute | solution.py:657
  208.9 8.7 %collective-permute-start.20 = (bf16[192,512]{1,0:T(8,128)(2,1)S(1)}, bf16[192,512]{1,0:T(8,128)(2,1)S(1)}, u32[]{:S(2)}, u32[]{:S(2)}) collective-permute-start(bf16[192,512]{1,0:T(8,128)(2,1)S(1)} %add_convert_fusion.8.p0), channel_id=1, source_target_pairs={{0,24},{8,16},{16,8},{24,0},{1,25},{9,17},{17,9},{25,1},{2,26},{10... | collective-permute-start | bytes 589832 | tf_op jit(solution)/shard_map/ppermute | solution.py:657
  211.3 7.8 %collective-permute-start.19 = (bf16[192,512]{1,0:T(8,128)(2,1)S(1)}, bf16[192,512]{1,0:T(8,128)(2,1)S(1)}, u32[]{:S(2)}, u32[]{:S(2)}) collective-permute-start(bf16[192,512]{1,0:T(8,128)(2,1)S(1)} %add_convert_fusion.8.p0), channel_id=1, source_target_pairs={{0,16},{8,24},{16,0},{24,8},{1,17},{9,25},{17,1},{25,9},{2,18},{10... | collective-permute-start | bytes 589832 | tf_op jit(solution)/shard_map/ppermute | solution.py:657
  212.1 7.0 %collective-permute-start.18 = (bf16[192,512]{1,0:T(8,128)(2,1)S(1)}, bf16[192,512]{1,0:T(8,128)(2,1)S(1)}, u32[]{:S(2)}, u32[]{:S(2)}) collective-permute-start(bf16[192,512]{1,0:T(8,128)(2,1)S(1)} %add_convert_fusion.8.p0), channel_id=1, source_target_pairs={{0,8},{8,0},{16,24},{24,16},{1,9},{9,1},{17,25},{25,17},{2,10},{10... | collective-permute-start | bytes 589832 | tf_op jit(solution)/shard_map/ppermute | solution.py:657
  (18 other events, 144.6 us)

commit v6 on v5

--- a/solution.py
+++ b/solution.py
@@ -264,8 +264,39 @@
     bias[...] = jnp.where(allowed, 0.0, -1e30)
 
 
-def time_kernel(labels, gain, scale, x2_in, grad_in, w_in_in, w_out_in, w_up_in, w_down_in, *rest):
-    outs, rest = rest[:10], rest[10:]
+def send_moved(copies, ids, held, outs):
+    if len(outs) == 1:
+        copies.send(held, outs[0])
+        return
+    for d in range(4):
+        at = 2 * (ids[1] ^ d)
+        copies.send(held.at[at + ids[0]], outs[0].at[d])
+        copies.send(held.at[at + 1 - ids[0]], outs[1].at[d])
+
+
+def fetch_moved(copies, ids, pieces, held):
+    if len(pieces) == 1:
+        return [copies.fetch(pieces[0], held)]
+    near, far, *others = pieces
+    at = 2 * ids[1]
+    got = [copies.fetch(near.at[0], held.at[at + ids[0]])]
+    got.append(copies.fetch(far.at[0], held.at[at + 1 - ids[0]]))
+    for d, piece in enumerate(others, 1):
+        at = 2 * (ids[1] ^ d)
+        got.append(copies.fetch(piece.at[0], held.at[at + ids[0]]))
+        got.append(copies.fetch(piece.at[1], held.at[at + 1 - ids[0]]))
+    return got
+
+
+def exchange_pieces(arrays):
+    if len(arrays) == 1:
+        return [lax.all_to_all(arrays[0], "tm", split_axis=0, concat_axis=0, tiled=True)]
+    near, far = arrays[0], swap(arrays[1], "tm", 8, 1)
+    return [near, far] + [swap(jnp.stack([near[d], far[d]]), "tm", 8, 2 * d) for d in range(1, 4)]
+
+
+def time_kernel(moved, labels, ids, gain, scale, x2_in, grad_in, w_in_in, w_out_in, w_up_in, w_down_in, *rest):
+    g0_outs, outs, rest = rest[:moved], (None,) + rest[moved : moved + 9], rest[moved + 9 :]
     x2, grad, w_in, w_out, w_up, w_down = rest[:6]
     held = rest[6:16]
     g0, out, z0, gqkv, o, e1, z1, eu, h, e2 = held
@@ -327,7 +358,7 @@
         block_of(g1 + unit_backward(gn * gain[...], unit0, inverse0), g0.at[:, pl.ds(pack, 1)])
 
     together([run(pack) for pack in range(packs)])
-    copies.send(g0, outs[0])
+    send_moved(copies, ids, g0, g0_outs)
     copies.send(out, outs[1])
     copies.finish()
 
@@ -398,8 +429,9 @@
         copy.wait()
 
 
-def space_kernel(hierarchical, ids, scale, inv1, *rest):
-    (g2_in, slope_in, z1_in, w_out_in, w_up_in, w_down_in, qkv_in, p_in), rest = rest[:8], rest[8:]
+def space_kernel(hierarchical, pieces, ids, scale, inv1, *rest):
+    g2_in, rest = rest[:pieces], rest[pieces:]
+    (slope_in, z1_in, w_out_in, w_up_in, w_down_in, qkv_in, p_in), rest = rest[:7], rest[7:]
     shared, one, rest = rest[:3], rest[3:11], rest[11:]
     (g1_out, gqkv_out), outs, scratch = rest[:2], rest[2 : 6 if hierarchical else 5], rest[6 if hierarchical else 5 :]
     g2, slope, w_out, w_up, w_down, qkv, p, go, g1, gp, gs = scratch[:11]
@@ -407,7 +439,7 @@
     copies = Copies(scratch[-1])
     packs, tokens, _ = g1.shape
     have = packs * tokens
-    got_g2 = copies.fetch(g2_in, g2)
+    got_g2 = fetch_moved(copies, ids, g2_in, g2)
     got_down = copies.fetch(w_down_in, w_down)
     got_slope = [copies.fetch(slope_in.at[pack], slope.at[pack]) for pack in range(packs)]
     got_up = copies.fetch(w_up_in, w_up)
@@ -427,7 +459,7 @@
                 got_rest.append(copies.fetch(source.at[pack], target.at[rows]))
         for source, target in zip(one, whole):
             got_rest.append(copies.fetch(source.at[0], target.at[pl.ds(have, tokens)]))
-    wait(got_g2)
+    wait(*got_g2)
 
     def run(pack):
         rows = slice(pack * tokens, (pack + 1) * tokens)
@@ -637,10 +669,11 @@
 
 def manual_call(kernel, ids, args, outs, scratch, semaphores, small=0, after=(), flops=0):
     anywhere = pl.BlockSpec(memory_space=pl.ANY)
+    scalars = ids if isinstance(ids, tuple) else (ids,)
     return pl.pallas_call(
-        without(kernel, 1 + len(args), len(after)),
+        without(kernel, len(scalars) + len(args), len(after)),
         out_shape=[jax.ShapeDtypeStruct(shape, dtype) for shape, dtype in outs],
-        in_specs=[pl.BlockSpec(memory_space=pltpu.SMEM)]
+        in_specs=[pl.BlockSpec(memory_space=pltpu.SMEM)] * len(scalars)
         + [pl.BlockSpec(memory_space=pltpu.VMEM)] * small
         + [anywhere] * (len(args) - small + len(after)),
         out_specs=[anywhere] * len(outs),
@@ -650,7 +683,7 @@
         cost_estimate=pl.CostEstimate(
             flops=int(flops * COST), bytes_accessed=0, transcendentals=0
         ),
-    )(ids, *args, *after)
+    )(*scalars, *args, *after)
 
 
 def swap(array, axis, size, mask):
@@ -673,15 +706,19 @@
     return halves, [add(a[1], b[1], half[1]) for a, b, half in zip(mine, got, halves)]
 
 
-def stream_rows(mine, got, halves, near):
+def stream_rows(mine, got, halves, near, *note):
     last = [swap(near[0], "stream", 4, 2), swap(near[1], "stream", 4, 1)]
     terms = list(zip(mine, got, halves, last))
     return [
-        jnp.concatenate([add(a[0][d], b[0][d], half[0][d], end[d]) for a, b, half, end in terms])
+        jnp.concatenate([add(a[0][d], b[0][d], half[0][d], end[d], *note) for a, b, half, end in terms])
         for d in range(4)
     ]
 
 
+def z_got(rows):
+    return [swap(rows[d], "tm", 8, 2 * d) for d in range(1, 4)]
+
+
 def z_sum(rows):
     return add(rows[0], *[swap(rows[d], "tm", 8, 2 * d) for d in range(1, 4)])
 
@@ -690,78 +727,17 @@
     return [final] + [swap(final, "stream", 4, d) for d in range(1, 4)]
 
 
-def marker(array):
-    def kernel(source, out):
-        out[...] = jnp.zeros_like(out)
+def marker(*arrays):
+    def kernel(*refs):
+        refs[-1][...] = jnp.zeros_like(refs[-1])
 
     return pl.pallas_call(
         kernel,
         out_shape=jax.ShapeDtypeStruct((1, CHUNK), F32),
-        in_specs=[pl.BlockSpec(memory_space=pl.ANY)],
+        in_specs=[pl.BlockSpec(memory_space=pl.ANY)] * len(arrays),
         out_specs=pl.BlockSpec(memory_space=pltpu.VMEM),
         cost_estimate=pl.CostEstimate(flops=10**12, bytes_accessed=10**8, transcendentals=0),
-    )(array)
-
-
-def stream_total(parts, own):
-    return add(*own, *[swap(part, "stream", 4, d + 1) for d, part in enumerate(parts)])
-
-
-def stream_total(parts, own):
-    return add(*own, *[swap(part, "stream", 4, d + 1) for d, part in enumerate(parts)])
-
-
-def stream_sum(parts, own):
-    got = [swap(part, "stream", 4, d + 1) for d, part in enumerate(parts)]
-    return [add(*[term[d] for term in (*own, *got)]) for d in range(4)]
-
-
-def halved_sum(mine, got, far, first, second):
-    half = swap(far, "stream", 4, first)
-    near = swap(add(mine[1], got[1], half[1]), "stream", 4, second)
-    return [(mine[0][d], got[0][d], half[0][d], near[d]) for d in range(4)]
-
-
-def z_sum(rows):
-    return add(rows[0], *[swap(rows[d], "tm", 8, 2 * d) for d in range(1, 4)])
-
-
-def gather_parts(final):
-    return [final] + [swap(final, "stream", 4, d) for d in range(1, 4)]
-
-
-def marker(array):
-    def kernel(source, out):
-        out[...] = jnp.zeros_like(out)
-
-    return pl.pallas_call(
-        kernel,
-        out_shape=jax.ShapeDtypeStruct((1, CHUNK), F32),
-        in_specs=[pl.BlockSpec(memory_space=pl.ANY)],
-        out_specs=pl.BlockSpec(memory_space=pltpu.VMEM),
-        cost_estimate=pl.CostEstimate(flops=10**12, bytes_accessed=10**8, transcendentals=0),
-    )(array)
-
-
-def add_call(mine, got, after):
-    def kernel(a, b, out):
-        out[...] = (a[...].astype(F32) + b[...].astype(F32)).astype(BF)
-
-    block = pl.BlockSpec((1,) + mine.shape[1:], lambda i: (i,) + (0,) * (mine.ndim - 1))
-    return pl.pallas_call(
-        without(kernel, 2, len(after)),
-        out_shape=jax.ShapeDtypeStruct(mine.shape, BF),
-        grid=(mine.shape[0],),
-        in_specs=[block, block] + [pl.BlockSpec(memory_space=pl.ANY)] * len(after),
-        out_specs=block,
-        compiler_params=pltpu.CompilerParams(vmem_limit_bytes=VMEM),
-    )(mine, got, *after)
-
-
-def scatter_sum(total):
-    share = lax.psum_scatter(total, "stream", scatter_dimension=0)
-    groups = [[0, 2, 4, 6], [1, 3, 5, 7]]
-    return lax.psum_scatter(share, "tm", scatter_dimension=0, axis_index_groups=groups)
+    )(*arrays)
 
 
 def as_row(col):
@@ -958,12 +934,14 @@
         for shape in (shared_w, shared_3, shared_w, shared_w, shared_w, shared_h, shared_h, shared_w)
     ]
     square = (some, HEADS, tokens, tokens)
-    g0, out, tz0, tgqkv, to, te1, tz1, teu, th, te2 = manual_call(
-        time_kernel,
-        clip_labels,
+    halves = (slots // 2,) + x2.shape[1:]
+    g0_outs = [(halves, BF)] * 2 if hierarchical else [(x2.shape, BF)]
+    *g0, out, tz0, tgqkv, to, te1, tz1, teu, th, te2 = manual_call(
+        functools.partial(time_kernel, len(g0_outs)),
+        (clip_labels, ids),
         [row(time_gain), row(time_scale), x2_moved, grad_moved]
         + [time_input, time_output, time_up, time_down],
-        time_outs,
+        g0_outs + time_outs[1:],
         [(x2.shape, BF)] * 2
         + [(w.shape, BF) for w in (time_input, time_output, time_up, time_down)]
         + time_outs
@@ -978,12 +956,12 @@
             ((some, 4, tokens, tokens), BF),
             (square, BF),
         ],
-        6 + 8 * some + 2,
+        6 + 8 * some + 9,
         small=2,
         after=(sz0_one,),
         flops=3 * some * flops,
     )
-    g0_moved = exchange(g0)
+    g0_moved = exchange_pieces(g0)
     out, g0_moved = lax.optimization_barrier((out, g0_moved))
     out_moved = exchange(out)
 
@@ -1005,7 +983,7 @@
             flops=packs * flops,
         )
         time_got = [swap(other, "tm", 8, 1) for other in time_terms[1::2]]
-        time_far = far_parts(time_terms[::2], time_got, marker(g0_moved))
+        time_far = far_parts(time_terms[::2], time_got, marker(*g0_moved[2:]))
         held_back = time_far
     else:
         grad_one = jnp.pad(tgv_one, ((0, 0), (0, 0), (2 * width, 0)))
@@ -1017,15 +995,15 @@
     whole_shapes = [((everything, a.shape[2]), BF) for a in space_one]
     parts_shapes = [((4, 4, 96, CHUNK), BF)] * 4
     sg1, sgqkv, *weights = manual_call(
-        functools.partial(space_kernel, hierarchical),
+        functools.partial(space_kernel, hierarchical, len(g0_moved)),
         ids,
-        [row(space_scale), sinv1, g0_moved, sslope, sz1, space_output, space_up, space_down]
+        [row(space_scale), sinv1, *g0_moved, sslope, sz1, space_output, space_up, space_down]
         + [sqkv, sp, sh, sz0, so]
         + space_one,
         [(shared_w, F32), (shared_3, BF)]
         + (parts_shapes if hierarchical else [whole_shapes[i] for i in (1, 3, 7)]),
         [
-            (g0_moved.shape, BF),
+            (x2.shape, BF),
             (sslope.shape, BF),
             (space_output.shape, BF),
             (space_up.shape, BF),
@@ -1039,7 +1017,7 @@
         ]
         + whole_shapes
         + (parts_shapes if hierarchical else []),
-        80,
+        96,
         small=2,
         after=held_back,
         flops=2 * packs * flops,
@@ -1052,7 +1030,6 @@
         mine = weights[::2]
         got = [swap(other, "tm", 8, 1) for other in weights[1::2]]
         far = far_parts(mine, got, marker(time_near[1]))
-        far, time_halves = lax.optimization_barrier((far, time_halves))
         held_back = far
     input_grad, result = shared.call(
         space_back_in,
@@ -1070,10 +1047,11 @@
         after=held_back,
     )
     if hierarchical:
+        time_halves, input_grad = lax.optimization_barrier((time_halves, input_grad))
         time_rows = stream_rows(time_mine, time_got, time_halves, time_near)
-        time_final = z_sum(time_rows)
-        got, time_final, input_grad = lax.optimization_barrier((got, time_final, input_grad))
-        final = z_sum(stream_rows(mine, got, *near_parts(mine, got, far)))
+        time_last = z_got(time_rows)
+        time_final = add(time_rows[0], *time_last)
+        final = z_sum(stream_rows(mine, got, *near_parts(mine, got, far), marker(*time_last)))
         grads = finish_call(
             finish_kernel,
             ids,

time: 226 us -> 220 us (0.973)
  starting transfers between devices: 49.6 us -> 44.4 us
  waiting for transfers between devices: 38.3 us -> 34 us
    all_to_all x4 -> x3, starting transfers between devices: 25.2 us -> 16.6 us  [exchange(): return lax.all_to_all(array, 'tm', split_axis=0, concat_axis=0, tiled=True)]
    all_to_all x4 -> x3, waiting for transfers between devices: 4.23 us -> 0.71 us  [exchange(): return lax.all_to_all(array, 'tm', split_axis=0, concat_axis=0, tiled=True)]
    convert_element_type x12, other arithmetic: 18.6 us -> 22 us  [add(): return total.astype(BF)]
    ppermute x24 -> x28, starting transfers between devices: 24.4 us -> 27.8 us  [swap(): return lax.ppermute(array, axis, [(i, i ^ mask) for i in range(size)])]
    ppermute x24 -> x28, waiting for transfers between devices: 34.1 us -> 33.3 us  [swap(): return lax.ppermute(array, axis, [(i, i ^ mask) for i in range(size)])]
  transfers between devices with their start and end apart: 28 -> 31, of which waited for: 12 -> 13; matrix products, arithmetic and copies ran while one was open for 9% -> 10% of each run, Pallas kernels for 36% -> 38%
where the time goes in v6:
time: 220 us; the launch traced here: 216 us
  Pallas kernels  109 us (50%)
  starting transfers between devices  44.4 us (20%)
  waiting for transfers between devices  34 us (15%)
  other arithmetic  22.7 us (10%)
  local copies, waits for them, and re-layouts  3.98 us (2%)
    pallas_call x3, Pallas kernels, manual_call(): pl.pallas_call(without(kernel, len(scalars) + len(args), len(after)), out...  57.8 us
    pallas_call x3, Pallas kernels, call(): pl.pallas_call(without(kernel, len(scalars) + len(args), unread), out_sha...  43.2 us
    ppermute x28, waiting for transfers between devices, swap(): return lax.ppermute(array, axis, [(i, i ^ mask) for i in range(size)])  33.3 us
    ppermute x28, starting transfers between devices, swap(): return lax.ppermute(array, axis, [(i, i ^ mask) for i in range(size)])  27.8 us
    convert_element_type x12, other arithmetic, add(): return total.astype(BF)  22 us
    all_to_all x3, starting transfers between devices, exchange(): return lax.all_to_all(array, 'tm', split_axis=0, concat_axis=0, tiled=True)  16.6 us
  transfers between devices with their start and end apart: 31, of which 13 were waited for; matrix products, arithmetic and copies ran while one was open for 10% of the time, Pallas kernels for 38%

profile of v6, /device:TPU:16, one launch (start us, length us, event | category | flops | bytes accessed | tf_op | source)
XLA Modules:
  0.0 216.0 jit_solution(10983476076940767853)
XLA Ops:
  0.6 2.8 %shard_map.254.refs_8_ = bf16[8,3,32,512]{3,2,1,0:T(8,128)(2,1)} custom-call(s32[4,8]{1,0:T(4,128)} %refs_0_.7, bf16[4,1,256,512]{3,2,1,0:T(8,128)(2,1)} %refs_2_.2), custom_call_target="tpu_custom_call" | custom-call | tf_op jit(solution)/shard_map/pallas_call | solution.py:816
  3.5 5.2 %all-to-all-start = ((bf16[8,3,32,512]{3,2,1,0:T(8,128)(2,1)}), bf16[8,3,32,512]{3,2,1,0:T(8,128)(2,1)S(1)}, u32[]{:S(2)}, u32[]{:S(2)}) async-start(bf16[8,3,32,512]{3,2,1,0:T(8,128)(2,1)} %shard_map.254.refs_8_), calls=%async_computation | async-start | bytes 1572864 | tf_op jit(solution)/shard_map/all_to_all | solution.py:863
  8.7 17.0 %shard_map.255 = (bf16[8,3,32,512]{3,2,1,0:T(8,128)(2,1)}, bf16[3,256,512]{2,1,0:T(8,128)(2,1)}, f32[3,256,128]{2,1,0:T(8,128)}, bf16[3,256,1536]{2,1,0:T(8,128)...) custom-call(s32[4,8]{1,0:T(4,128)} %refs_0_.7, ...), custom_call_target="tpu_custom_call" | custom-call | flops 4831838208 | bytes 8130560 | tf_op jit(solution)/shard_map/pallas_call | solution.py:566
  26.4 7.0 %all-to-all-start.1 = ((bf16[8,3,32,512]{3,2,1,0:T(8,128)(2,1)}), bf16[8,3,32,512]{3,2,1,0:T(8,128)(2,1)S(1)}, u32[]{:S(2)}, u32[]{:S(2)}) async-start(bf16[8,3,32,512]{3,2,1,0:T(8,128)(2,1)} %get-tuple-element.92.refs_15_), calls=%async_computation.1 | async-start | bytes 1572864 | tf_op jit(solution)/shard_map/all_to_all | solution.py:863
  34.0 18.8 %shard_map.256 = (f32[4,1,256,512]{3,2,1,0:T(8,128)}, f32[4,1,256,512]{3,2,1,0:T(8,128)}, bf16[1,256,512]{2,1,0:T(8,128)(2,1)}, bf16[1,256,512]{2,1,0:T(8,128)(2...) custom-call(s32[4,8]{1,0:T(4,128)} %refs_0_.7, ...), custom_call_target="tpu_custom_call" | custom-call | flops 9663676416 | bytes 15474688 | tf_op jit(solution)/shard_map/pallas_call | solution.py:566
  53.8 23.3 %shard_map.257 = (bf16[4,3,32,512]{3,2,1,0:T(8,128)(2,1)}, bf16[4,3,32,512]{3,2,1,0:T(8,128)(2,1)}, bf16[8,3,32,512]{3,2,1,0:T(8,128)(2,1)}, bf16[3,256,512]{2,1...) custom-call(s32[4,8]{1,0:T(4,128)} %refs_0_.7, ...), custom_call_target="tpu_custom_call" | custom-call | flops 14495514624 | tf_op jit(solution)/shard_map/pallas_call | solution.py:673
  79.1 1.5 collective-permute-start.3
  81.3 1.5 collective-permute-start.5
  82.8 13.2 %shard_map.258 = (bf16[4,4,96,512]{3,2,1,0:T(8,128)(2,1)}, bf16[4,4,96,512]{3,2,1,0:T(8,128)(2,1)}, bf16[4,4,96,512]{3,2,1,0:T(8,128)(2,1)}, bf16[4,4,96,512]{3,2,1,0:T(8,128)(2,1)}) custom-call(s32[3]{0:T(128)} %pad_add_fusion.refs_1_.refs_0_.ids, bf16[3,256,512]{2,1,0:T(8,128)(2,1)} %get-tuple-element.95.refs_1_, ...), custom_call_target="tpu_custom_call" | custom-call | flops 6442450944 | tf_op jit(solution)/shard_map/pallas_call | solution.py:673
  96.6 3.5 %collective-permute-done.5.refs_2_.refs_7_ = bf16[2,3,32,512]{3,2,1,0:T(8,128)(2,1)S(1)} collective-permute-done((bf16[2,3,32,512]{3,2,1,0:T(8,128)(2,1)S(1)}, bf16[2,3,32,512]{3,2,1,0:T(8,128)(2,1)S(1)}, u32[]{:S(2)}, u32[]{:S(2)}) %collective-permute-start.5) | collective-permute-done | bytes 196640 | tf_op jit(solution)/shard_map/ppermute | solution.py:690
  100.8 4.4 %all-to-all-start.2 = ((bf16[8,3,32,512]{3,2,1,0:T(8,128)(2,1)}), bf16[8,3,32,512]{3,2,1,0:T(8,128)(2,1)}, u32[]{:S(2)}, u32[]{:S(2)}) async-start(bf16[8,3,32,512]{3,2,1,0:T(8,128)(2,1)} %get-tuple-element.142), calls=%async_computation.2 | async-start | bytes 1572864 | tf_op jit(solution)/shard_map/all_to_all | solution.py:863
  107.1 3.0 %add_convert_fusion.2 = (bf16[2,4,96,512]{3,2,1,0:T(8,128)(2,1)}, bf16[2,4,96,512]{3,2,1,0:T(8,128)(2,1)}) fusion(bf16[4,4,96,512]{3,2,1,0:T(8,128)(2,1)} %collective-permute-done.1, bf16[4,4,96,512]{3,2,1,0:T(8,128)(2,1)S(1)} %copy-done.13, f32[512]{0:T(512)} %bitcast.151, bf16[4,4,96,512]{3,2,1,0:T(8,128)(2,1)} %collective-permute-done, ...), kind=kLoop, calls=%fused_computation.2 | loop fusion | flops 3932160 | bytes 4720640 | tf_op jit(solution)/shard_map/convert_element_type | solution.py:697
  113.1 21.3 %shard_map.260 = (f32[3,256,512]{2,1,0:T(8,128)}, bf16[3,256,1536]{2,1,0:T(8,128)(2,1)}, bf16[4,4,96,512]{3,2,1,0:T(8,128)(2,1)}, bf16[4,4,96,512]{3,2,1,0:T(8,1...) custom-call(s32[3]{0:T(128)} %pad_add_fusion.refs_1_.refs_0_.ids, f32[1,512]{1,0:T(1,128)} %bitcast.146, ...), custom_call_target="tpu_custom_call" | custom-call | flops 12884901888 | tf_op jit(solution)/shard_map/pallas_call | solution.py:673
  135.0 2.2 fusion.refs_0_
  140.5 2.1 add_convert_fusion
  145.5 7.4 %shard_map.262 = (f32[4,1,256,512]{3,2,1,0:T(8,128)}, f32[4,1,256,512]{3,2,1,0:T(8,128)}) custom-call(s32[4,8]{1,0:T(4,128)} %refs_0_.7, bf16[3,256,1536]{2,1,0:T(8,128)(2,1)} %get-tuple-element.139.refs_1_, bf16[512,1536]{1,0:T(8,128)(2,1)} %w_in.2, f32[1,512]{1,0:T(1,128)} %bitcast.136, ...), custom_call_target="tpu_custom_call", output_to_operand_aliasing={{0}: (8, {}), {1}: (9, {})} | custom-call | flops 1207959552 | bytes 13240320 | tf_op jit(solution)/shard_map/pallas_call | solution.py:566
  152.8 2.3 %fusion.4 = (bf16[96,512]{1,0:T(8,128)(2,1)}, bf16[96,512]{1,0:T(8,128)(2,1)S(1)}, bf16[96,512]{1,0:T(8,128)(2,1)S(1)}, bf16[96,512]{1,0:T(8,128)(2,1)S(1)}) fusion(bf16[4,96,512]{2,1,0:T(8,128)(2,1)} %collective-permute-done.13, bf16[2,4,96,512]{3,2,1,0:T(8,128)(2,1)} %copy-done.16, bf16[4,4,96,512]{3,2,1,0:T(8,128)(2,1)} %collective-permute-done.1, ...), kind=kLoop, calls=%fused_computation.24 | loop fusion | flops 1572864 | bytes 1966080 | tf_op jit(solution)/shard_map/convert_element_type | solution.py:697
  155.2 2.3 %fusion.5 = (bf16[96,512]{1,0:T(8,128)(2,1)}, bf16[96,512]{1,0:T(8,128)(2,1)S(1)}, bf16[96,512]{1,0:T(8,128)(2,1)S(1)}, bf16[96,512]{1,0:T(8,128)(2,1)S(1)}) fusion(bf16[4,96,512]{2,1,0:T(8,128)(2,1)} %collective-permute-done.12, bf16[2,4,96,512]{3,2,1,0:T(8,128)(2,1)} %collective-permute-done.9, bf16[4,4,96,512]{3,2,1,0:T(8,128)(2,1)} %collective-permute-done, ...), kind=kLoop, calls=%fused_computation.26 | loop fusion | flops 1572864 | bytes 1966080 | tf_op jit(solution)/shard_map/convert_element_type | solution.py:697
  157.5 1.5 collective-permute-start.14
  161.2 6.4 %collective-permute-done.17 = bf16[2,4,96,512]{3,2,1,0:T(8,128)(2,1)} collective-permute-done((bf16[2,4,96,512]{3,2,1,0:T(8,128)(2,1)S(1)}, bf16[2,4,96,512]{3,2,1,0:T(8,128)(2,1)}, u32[]{:S(2)}, u32[]{:S(2)}) %collective-permute-start.17) | collective-permute-done | bytes 786464 | tf_op jit(solution)/shard_map/ppermute | solution.py:690
  167.6 2.1 fusion.3
  171.1 2.0 fusion.1
  173.7 3.6 %collective-permute-done.16.refs_2_ = bf16[192,512]{1,0:T(8,128)(2,1)} collective-permute-done((bf16[192,512]{1,0:T(8,128)(2,1)S(1)}, bf16[192,512]{1,0:T(8,128)(2,1)}, u32[]{:S(2)}, u32[]{:S(2)}) %collective-permute-start.16) | collective-permute-done | bytes 196640 | tf_op jit(solution)/shard_map/ppermute | solution.py:690
  177.9 2.3 %collective-permute-done.18 = bf16[4,96,512]{2,1,0:T(8,128)(2,1)} collective-permute-done((bf16[4,96,512]{2,1,0:T(8,128)(2,1)}, bf16[4,96,512]{2,1,0:T(8,128)(2,1)}, u32[]{:S(2)}, u32[]{:S(2)}) %collective-permute-start.18) | collective-permute-done | bytes 393248 | tf_op jit(solution)/shard_map/ppermute | solution.py:690
  180.2 1.7 fusion.19
  183.1 1.8 fusion.27
  193.7 5.8 %collective-permute-done.20 = bf16[192,512]{1,0:T(8,128)(2,1)S(1)} collective-permute-done((bf16[192,512]{1,0:T(8,128)(2,1)S(1)}, bf16[192,512]{1,0:T(8,128)(2,1)S(1)}, u32[]{:S(2)}, u32[]{:S(2)}) %collective-permute-start.20) | collective-permute-done | bytes 196640 | tf_op jit(solution)/shard_map/ppermute | solution.py:690
  199.5 4.0 %collective-permute-done.21 = bf16[192,512]{1,0:T(8,128)(2,1)S(1)} collective-permute-done((bf16[192,512]{1,0:T(8,128)(2,1)S(1)}, bf16[192,512]{1,0:T(8,128)(2,1)S(1)}, u32[]{:S(2)}, u32[]{:S(2)}) %collective-permute-start.21) | collective-permute-done | bytes 196640 | tf_op jit(solution)/shard_map/ppermute | solution.py:690
  207.2 1.9 shard_map.265
  209.2 2.8 %collective-permute-done.24.p3 = bf16[192,512]{1,0:T(8,128)(2,1)S(1)} collective-permute-done((bf16[192,512]{1,0:T(8,128)(2,1)S(1)}, bf16[192,512]{1,0:T(8,128)(2,1)S(1)}, u32[]{:S(2)}, u32[]{:S(2)}) %collective-permute-start.24) | collective-permute-done | bytes 196640 | tf_op jit(solution)/shard_map/ppermute | solution.py:690
  212.0 1.7 collective-permute-done.23.p2
  213.8 1.9 shard_map.264
  (124 shorter events, 36.1 us)
Async XLA Ops:
  3.5 22.9 %all-to-all-start = ((bf16[8,3,32,512]{3,2,1,0:T(8,128)(2,1)}), bf16[8,3,32,512]{3,2,1,0:T(8,128)(2,1)S(1)}, u32[]{:S(2)}, u32[]{:S(2)}) async-start(bf16[8,3,32,512]{3,2,1,0:T(8,128)(2,1)} %shard_map.254.refs_8_), calls=%async_computation | async-start | bytes 1572864 | tf_op jit(solution)/shard_map/all_to_all | solution.py:863
  26.4 26.5 %copy-start.14 = (bf16[8,3,32,512]{3,2,1,0:T(8,128)(2,1)}, bf16[8,3,32,512]{3,2,1,0:T(8,128)(2,1)S(1)}, u32[]{:S(2)}) copy-start(bf16[8,3,32,512]{3,2,1,0:T(8,128)(2,1)S(1)} %all-to-all-done.refs_5_) | copy-start | bytes 2359300
  26.4 26.5 %all-to-all-start.1 = ((bf16[8,3,32,512]{3,2,1,0:T(8,128)(2,1)}), bf16[8,3,32,512]{3,2,1,0:T(8,128)(2,1)S(1)}, u32[]{:S(2)}, u32[]{:S(2)}) async-start(bf16[8,3,32,512]{3,2,1,0:T(8,128)(2,1)} %get-tuple-element.92.refs_15_), calls=%async_computation.1 | async-start | bytes 1572864 | tf_op jit(solution)/shard_map/all_to_all | solution.py:863
  77.1 2.0 collective-permute-start.2
  79.1 17.5 %collective-permute-start.3 = (bf16[2,3,32,512]{3,2,1,0:T(8,128)(2,1)S(1)}, bf16[2,3,32,512]{3,2,1,0:T(8,128)(2,1)S(1)}, u32[]{:S(2)}, u32[]{:S(2)}) collective-permute-start(bf16[2,3,32,512]{3,2,1,0:T(8,128)(2,1)S(1)} %pad_maximum_fusion), channel_id=1, source_target_pairs={{0,2},{1,3},{2,0},{3,1},{4,6},{5,7},{6,4},{7,5},{8,10},{9,11},{10,... | collective-permute-start | bytes 589832 | tf_op jit(solution)/shard_map/ppermute | solution.py:690
  80.7 15.9 %collective-permute-start.4 = (bf16[2,3,32,512]{3,2,1,0:T(8,128)(2,1)S(1)}, bf16[2,3,32,512]{3,2,1,0:T(8,128)(2,1)S(1)}, u32[]{:S(2)}, u32[]{:S(2)}) collective-permute-start(bf16[2,3,32,512]{3,2,1,0:T(8,128)(2,1)S(1)} %pad_maximum_fusion.1), channel_id=1, source_target_pairs={{0,4},{1,5},{2,6},{3,7},{4,0},{5,1},{6,2},{7,3},{8,12},{9,13},{10,... | collective-permute-start | bytes 589832 | tf_op jit(solution)/shard_map/ppermute | solution.py:690
  81.3 18.8 %collective-permute-start.5 = (bf16[2,3,32,512]{3,2,1,0:T(8,128)(2,1)S(1)}, bf16[2,3,32,512]{3,2,1,0:T(8,128)(2,1)S(1)}, u32[]{:S(2)}, u32[]{:S(2)}) collective-permute-start(bf16[2,3,32,512]{3,2,1,0:T(8,128)(2,1)S(1)} %pad_maximum_fusion.2), channel_id=1, source_target_pairs={{0,6},{1,7},{2,4},{3,5},{4,2},{5,3},{6,0},{7,1},{8,14},{9,15},{10,... | collective-permute-start | bytes 589832 | tf_op jit(solution)/shard_map/ppermute | solution.py:690
  96.0 9.7 %collective-permute-start = (bf16[4,4,96,512]{3,2,1,0:T(8,128)(2,1)}, bf16[4,4,96,512]{3,2,1,0:T(8,128)(2,1)}, u32[]{:S(2)}, u32[]{:S(2)}) collective-permute-start(bf16[4,4,96,512]{3,2,1,0:T(8,128)(2,1)} %get-tuple-element.111), channel_id=1, source_target_pairs={{0,1},{1,0},{2,3},{3,2},{4,5},{5,4},{6,7},{7,6},{8,9},{9,8},{10,11... | collective-permute-start | bytes 4718600 | tf_op jit(solution)/shard_map/ppermute | solution.py:690
  96.1 9.7 %collective-permute-start.1 = (bf16[4,4,96,512]{3,2,1,0:T(8,128)(2,1)}, bf16[4,4,96,512]{3,2,1,0:T(8,128)(2,1)}, u32[]{:S(2)}, u32[]{:S(2)}) collective-permute-start(bf16[4,4,96,512]{3,2,1,0:T(8,128)(2,1)} %get-tuple-element.112), channel_id=1, source_target_pairs={{0,1},{1,0},{2,3},{3,2},{4,5},{5,4},{6,7},{7,6},{8,9},{9,8},{10,11... | collective-permute-start | bytes 4718600 | tf_op jit(solution)/shard_map/ppermute | solution.py:690
  100.8 44.7 %all-to-all-start.2 = ((bf16[8,3,32,512]{3,2,1,0:T(8,128)(2,1)}), bf16[8,3,32,512]{3,2,1,0:T(8,128)(2,1)}, u32[]{:S(2)}, u32[]{:S(2)}) async-start(bf16[8,3,32,512]{3,2,1,0:T(8,128)(2,1)} %get-tuple-element.142), calls=%async_computation.2 | async-start | bytes 1572864 | tf_op jit(solution)/shard_map/all_to_all | solution.py:863
  110.0 24.9 %collective-permute-start.7 = (bf16[2,4,96,512]{3,2,1,0:T(8,128)(2,1)}, bf16[2,4,96,512]{3,2,1,0:T(8,128)(2,1)S(1)}, u32[]{:S(2)}, u32[]{:S(2)}) collective-permute-start(bf16[2,4,96,512]{3,2,1,0:T(8,128)(2,1)} %get-tuple-element.192.refs_27_), channel_id=1, source_target_pairs={{0,16},{8,24},{16,0},{24,8},{1,17},{9,25},{17,1},{25,9},{2,18},{10... | collective-permute-start | bytes 2359304 | tf_op jit(solution)/shard_map/ppermute | solution.py:690
  111.6 26.7 %collective-permute-start.9 = (bf16[2,4,96,512]{3,2,1,0:T(8,128)(2,1)}, bf16[2,4,96,512]{3,2,1,0:T(8,128)(2,1)}, u32[]{:S(2)}, u32[]{:S(2)}) collective-permute-start(bf16[2,4,96,512]{3,2,1,0:T(8,128)(2,1)} %get-tuple-element.193.refs_26_), channel_id=1, source_target_pairs={{0,8},{8,0},{16,24},{24,16},{1,9},{9,1},{17,25},{25,17},{2,10},{10... | collective-permute-start | bytes 2359304 | tf_op jit(solution)/shard_map/ppermute | solution.py:690
  134.4 5.8 %collective-permute-start.6 = (bf16[4,4,96,512]{3,2,1,0:T(8,128)(2,1)}, bf16[4,4,96,512]{3,2,1,0:T(8,128)(2,1)}, u32[]{:S(2)}, u32[]{:S(2)}) collective-permute-start(bf16[4,4,96,512]{3,2,1,0:T(8,128)(2,1)} %get-tuple-element.146), channel_id=1, source_target_pairs={{0,1},{1,0},{2,3},{3,2},{4,5},{5,4},{6,7},{7,6},{8,9},{9,8},{10,11... | collective-permute-start | bytes 4718600 | tf_op jit(solution)/shard_map/ppermute | solution.py:690
  134.5 6.0 %collective-permute-start.8 = (bf16[4,4,96,512]{3,2,1,0:T(8,128)(2,1)}, bf16[4,4,96,512]{3,2,1,0:T(8,128)(2,1)}, u32[]{:S(2)}, u32[]{:S(2)}) collective-permute-start(bf16[4,4,96,512]{3,2,1,0:T(8,128)(2,1)} %get-tuple-element.149), channel_id=1, source_target_pairs={{0,1},{1,0},{2,3},{3,2},{4,5},{5,4},{6,7},{7,6},{8,9},{9,8},{10,11... | collective-permute-start | bytes 4718600 | tf_op jit(solution)/shard_map/ppermute | solution.py:690
  137.7 15.1 %collective-permute-start.13 = (bf16[4,96,512]{2,1,0:T(8,128)(2,1)}, bf16[4,96,512]{2,1,0:T(8,128)(2,1)}, u32[]{:S(2)}, u32[]{:S(2)}) collective-permute-start(bf16[4,96,512]{2,1,0:T(8,128)(2,1)} %fusion.refs_0_), channel_id=1, source_target_pairs={{0,8},{8,0},{16,24},{24,16},{1,9},{9,1},{17,25},{25,17},{2,10},{10... | collective-permute-start | bytes 1179656 | tf_op jit(solution)/shard_map/ppermute | solution.py:690
  139.7 15.5 %collective-permute-start.12 = (bf16[4,96,512]{2,1,0:T(8,128)(2,1)S(1)}, bf16[4,96,512]{2,1,0:T(8,128)(2,1)}, u32[]{:S(2)}, u32[]{:S(2)}) collective-permute-start(bf16[4,96,512]{2,1,0:T(8,128)(2,1)S(1)} %fusion.2), channel_id=1, source_target_pairs={{0,16},{8,24},{16,0},{24,8},{1,17},{9,25},{17,1},{25,9},{2,18},{10... | collective-permute-start | bytes 1179656 | tf_op jit(solution)/shard_map/ppermute | solution.py:690
  142.6 25.0 %collective-permute-start.17 = (bf16[2,4,96,512]{3,2,1,0:T(8,128)(2,1)S(1)}, bf16[2,4,96,512]{3,2,1,0:T(8,128)(2,1)}, u32[]{:S(2)}, u32[]{:S(2)}) collective-permute-start(bf16[2,4,96,512]{3,2,1,0:T(8,128)(2,1)S(1)} %get-tuple-element.190.refs_11_), channel_id=1, source_target_pairs={{0,16},{8,24},{16,0},{24,8},{1,17},{9,25},{17,1},{25,9},{2,18},{10... | collective-permute-start | bytes 2359304 | tf_op jit(solution)/shard_map/ppermute | solution.py:690
  144.0 27.1 %collective-permute-start.10 = (bf16[2,4,96,512]{3,2,1,0:T(8,128)(2,1)S(1)}, bf16[2,4,96,512]{3,2,1,0:T(8,128)(2,1)}, u32[]{:S(2)}, u32[]{:S(2)}) collective-permute-start(bf16[2,4,96,512]{3,2,1,0:T(8,128)(2,1)S(1)} %get-tuple-element.191.refs_10_), channel_id=1, source_target_pairs={{0,8},{8,0},{16,24},{24,16},{1,9},{9,1},{17,25},{25,17},{2,10},{10... | collective-permute-start | bytes 2359304 | tf_op jit(solution)/shard_map/ppermute | solution.py:690
  157.5 16.2 %collective-permute-start.14 = (bf16[192,512]{1,0:T(8,128)(2,1)S(1)}, bf16[192,512]{1,0:T(8,128)(2,1)S(1)}, u32[]{:S(2)}, u32[]{:S(2)}) collective-permute-start(bf16[192,512]{1,0:T(8,128)(2,1)S(1)} %pad_maximum_fusion.3), channel_id=1, source_target_pairs={{0,2},{1,3},{2,0},{3,1},{4,6},{5,7},{6,4},{7,5},{8,10},{9,11},{10,... | collective-permute-start | bytes 589832 | tf_op jit(solution)/shard_map/ppermute | solution.py:690
  159.0 14.6 %collective-permute-start.15 = (bf16[192,512]{1,0:T(8,128)(2,1)S(1)}, bf16[192,512]{1,0:T(8,128)(2,1)S(1)}, u32[]{:S(2)}, u32[]{:S(2)}) collective-permute-start(bf16[192,512]{1,0:T(8,128)(2,1)S(1)} %pad_maximum_fusion.4), channel_id=1, source_target_pairs={{0,4},{1,5},{2,6},{3,7},{4,0},{5,1},{6,2},{7,3},{8,12},{9,13},{10,... | collective-permute-start | bytes 589832 | tf_op jit(solution)/shard_map/ppermute | solution.py:690
  159.7 17.6 %collective-permute-start.16 = (bf16[192,512]{1,0:T(8,128)(2,1)S(1)}, bf16[192,512]{1,0:T(8,128)(2,1)}, u32[]{:S(2)}, u32[]{:S(2)}) collective-permute-start(bf16[192,512]{1,0:T(8,128)(2,1)S(1)} %pad_maximum_fusion.5), channel_id=1, source_target_pairs={{0,6},{1,7},{2,4},{3,5},{4,2},{5,3},{6,0},{7,1},{8,14},{9,15},{10,... | collective-permute-start | bytes 589832 | tf_op jit(solution)/shard_map/ppermute | solution.py:690
  169.8 10.4 %collective-permute-start.18 = (bf16[4,96,512]{2,1,0:T(8,128)(2,1)}, bf16[4,96,512]{2,1,0:T(8,128)(2,1)}, u32[]{:S(2)}, u32[]{:S(2)}) collective-permute-start(bf16[4,96,512]{2,1,0:T(8,128)(2,1)} %fusion.3), channel_id=1, source_target_pairs={{0,8},{8,0},{16,24},{24,16},{1,9},{9,1},{17,25},{25,17},{2,10},{10... | collective-permute-start | bytes 1179656 | tf_op jit(solution)/shard_map/ppermute | solution.py:690
  173.1 10.0 %collective-permute-start.11 = (bf16[4,96,512]{2,1,0:T(8,128)(2,1)}, bf16[4,96,512]{2,1,0:T(8,128)(2,1)}, u32[]{:S(2)}, u32[]{:S(2)}) collective-permute-start(bf16[4,96,512]{2,1,0:T(8,128)(2,1)} %fusion.1), channel_id=1, source_target_pairs={{0,16},{8,24},{16,0},{24,8},{1,17},{9,25},{17,1},{25,9},{2,18},{10... | collective-permute-start | bytes 1179656 | tf_op jit(solution)/shard_map/ppermute | solution.py:690
  185.0 8.0 %collective-permute-start.19 = (bf16[192,512]{1,0:T(8,128)(2,1)S(1)}, bf16[192,512]{1,0:T(8,128)(2,1)S(1)}, u32[]{:S(2)}, u32[]{:S(2)}) collective-permute-start(bf16[192,512]{1,0:T(8,128)(2,1)S(1)} %pad_maximum_fusion.6), channel_id=1, source_target_pairs={{0,2},{1,3},{2,0},{3,1},{4,6},{5,7},{6,4},{7,5},{8,10},{9,11},{10,... | collective-permute-start | bytes 589832 | tf_op jit(solution)/shard_map/ppermute | solution.py:690
  186.5 13.0 %collective-permute-start.20 = (bf16[192,512]{1,0:T(8,128)(2,1)S(1)}, bf16[192,512]{1,0:T(8,128)(2,1)S(1)}, u32[]{:S(2)}, u32[]{:S(2)}) collective-permute-start(bf16[192,512]{1,0:T(8,128)(2,1)S(1)} %pad_maximum_fusion.7), channel_id=1, source_target_pairs={{0,4},{1,5},{2,6},{3,7},{4,0},{5,1},{6,2},{7,3},{8,12},{9,13},{10,... | collective-permute-start | bytes 589832 | tf_op jit(solution)/shard_map/ppermute | solution.py:690
  187.2 16.3 %collective-permute-start.21 = (bf16[192,512]{1,0:T(8,128)(2,1)S(1)}, bf16[192,512]{1,0:T(8,128)(2,1)S(1)}, u32[]{:S(2)}, u32[]{:S(2)}) collective-permute-start(bf16[192,512]{1,0:T(8,128)(2,1)S(1)} %pad_maximum_fusion.8), channel_id=1, source_target_pairs={{0,6},{1,7},{2,4},{3,5},{4,2},{5,3},{6,0},{7,1},{8,14},{9,15},{10,... | collective-permute-start | bytes 589832 | tf_op jit(solution)/shard_map/ppermute | solution.py:690
  189.7 16.4 %collective-permute-start.27 = (bf16[192,512]{1,0:T(8,128)(2,1)S(1)}, bf16[192,512]{1,0:T(8,128)(2,1)S(1)}, u32[]{:S(2)}, u32[]{:S(2)}) collective-permute-start(bf16[192,512]{1,0:T(8,128)(2,1)S(1)} %add_convert_fusion.8.p0), channel_id=1, source_target_pairs={{0,24},{8,16},{16,8},{24,0},{1,25},{9,17},{17,9},{25,1},{2,26},{10... | collective-permute-start | bytes 589832 | tf_op jit(solution)/shard_map/ppermute | solution.py:690
  190.6 16.6 %collective-permute-start.26 = (bf16[192,512]{1,0:T(8,128)(2,1)S(1)}, bf16[192,512]{1,0:T(8,128)(2,1)S(1)}, u32[]{:S(2)}, u32[]{:S(2)}) collective-permute-start(bf16[192,512]{1,0:T(8,128)(2,1)S(1)} %add_convert_fusion.8.p0), channel_id=1, source_target_pairs={{0,16},{8,24},{16,0},{24,8},{1,17},{9,25},{17,1},{25,9},{2,18},{10... | collective-permute-start | bytes 589832 | tf_op jit(solution)/shard_map/ppermute | solution.py:690
  193.0 14.2 %collective-permute-start.25 = (bf16[192,512]{1,0:T(8,128)(2,1)S(1)}, bf16[192,512]{1,0:T(8,128)(2,1)S(1)}, u32[]{:S(2)}, u32[]{:S(2)}) collective-permute-start(bf16[192,512]{1,0:T(8,128)(2,1)S(1)} %add_convert_fusion.8.p0), channel_id=1, source_target_pairs={{0,8},{8,0},{16,24},{24,16},{1,9},{9,1},{17,25},{25,17},{2,10},{10... | collective-permute-start | bytes 589832 | tf_op jit(solution)/shard_map/ppermute | solution.py:690
  203.6 8.4 %collective-permute-start.24 = (bf16[192,512]{1,0:T(8,128)(2,1)S(1)}, bf16[192,512]{1,0:T(8,128)(2,1)S(1)}, u32[]{:S(2)}, u32[]{:S(2)}) collective-permute-start(bf16[192,512]{1,0:T(8,128)(2,1)S(1)} %add_convert_fusion.9.p0), channel_id=1, source_target_pairs={{0,24},{8,16},{16,8},{24,0},{1,25},{9,17},{17,9},{25,1},{2,26},{10... | collective-permute-start | bytes 589832 | tf_op jit(solution)/shard_map/ppermute | solution.py:690
  204.6 9.1 %collective-permute-start.23 = (bf16[192,512]{1,0:T(8,128)(2,1)S(1)}, bf16[192,512]{1,0:T(8,128)(2,1)S(1)}, u32[]{:S(2)}, u32[]{:S(2)}) collective-permute-start(bf16[192,512]{1,0:T(8,128)(2,1)S(1)} %add_convert_fusion.9.p0), channel_id=1, source_target_pairs={{0,16},{8,24},{16,0},{24,8},{1,17},{9,25},{17,1},{25,9},{2,18},{10... | collective-permute-start | bytes 589832 | tf_op jit(solution)/shard_map/ppermute | solution.py:690
  206.1 7.6 %collective-permute-start.22 = (bf16[192,512]{1,0:T(8,128)(2,1)S(1)}, bf16[192,512]{1,0:T(8,128)(2,1)S(1)}, u32[]{:S(2)}, u32[]{:S(2)}) collective-permute-start(bf16[192,512]{1,0:T(8,128)(2,1)S(1)} %add_convert_fusion.9.p0), channel_id=1, source_target_pairs={{0,8},{8,0},{16,24},{24,16},{1,9},{9,1},{17,25},{25,17},{2,10},{10... | collective-permute-start | bytes 589832 | tf_op jit(solution)/shard_map/ppermute | solution.py:690
  (28 other events, 231.8 us)
